TPU v7x, 32 devices: a whole 2x2x4 slice. The times are simulated.
32 devices in a mesh: dp: 8 (over z, y), vocab: 4 (over x, core).
Axes of the slice: x: 2, y: 2, z: 4, core: 2. Of those that a mesh axis runs over, the one named last changes fastest.
Arguments:
- hidden: bfloat16 [6144, 2048], P('dp', 'vocab')
- gain: bfloat16 [2048], replicated, may hold values from 0.5 to 1.5
- head: bfloat16 [2048, 32000], P('dp', 'vocab')
- target_ids: int32 [6144], P('dp'), may hold values from 0 to 31999
- seq_lens: int32 [16], replicated, may hold values from 64 to 704, as said below
- seq_owner: int32 [16], replicated, may hold values from 0 to 7, as said below
Outputs:
- logprob: float32 [6144], P('dp')
- entropy: float32 [6144], P('dp')
Inputs may be any that keep to these rules, and one draw needn't show every extreme that they name: `seq_lens`: the lengths of the sequences owned by one dp index sum to at most 768; in every draw the sequences of some dp index sum to exactly 768. `seq_owner`: every dp index owns exactly 2 sequences.
All inputs are finite; a program needn't handle non-finite values.
Results may differ from a plain program's by a relative error of at most 0.0075.
Values may be sent and summed in bfloat16 or wider, within the bound.
No kernel may reach another device: no remote copies, remote signals or barrier semaphores. Data moves between devices by JAX's collectives and lax.ppermute only.
A program may use at most 128 MiB of HBM per device.

v0:
```python
import jax
import jax.numpy as jnp
from jax import lax
from jax.sharding import PartitionSpec as P

EPS = 1e-05


def row_stats(normed, token_ids, columns, offset):
    count = normed.shape[0]
    width = normed.shape[1]
    block_rows = min(128, count)
    blocks = count // block_rows
    breadth = columns.shape[1]

    def compute(block_norm, block_ids):
        logits = jnp.dot(block_norm, columns, preferred_element_type=jnp.float32)
        top = jnp.max(logits, axis=1)
        expo = jnp.exp(logits - top[:, None])
        total = jnp.sum(expo, axis=1)
        weighted = jnp.sum(expo * logits, axis=1)
        local_id = block_ids - offset
        matches = jnp.arange(breadth, dtype=jnp.int32)[None, :] == local_id[:, None]
        picked = jnp.sum(jnp.where(matches, logits, 0.0), axis=1)
        return (top, total, weighted, picked)

    def per_block(item):
        block_norm, block_ids, start = item
        return compute(block_norm, block_ids)

    starts = jnp.arange(blocks, dtype=jnp.int32) * block_rows
    result = lax.map(
        per_block,
        (normed.reshape(blocks, block_rows, width), token_ids.reshape(blocks, block_rows), starts),
    )
    return tuple((member.reshape(count) for member in result))


def local(hidden, gain, head, target_ids, seq_lens, seq_owner):
    groups = lax.axis_size("dp")
    position = lax.axis_index("dp")
    slice_index = lax.axis_index("vocab")
    slots = hidden.shape[0]
    breadth = head.shape[1]
    owners = jnp.arange(groups, dtype=jnp.int32)
    loads = jnp.sum(jnp.where(seq_owner[:, None] == owners[None, :], seq_lens[:, None], 0), axis=0)
    own_live = jnp.arange(slots, dtype=jnp.int32) < loads[position]
    features = lax.all_gather(hidden, "vocab", axis=1, tiled=True)
    wide = features.astype(jnp.float32)
    normed = (
        wide
        * lax.rsqrt(jnp.mean(wide * wide, axis=1, keepdims=True) + EPS)
        * gain.astype(jnp.float32)
    ).astype(jnp.bfloat16)
    columns = lax.all_gather(head, "dp", axis=0, tiled=True)
    stats = row_stats(normed, target_ids, columns, slice_index * breadth)
    top = lax.pmax(stats[0], "vocab")
    factor = jnp.exp(stats[0] - top)
    total, weighted, picked = lax.psum((stats[1] * factor, stats[2] * factor, stats[3]), "vocab")
    lse = top + jnp.log(total)
    logprob = picked - lse
    entropy = lse - weighted / total
    return (jnp.where(own_live, logprob, 0.0), jnp.where(own_live, entropy, 0.0))


def solution(mesh):
    return jax.shard_map(
        local,
        mesh=mesh,
        in_specs=(P("dp", "vocab"), P(), P("dp", "vocab"), P("dp"), P(), P()),
        out_specs=(P("dp"), P("dp")),
        check_vma=False,
    )
```

profile of v0, /device:TPU:4, one launch (start us, length us, event | category | flops | bytes accessed | tf_op | source)
XLA Modules:
  0.0 812.9 jit_solution(16811034629249649305)
XLA Ops:
  7.9 6.4 copy.9
  15.8 23.6 %all-gather.3.cloned.1.call-done = bf16[768,2048]{1,0:T(8,128)(2,1)} async-done(((bf16[768,512]{1,0:T(8,128)(2,1)}), bf16[768,2048]{1,0:T(8,128)(2,1)}) %all-gather.3.cloned.1.call-update) | async-done | bytes 3145744 | tf_op jit(solution)/shard_map/all_gather | solution.py:48
  39.3 2.7 fusion.5
  42.2 0.8 fusion.7
  43.0 624.7 %all-gather.5.cloned.1.call-done = bf16[2048,8000]{1,0:T(8,128)(2,1)} async-done(((bf16[256,8000]{1,0:T(8,128)(2,1)}), bf16[2048,8000]{1,0:T(8,128)(2,1)}) %all-gather.5.cloned.1.call-update) | async-done | bytes 32768016 | tf_op jit(solution)/shard_map/all_gather | solution.py:55
  667.7 120.0 %while.16 = (s32[]{:T(128)}, f32[6,128]{1,0:T(8,128)S(1)}, f32[6,128]{1,0:T(8,128)S(1)}, f32[6,128]{1,0:T(8,128)S(1)}, f32[6,128]{1,0:T(8,128)S(1)}, /*index=5*/...) while((s32[]{:T(128)}, f32[6,128]{1,0:T(8,128)S(1)}, ...), condition=%wide.region_7.8_spmd, body=%wide.region_2.7_spmd.sunk | while | flops 4202495488 | bytes 41492616 | solution.py:32
  667.7 17.8 %fusion.13 = (f32[128]{0:T(128)S(1)}, f32[128,8000]{0,1:T(8,128)S(1)}) fusion(bf16[2048,8000]{1,0:T(8,128)(2,1)} %get-tuple-element.179, bf16[6,128,2048]{2,1,0:T(8,128)(2,1)S(1)} %get-tuple-element.178, s32[]{:T(128)} %get-tuple-element.162), kind=kOutput, calls=%fused_computation.25.clone.1 | convolution fusion | flops 4195328000 | bytes 37388804 | tf_op jit(solution)/shard_map/while/body/eval_jaxpr/dot_general | solution.py:17
  685.5 0.7 subtract_bitcast_fusion.2
  686.2 1.3 multiply_reduce_fusion.2
  687.7 17.8 %fusion.13 = (f32[128]{0:T(128)S(1)}, f32[128,8000]{0,1:T(8,128)S(1)}) fusion(bf16[2048,8000]{1,0:T(8,128)(2,1)} %get-tuple-element.179, bf16[6,128,2048]{2,1,0:T(8,128)(2,1)S(1)} %get-tuple-element.178, s32[]{:T(128)} %get-tuple-element.162), kind=kOutput, calls=%fused_computation.25.clone.1 | convolution fusion | flops 4195328000 | bytes 37388804 | tf_op jit(solution)/shard_map/while/body/eval_jaxpr/dot_general | solution.py:17
  705.5 0.7 subtract_bitcast_fusion.2
  706.2 1.3 multiply_reduce_fusion.2
  707.7 17.8 %fusion.13 = (f32[128]{0:T(128)S(1)}, f32[128,8000]{0,1:T(8,128)S(1)}) fusion(bf16[2048,8000]{1,0:T(8,128)(2,1)} %get-tuple-element.179, bf16[6,128,2048]{2,1,0:T(8,128)(2,1)S(1)} %get-tuple-element.178, s32[]{:T(128)} %get-tuple-element.162), kind=kOutput, calls=%fused_computation.25.clone.1 | convolution fusion | flops 4195328000 | bytes 37388804 | tf_op jit(solution)/shard_map/while/body/eval_jaxpr/dot_general | solution.py:17
  725.5 0.7 subtract_bitcast_fusion.2
  726.2 1.3 multiply_reduce_fusion.2
  727.7 17.8 %fusion.13 = (f32[128]{0:T(128)S(1)}, f32[128,8000]{0,1:T(8,128)S(1)}) fusion(bf16[2048,8000]{1,0:T(8,128)(2,1)} %get-tuple-element.179, bf16[6,128,2048]{2,1,0:T(8,128)(2,1)S(1)} %get-tuple-element.178, s32[]{:T(128)} %get-tuple-element.162), kind=kOutput, calls=%fused_computation.25.clone.1 | convolution fusion | flops 4195328000 | bytes 37388804 | tf_op jit(solution)/shard_map/while/body/eval_jaxpr/dot_general | solution.py:17
  746.2 1.3 multiply_reduce_fusion.2
  747.7 17.8 %fusion.13 = (f32[128]{0:T(128)S(1)}, f32[128,8000]{0,1:T(8,128)S(1)}) fusion(bf16[2048,8000]{1,0:T(8,128)(2,1)} %get-tuple-element.179, bf16[6,128,2048]{2,1,0:T(8,128)(2,1)S(1)} %get-tuple-element.178, s32[]{:T(128)} %get-tuple-element.162), kind=kOutput, calls=%fused_computation.25.clone.1 | convolution fusion | flops 4195328000 | bytes 37388804 | tf_op jit(solution)/shard_map/while/body/eval_jaxpr/dot_general | solution.py:17
  766.2 1.3 multiply_reduce_fusion.2
  767.7 17.8 %fusion.13 = (f32[128]{0:T(128)S(1)}, f32[128,8000]{0,1:T(8,128)S(1)}) fusion(bf16[2048,8000]{1,0:T(8,128)(2,1)} %get-tuple-element.179, bf16[6,128,2048]{2,1,0:T(8,128)(2,1)S(1)} %get-tuple-element.178, s32[]{:T(128)} %get-tuple-element.162), kind=kOutput, calls=%fused_computation.25.clone.1 | convolution fusion | flops 4195328000 | bytes 37388804 | tf_op jit(solution)/shard_map/while/body/eval_jaxpr/dot_general | solution.py:17
  786.2 1.3 multiply_reduce_fusion.2
  787.6 7.1 pmax.7
  794.8 10.1 %all-reduce = (f32[768]{0:T(1024)S(1)}, f32[768]{0:T(1024)S(1)}, f32[768]{0:T(1024)S(1)}) all-reduce(f32[768]{0:T(1024)S(1)} %bitcast.43, f32[768]{0:T(1024)S(1)} %get-tuple-element.85, f32[768]{0:T(1024)S(1)} %get-tuple-element.84), channel_id=1, replica_groups=mesh['dp'=8,'vocab'=4] {'vocab'}, use_global_device_ids=true, to_apply=%region_8.9 | all-reduce | flops 2304 | bytes 18432 | tf_op jit(solution)/shard_map/psum | solution.py:59
  804.9 1.2 subtract_select_fusion
  (48 shorter events, 5.1 us)
Async XLA Ops:
  7.2 32.2 %all-gather.3.cloned.1.call-start = ((), (), s32[]{:S(2)}) async-start(), calls=%async_computation | async-start | bytes 3932160 | tf_op jit(solution)/shard_map/all_gather | solution.py:48
  7.9 659.8 %all-gather.5.cloned.1.call-start = ((), (), s32[]{:S(2)}) async-start(), calls=%async_computation.1 | async-start | bytes 37158912 | tf_op jit(solution)/shard_map/all_gather | solution.py:55
  14.4 0.7 copy-start.1
  14.4 0.7 copy-start.2
  14.4 0.7 copy-start.3
  39.3 2.8 copy-start
Sparse Core Ops, SparseCore 0:
  9.6 29.7 all-gather.2
  40.9 626.7 all-gather.4
where the time goes:
time: 816 us; the launch traced here: 813 us
  waiting for transfers between devices  649 us (80%)
  matrix products  107 us (13%)
  blocking collectives  17.2 us (2%)
  other arithmetic  17 us (2%)
  between operations  14.1 us (2%)
  local copies, waits for them, and re-layouts  8.55 us (1%)
    all_gather x1, waiting for transfers between devices, local(): columns = lax.all_gather(head, 'dp', axis=0, tiled=True)  625 us
    dot_general x6, matrix products, compute(): logits = jnp.dot(block_norm, columns, preferred_element_type=jnp.float32)  107 us
    all_gather x1, waiting for transfers between devices, local(): features = lax.all_gather(hidden, 'vocab', axis=1, tiled=True)  23.6 us
  transfers between devices with their start and end apart: 2, of which 2 were waited for; matrix products, arithmetic and copies ran while one was open for 1% of the time, Pallas kernels for 0%

commit v1 on v0

v1 whole, which is shorter than its diff:
```python
import functools

import jax
import jax.numpy as jnp
from jax import lax
from jax.experimental import pallas as pl
from jax.experimental.pallas import tpu as pltpu
from jax.sharding import PartitionSpec as P

EPS = 1e-05
LOW = -3.0e38
LANES = 128
TILE = 16
PIECES = (8, 7, 6, 4)
ROWS = 256
TOKEN_BYTES = 17 * 2**20


def assemble_kernel(count, place, gain_ref, *refs):
    target = refs[-1]
    sources = [(ref, index) for ref in refs[:count] for index in range(ref.shape[1])]
    features = refs[0].shape[3]
    for start in range(0, target.shape[3], LANES):
        lanes = slice(start, start + LANES)
        square = sum(
            jnp.sum(jnp.square(ref[0, at, lanes].astype(jnp.float32)), axis=1, keepdims=True) for ref, at in sources
        )
        scale = lax.rsqrt(square / (features * len(sources)) + EPS)
        for number, (ref, at) in enumerate(sources):
            first = pl.multiple_of((place[0] ^ place[1 + number]) * features, features)
            value = ref[0, at, lanes].astype(jnp.float32) * scale * gain_ref[:, pl.ds(first, features)]
            target[0, 0, pl.ds(first, features), lanes] = value.T.astype(target.dtype)


def assemble(part, offsets, gain, sources, rows, at, groups, splits, whole):
    count, _, _, features = sources[0].shape
    wide = features * len(offsets)
    place = jnp.stack([part] + [jnp.int32(offset) for offset in offsets]).astype(jnp.int32)
    before = [] if whole is None else [whole]
    return pl.pallas_call(
        functools.partial(assemble_kernel, len(sources)),
        grid_spec=pltpu.PrefetchScalarGridSpec(
            num_scalar_prefetch=1,
            grid=(count, splits),
            in_specs=[pl.BlockSpec((1, wide), lambda i, j, s: (0, 0))]
            + [pl.BlockSpec((1, y.shape[1], rows, features), lambda i, j, s: (i, 0, j, 0)) for y in sources]
            + [pl.BlockSpec(memory_space=pl.ANY)] * len(before),
            out_specs=pl.BlockSpec((1, 1, wide, rows), lambda i, j, s: (at + i, j, 0, 0)),
        ),
        out_shape=jax.ShapeDtypeStruct((groups, splits, wide, rows), sources[0].dtype),
        input_output_aliases={2 + len(sources): 0} if before else {},
        compiler_params=pltpu.CompilerParams(vmem_limit_bytes=24 * 2**20),
        cost_estimate=pl.CostEstimate(
            flops=6 * count * splits * rows * wide,
            bytes_accessed=4 * count * splits * rows * wide,
            transcendentals=count * splits * rows,
        ),
    )(place, gain, *sources, *before)


def stats_kernel(masked, scalars, *refs):
    x_ref, ids_ref = refs[:2]
    head_refs, (out_ref, head, logits, sems) = refs[2:-4], refs[-4:]
    step = pl.program_id(0)
    live = scalars[0]
    rows = x_ref.shape[3]
    count, width, depth = head_refs[0].shape

    @pl.when(step == 0)
    def _():
        copies = []
        for away, source in enumerate(head_refs):
            for index in range(count):
                start = pl.multiple_of((index * len(head_refs) + (scalars[2] ^ away)) * depth, depth)
                copies.append(
                    pltpu.make_async_copy(source.at[index], head.at[:, pl.ds(start, depth)], sems.at[len(copies)])
                )
        for copy in copies:
            copy.start()
        for copy in copies:
            copy.wait()

    def multiply():
        logits[lax.rem(step, 2)] = lax.dot_general(
            head[...], x_ref[0, 0], (((1,), (0,)), ((), ())), preferred_element_type=jnp.float32
        )

    def reduce():
        slot = lax.rem(step + 1, 2)
        column = lax.broadcasted_iota(jnp.int32, (width, LANES), 0)
        for start in range(0, rows, LANES):
            lanes = slice(start, start + LANES)
            block = logits[slot, :, lanes]
            if masked:
                block = jnp.where(column < scalars[1], block, LOW)
            top = jnp.max(block, axis=0, keepdims=True)
            shifted = jnp.maximum(block - top, -1.0e4)
            expo = jnp.exp(shifted)
            out_ref[0, 0:1, lanes] = top
            out_ref[0, 1:2, lanes] = jnp.sum(expo, axis=0, keepdims=True)
            out_ref[0, 2:3, lanes] = jnp.sum(expo * shifted, axis=0, keepdims=True)
            out_ref[0, 3:4, lanes] = jnp.sum(
                jnp.where(column == ids_ref[0, :, lanes], block, 0.0), axis=0, keepdims=True
            )

    @pl.when(step == 0)
    def _():
        multiply()

    @pl.when((step > 0) & (step < live))
    def _():
        multiply()
        reduce()

    @pl.when(step == live)
    def _():
        reduce()


def stats(alive, real, low, x, ids, heads, masked):
    groups, per, wide, rows = x.shape
    blocks = groups * per
    count, width, depth = heads[0].shape
    order = jnp.argsort(jnp.logical_not(alive))
    number = jnp.sum(alive.astype(jnp.int32))
    scalars = jnp.concatenate([jnp.stack([number, real, low]), order]).astype(jnp.int32)

    def here(i, s):
        return s[3 + jnp.minimum(i, s[0] - 1)]

    def before(i, s):
        return s[3 + jnp.minimum(jnp.maximum(i - 1, 0), s[0] - 1)]

    return pl.pallas_call(
        functools.partial(stats_kernel, masked),
        grid_spec=pltpu.PrefetchScalarGridSpec(
            num_scalar_prefetch=1,
            grid=(blocks + 1,),
            in_specs=[
                pl.BlockSpec((1, 1, wide, rows), lambda i, s: (here(i, s) // per, here(i, s) % per, 0, 0)),
                pl.BlockSpec((1, 1, rows), lambda i, s: (before(i, s), 0, 0)),
            ]
            + [pl.BlockSpec(memory_space=pl.ANY)] * len(heads),
            out_specs=pl.BlockSpec((1, 4, rows), lambda i, s: (before(i, s), 0, 0)),
            scratch_shapes=[
                pltpu.VMEM((width, wide), jnp.bfloat16),
                pltpu.VMEM((2, width, rows), jnp.float32),
                pltpu.SemaphoreType.DMA((count * len(heads),)),
            ],
        ),
        out_shape=jax.ShapeDtypeStruct((blocks, 4, rows), jnp.float32),
        compiler_params=pltpu.CompilerParams(vmem_limit_bytes=32 * 2**20),
        cost_estimate=pl.CostEstimate(
            flops=2 * blocks * rows * wide * width,
            bytes_accessed=x.size * 2 + wide * width * 2,
            transcendentals=blocks * rows * width,
        ),
    )(scalars, x, ids, *heads)


def merge(members):
    top, total, weighted, picked = (jnp.stack([m[..., i, :] for m in members]) for i in range(4))
    best = jnp.max(top, axis=0)
    shift = jnp.maximum(top - best[None], -1.0e4)
    factor = jnp.exp(shift)
    return jnp.stack(
        [
            best,
            jnp.sum(total * factor, axis=0),
            jnp.sum(factor * (weighted + total * shift), axis=0),
            jnp.sum(picked, axis=0),
        ],
        axis=-2,
    )


def by_collectives(hidden, gain, head, target_ids, loads):
    groups = lax.axis_size("dp")
    parts = lax.axis_size("vocab")
    slots, features = hidden.shape
    depth, breadth = head.shape
    width = -(-breadth // (groups * TILE)) * TILE
    base = lax.axis_index("dp") * width
    real = jnp.clip(breadth - base, 0, width)
    places = lax.all_gather(target_ids, "dp", axis=0) - (lax.axis_index("vocab") * breadth + base)
    places = jnp.where(places < real, places, -1)

    spread = jnp.pad(head.T, ((0, groups * width - breadth), (0, 0))).reshape(groups, width, depth)
    columns = lax.all_to_all(spread, "dp", split_axis=0, concat_axis=0, tiled=True)
    columns = columns.transpose(1, 0, 2).reshape(1, width, groups * depth)

    splits = -(-groups * slots * features * parts * 2 // TOKEN_BYTES)
    while slots % splits or (slots // splits) % LANES:
        splits += 1
    rows = slots // splits
    zero = jnp.int32(0)
    results = []
    for start in range(0, slots, rows):
        piece = hidden[start : start + rows]
        if results:
            piece, _ = lax.optimization_barrier((piece, results[-1]))
        x = lax.all_gather(piece, ("dp", "vocab"), axis=0).reshape(groups, parts, rows, features)
        x = assemble(zero, tuple(range(parts)), gain, [x], rows, 0, groups, 1, None)
        ids = places[:, None, start : start + rows]
        results.append(stats(start < loads, real, zero, x, ids, [columns], True))
    found = lax.all_to_all(jnp.concatenate(results, axis=2), "dp", split_axis=0, concat_axis=0, tiled=True)
    mine = lax.all_gather(merge(list(found)), "vocab", axis=0)
    return merge(list(mine))


def by_axes(hidden, gain, head, target_ids, loads):
    groups = lax.axis_size("dp")
    parts = lax.axis_size("vocab")
    position = lax.axis_index("dp")
    part = lax.axis_index("vocab")
    tall = groups // 2
    hi = position // 2
    low = position % 2
    slots, features = hidden.shape
    depth, breadth = head.shape
    chunk = breadth // tall
    ends = [chunk * sum(PIECES[:n]) // sum(PIECES) // TILE * TILE for n in range(len(PIECES))] + [chunk]
    cuts = [(start, end - start) for start, end in zip(ends, ends[1:])]
    lines = [[2 * index + side for index in range(tall)] for side in range(2)]

    def swap_hi(x, step):
        return lax.ppermute(x, "dp", [(g, g ^ (2 * step)) for g in range(groups)])

    def swap_lo(x):
        return lax.ppermute(x, "dp", [(g, g ^ 1) for g in range(groups)])

    def swap_part(x, step):
        return lax.ppermute(x, "vocab", [(v, v ^ step) for v in range(parts)])

    def along(x, moves):
        return lax.ppermute(x, "dp", [(2 * a + side, 2 * b + side) for a, b in moves for side in range(2)])

    turned = head.T.reshape(tall, chunk, depth)
    heads = []
    for start, width in cuts:
        mine = lax.all_to_all(
            turned[:, start : start + width], "dp", split_axis=0, concat_axis=0, axis_index_groups=lines, tiled=True
        )
        heads.append([mine, swap_lo(mine)])

    code = jnp.concatenate([target_ids >> 8, target_ids & 255]).astype(hidden.dtype)
    code = jnp.pad(code, (0, TILE * features - 2 * slots)).reshape(TILE, features)
    own = jnp.concatenate([hidden, code])
    middle = (hi == 1) | (hi == 2)
    near = swap_hi(own, 1)
    cross = along(own, [(1, 2), (2, 1)])
    cross_near = along(near, [(1, 2), (2, 1)])
    out = along(cross, [(1, 0), (2, 3)])
    out_near = along(cross_near, [(1, 0), (2, 3)])
    order = [0, 1, jnp.where(middle, 3, 2), jnp.where(middle, 2, 3)]
    splits = slots // ROWS
    x = None
    codes = []
    for index, y in enumerate([own, near, jnp.where(middle, cross, out), jnp.where(middle, cross_near, out_near)]):
        held = [y]
        offsets = [0]
        for step in (2, 1):
            held = held + [swap_part(z, step) for z in held]
            offsets = offsets + [offset ^ step for offset in offsets]
        x = assemble(part, offsets, gain, [z[None, None] for z in held], ROWS, index, tall, splits, x)
        codes.append(y[slots:].reshape(TILE * features)[: 2 * slots].astype(jnp.int32))
    code = jnp.stack(codes)
    ids = (code[:, :slots] * 256 + code[:, slots:]).reshape(tall * splits, 1, ROWS)

    first = jnp.arange(splits, dtype=jnp.int32) * ROWS
    own_loads = loads[2 * (hi ^ jnp.stack([jnp.int32(away) for away in order])) + low]
    alive = (first[None, :] < own_loads[:, None]).reshape(-1)
    found = []
    for (start, width), members in zip(cuts, heads):
        places = ids - (part * breadth + hi * chunk + start)
        places = jnp.where(places < width, places, -1)
        found.append(stats(alive, jnp.int32(width), low, x, places, members, False))
    found = merge(found).reshape(tall, splits, 4, ROWS).transpose(0, 2, 1, 3).reshape(tall, 4, slots)

    def of(step):
        return lax.dynamic_index_in_dim(found, order[step], keepdims=False)

    mine = merge([of(0)] + [swap_hi(of(step), step) for step in range(1, tall)])
    return merge([mine] + [swap_part(mine, step) for step in range(1, parts)])


def local(hidden, gain, head, target_ids, seq_lens, seq_owner):
    groups = lax.axis_size("dp")
    slots, features = hidden.shape
    owners = jnp.arange(groups, dtype=jnp.int32)
    loads = jnp.sum(jnp.where(seq_owner[:, None] == owners[None, :], seq_lens[:, None], 0), axis=0).astype(jnp.int32)
    fits = (
        (groups, lax.axis_size("vocab")) == (8, 4)
        and slots % ROWS == 0
        and 2 * slots <= TILE * features
        and head.shape[1] % (groups // 2 * TILE) == 0
    )
    transport = by_axes if fits else by_collectives
    scores = transport(hidden, gain.astype(jnp.float32)[None], head, target_ids, loads)
    top, total, weighted, picked = (scores[index] for index in range(4))
    spread = jnp.log(total)
    logprob = picked - (top + spread)
    entropy = spread - weighted / total
    live = jnp.arange(slots, dtype=jnp.int32) < loads[lax.axis_index("dp")]
    return (jnp.where(live, logprob, 0.0), jnp.where(live, entropy, 0.0))


def solution(mesh):
    return jax.shard_map(
        local,
        mesh=mesh,
        in_specs=(P("dp", "vocab"), P(), P("dp", "vocab"), P("dp"), P(), P()),
        out_specs=(P("dp"), P("dp")),
        check_vma=False,
    )
```

time: 816 us -> 257 us (0.31)
  waiting for transfers between devices: 649 us -> 106 us
  matrix products: 107 us -> 0 us
  Pallas kernels: 0 us -> 54.9 us
  starting transfers between devices: 0.08 us -> 42.6 us
  local copies, waits for them, and re-layouts: 8.55 us -> 38.7 us
  blocking collectives: 17.2 us -> 0 us
  between operations: 14.1 us -> 1.21 us
  other arithmetic: 17 us -> 8.25 us
    all_gather x2 -> x0, waiting for transfers between devices: 648 us -> none  [the longest x1 625 us: local(): columns = lax.all_gather(head, 'dp', axis=0, tiled=True)]
    dot_general x6 -> x0, matrix products: 107 us -> none  [compute(): logits = jnp.dot(block_norm, columns, preferred_element_type=jnp.float32)]
    ppermute x0 -> x27, waiting for transfers between devices: none -> 91.3 us  [the longest x4 38.2 us: along(): lax.ppermute(x, 'dp', [(2 * a + side, 2 * b + side) for a, b in moves for...]
    pallas_call x0 -> x8, Pallas kernels: none -> 54.9 us  [the longest x4 40.3 us: stats(): pl.pallas_call(functools.partial(stats_kernel, masked), grid_spec=pltpu.P...]
    ppermute x0 -> x27, starting transfers between devices: none -> 24 us  [the longest x15 9.46 us: swap_part(): return lax.ppermute(x, 'vocab', [(v, v ^ step) for v in range(parts)])]
    unnamed x9 -> x36, local copies, waits for them, and re-layouts: 7.15 us -> 28 us
    all_to_all x0 -> x4, starting transfers between devices: none -> 18.7 us  [by_axes(): lax.all_to_all(turned[:, start:start + width], 'dp', split_axis=0, concat...]
    all_to_all x0 -> x4, waiting for transfers between devices: none -> 15.2 us  [by_axes(): lax.all_to_all(turned[:, start:start + width], 'dp', split_axis=0, concat...]
  transfers between devices with their start and end apart: 2 -> 31, of which waited for: 2 -> 12; matrix products, arithmetic and copies ran while one was open for 1% -> 6% of each run, Pallas kernels for 0% -> 17%
where the time goes in v1:
time: 257 us; the launch traced here: 252 us
  waiting for transfers between devices  106 us (41%)
  Pallas kernels  54.9 us (21%)
  starting transfers between devices  42.6 us (17%)
  local copies, waits for them, and re-layouts  38.7 us (15%)
  other arithmetic  8.25 us (3%)
    pallas_call x4, Pallas kernels, stats(): pl.pallas_call(functools.partial(stats_kernel, masked), grid_spec=pltpu.P...  40.3 us
    ppermute x4, waiting for transfers between devices, along(): lax.ppermute(x, 'dp', [(2 * a + side, 2 * b + side) for a, b in moves for...  38.2 us
    ppermute x4, waiting for transfers between devices, swap_hi(): return lax.ppermute(x, 'dp', [(g, g ^ 2 * step) for g in range(groups)])  29.9 us
    unnamed x36, local copies, waits for them, and re-layouts  28 us
    ppermute x4, waiting for transfers between devices, swap_lo(): return lax.ppermute(x, 'dp', [(g, g ^ 1) for g in range(groups)])  19 us
    all_to_all x4, starting transfers between devices, by_axes(): lax.all_to_all(turned[:, start:start + width], 'dp', split_axis=0, concat...  18.7 us
    all_to_all x4, waiting for transfers between devices, by_axes(): lax.all_to_all(turned[:, start:start + width], 'dp', split_axis=0, concat...  15.2 us
    pallas_call x4, Pallas kernels, assemble(): pl.pallas_call(functools.partial(assemble_kernel, len(sources)), grid_spe...  14.6 us
  transfers between devices with their start and end apart: 31, of which 12 were waited for; matrix products, arithmetic and copies ran while one was open for 6% of the time, Pallas kernels for 17%

profile of v1, /device:TPU:4, one launch (start us, length us, event | category | flops | bytes accessed | tf_op | source)
XLA Modules:
  0.0 252.1 jit_solution(9863376425977761740)
XLA Ops:
  2.6 4.9 %all-to-all-start.3 = ((bf16[4,320,256]{2,1,0:T(8,128)(2,1)}), bf16[4,320,256]{2,1,0:T(8,128)(2,1)S(1)}, u32[]{:S(2)}, u32[]{:S(2)}) async-start(bf16[4,320,256]{2,1,0:T(8,128)(2,1)} %slice.252), calls=%async_computation.3 | async-start | bytes 1310720 | tf_op jit(solution)/shard_map/all_to_all | solution.py:241
  9.7 15.1 %all-to-all-done.3.refs_2_ = bf16[4,320,256]{2,1,0:T(8,128)(2,1)S(1)} async-done(((bf16[4,320,256]{2,1,0:T(8,128)(2,1)}), bf16[4,320,256]{2,1,0:T(8,128)(2,1)S(1)}, u32[]{:S(2)}, u32[]{:S(2)}) %all-to-all-start.3) | async-done | bytes 655392 | tf_op jit(solution)/shard_map/all_to_all | solution.py:241
  24.8 4.2 %all-to-all-start.2 = ((bf16[4,480,256]{2,1,0:T(8,128)(2,1)}), bf16[4,480,256]{2,1,0:T(8,128)(2,1)}, u32[]{:S(2)}, u32[]{:S(2)}) async-start(bf16[4,480,256]{2,1,0:T(8,128)(2,1)} %slice.250), calls=%async_computation.2 | async-start | bytes 1966080 | tf_op jit(solution)/shard_map/all_to_all | solution.py:241
  35.9 28.1 %collective-permute-done = bf16[784,512]{1,0:T(8,128)(2,1)} collective-permute-done((bf16[784,512]{1,0:T(8,128)(2,1)S(1)}, bf16[784,512]{1,0:T(8,128)(2,1)}, u32[]{:S(2)}, u32[]{:S(2)}) %collective-permute-start) | collective-permute-done | bytes 802848 | tf_op jit(solution)/shard_map/ppermute | solution.py:227
  65.5 4.7 %all-to-all-start.1 = ((bf16[4,560,256]{2,1,0:T(8,128)(2,1)}), bf16[4,560,256]{2,1,0:T(8,128)(2,1)}, u32[]{:S(2)}, u32[]{:S(2)}) async-start(bf16[4,560,256]{2,1,0:T(8,128)(2,1)} %slice.248), calls=%async_computation.1 | async-start | bytes 2293760 | tf_op jit(solution)/shard_map/all_to_all | solution.py:241
  82.0 19.7 %collective-permute-done.7 = bf16[784,512]{1,0:T(8,128)(2,1)} collective-permute-done((bf16[784,512]{1,0:T(8,128)(2,1)S(1)}, bf16[784,512]{1,0:T(8,128)(2,1)}, u32[]{:S(2)}, u32[]{:S(2)}) %collective-permute-start.7) | collective-permute-done | bytes 802848 | tf_op jit(solution)/shard_map/ppermute | solution.py:236
  107.5 4.5 %copy-done = bf16[4,3,2048,256]{3,2,1,0:T(8,128)(2,1)} copy-done((bf16[4,3,2048,256]{3,2,1,0:T(8,128)(2,1)}, bf16[4,3,2048,256]{3,2,1,0:T(8,128)(2,1)S(1)}, u32[]{:S(2)}) %copy-start) | copy-done | bytes 12582936
  112.0 4.9 %all-to-all-start = ((bf16[4,640,256]{2,1,0:T(8,128)(2,1)}), bf16[4,640,256]{2,1,0:T(8,128)(2,1)S(1)}, u32[]{:S(2)}, u32[]{:S(2)}) async-start(bf16[4,640,256]{2,1,0:T(8,128)(2,1)} %slice.246), calls=%async_computation | async-start | bytes 2621440 | tf_op jit(solution)/shard_map/all_to_all | solution.py:241
  117.0 18.5 %collective-permute-done.2 = bf16[784,512]{1,0:T(8,128)(2,1)} collective-permute-done((bf16[784,512]{1,0:T(8,128)(2,1)}, bf16[784,512]{1,0:T(8,128)(2,1)}, u32[]{:S(2)}, u32[]{:S(2)}) %collective-permute-start.2) | collective-permute-done | bytes 802848 | tf_op jit(solution)/shard_map/ppermute | solution.py:236
  139.8 4.6 %copy-done.1 = bf16[4,3,2048,256]{3,2,1,0:T(8,128)(2,1)S(1)} copy-done((bf16[4,3,2048,256]{3,2,1,0:T(8,128)(2,1)S(1)}, bf16[4,3,2048,256]{3,2,1,0:T(8,128)(2,1)}, u32[]{:S(2)}) %copy-start.1) | copy-done | bytes 12582936
  144.4 4.2 %shard_map.78.refs_4_ = bf16[4,3,2048,256]{3,2,1,0:T(8,128)(2,1)S(1)} custom-call(s32[5]{0:T(128)S(1)} %stack.101.place, f32[1,2048]{1,0:T(1,128)S(1)} %bitcast.100, bf16[1,1,784,512]{3,2,1,0:T(8,128)(2,1)} %bitcast.16.refs_0_, bf16[1,1,784,512]{3,2,1,0:T(8,128)(2,1)} %bitcast.17.refs_1_, ...), custom_call_target="tpu_custom_call", output_to_operand_aliasing={{}: (6, {})} | custom-call | flops 9437184 | bytes 6291456 | tf_op jit(solution)/shard_map/pallas_call | solution.py:40
  152.6 3.9 %shard_map.79.refs_4_ = bf16[4,3,2048,256]{3,2,1,0:T(8,128)(2,1)S(1)} custom-call(s32[5]{0:T(128)S(1)} %stack.101.place, f32[1,2048]{1,0:T(1,128)S(1)} %bitcast.101, bf16[1,1,784,512]{3,2,1,0:T(8,128)(2,1)S(1)} %bitcast.92, bf16[1,1,784,512]{3,2,1,0:T(8,128)(2,1)} %bitcast.13.refs_1_, ...), custom_call_target="tpu_custom_call", output_to_operand_aliasing={{}: (6, {})} | custom-call | flops 9437184 | bytes 6291456 | tf_op jit(solution)/shard_map/pallas_call | solution.py:40
  156.5 4.5 %copy-done.2 = bf16[4,3,2048,256]{3,2,1,0:T(8,128)(2,1)} copy-done((bf16[4,3,2048,256]{3,2,1,0:T(8,128)(2,1)}, bf16[4,3,2048,256]{3,2,1,0:T(8,128)(2,1)S(1)}, u32[]{:S(2)}) %copy-start.2) | copy-done | bytes 12582936
  161.5 4.6 %copy-done.3 = bf16[4,3,2048,256]{3,2,1,0:T(8,128)(2,1)S(1)} copy-done((bf16[4,3,2048,256]{3,2,1,0:T(8,128)(2,1)S(1)}, bf16[4,3,2048,256]{3,2,1,0:T(8,128)(2,1)}, u32[]{:S(2)}) %copy-start.3) | copy-done | bytes 12582936
  166.1 4.0 %shard_map.80.refs_0_ = bf16[4,3,2048,256]{3,2,1,0:T(8,128)(2,1)S(1)} custom-call(s32[5]{0:T(128)S(1)} %stack.101.place, f32[1,2048]{1,0:T(1,128)S(1)} %bitcast.102, bf16[1,1,784,512]{3,2,1,0:T(8,128)(2,1)S(1)} %bitcast.93, bf16[1,1,784,512]{3,2,1,0:T(8,128)(2,1)} %bitcast.9.refs_1_, ...), custom_call_target="tpu_custom_call", output_to_operand_aliasing={{}: (6, {})} | custom-call | flops 9437184 | bytes 6291456 | tf_op jit(solution)/shard_map/pallas_call | solution.py:40
  170.2 4.5 %copy-done.4 = bf16[4,3,2048,256]{3,2,1,0:T(8,128)(2,1)} copy-done((bf16[4,3,2048,256]{3,2,1,0:T(8,128)(2,1)}, bf16[4,3,2048,256]{3,2,1,0:T(8,128)(2,1)S(1)}, u32[]{:S(2)}) %copy-start.4) | copy-done | bytes 12582936
  174.7 4.6 %copy-done.5 = bf16[4,3,2048,256]{3,2,1,0:T(8,128)(2,1)S(1)} copy-done((bf16[4,3,2048,256]{3,2,1,0:T(8,128)(2,1)S(1)}, bf16[4,3,2048,256]{3,2,1,0:T(8,128)(2,1)}, u32[]{:S(2)}) %copy-start.5) | copy-done | bytes 12582936
  179.2 7.8 %shard_map.84 = f32[12,4,256]{2,1,0:T(4,128)S(1)} custom-call(s32[15]{0:T(128)S(1)} %get-tuple-element.73.scalars, bf16[4,3,2048,256]{3,2,1,0:T(8,128)(2,1)S(1)} %copy-done.5, s32[12,1,256]{2,1,0:T(1,128)S(1)} %compare_select_fusion.refs_1_, bf16[4,320,256]{2,1,0:T(8,128)(2,1)S(1)} %copy-done.7, bf16[4,320,256]{2,1,0:T(8,128)(2,1)} %collective-permute-done.20.refs_3_), custom_call_target="tpu_custom_call" | custom-call | flops 4026531840 | bytes 13893632 | tf_op jit(solution)/shard_map/pallas_call | solution.py:134
  187.1 10.2 %shard_map.83 = f32[12,4,256]{2,1,0:T(4,128)S(1)} custom-call(s32[15]{0:T(128)S(1)} %get-tuple-element.72.scalars, bf16[4,3,2048,256]{3,2,1,0:T(8,128)(2,1)S(1)} %copy-done.5, s32[12,1,256]{2,1,0:T(1,128)S(1)} %compare_select_fusion.1.refs_1_, bf16[4,480,256]{2,1,0:T(8,128)(2,1)} %all-to-all-done.2.refs_2_, bf16[4,480,256]{2,1,0:T(8,128)(2,1)} %collective-permute-done.19.refs_3_), custom_call_target="tpu_custom_call" | custom-call | flops 6039797760 | bytes 14548992 | tf_op jit(solution)/shard_map/pallas_call | solution.py:134
  197.3 2.6 %collective-permute-done.18.refs_3_ = bf16[4,560,256]{2,1,0:T(8,128)(2,1)} collective-permute-done((bf16[4,560,256]{2,1,0:T(8,128)(2,1)}, bf16[4,560,256]{2,1,0:T(8,128)(2,1)}, u32[]{:S(2)}, u32[]{:S(2)}) %collective-permute-start.18) | collective-permute-done | bytes 1146912 | tf_op jit(solution)/shard_map/ppermute | solution.py:230
  199.9 11.2 %shard_map.82 = f32[12,4,256]{2,1,0:T(4,128)S(1)} custom-call(s32[15]{0:T(128)S(1)} %get-tuple-element.71.scalars, bf16[4,3,2048,256]{3,2,1,0:T(8,128)(2,1)S(1)} %copy-done.5, s32[12,1,256]{2,1,0:T(1,128)S(1)} %compare_select_fusion.2.refs_1_, bf16[4,560,256]{2,1,0:T(8,128)(2,1)} %all-to-all-done.1.refs_2_, bf16[4,560,256]{2,1,0:T(8,128)(2,1)} %collective-permute-done.18.refs_3_), custom_call_target="tpu_custom_call" | custom-call | flops 7046430720 | bytes 14876672 | tf_op jit(solution)/shard_map/pallas_call | solution.py:134
  211.1 16.4 %collective-permute-done.17.refs_3_ = bf16[4,640,256]{2,1,0:T(8,128)(2,1)S(1)} collective-permute-done((bf16[4,640,256]{2,1,0:T(8,128)(2,1)S(1)}, bf16[4,640,256]{2,1,0:T(8,128)(2,1)S(1)}, u32[]{:S(2)}, u32[]{:S(2)}) %collective-permute-start.17) | collective-permute-done | bytes 1310752 | tf_op jit(solution)/shard_map/ppermute | solution.py:230
  227.5 11.1 %shard_map.81 = f32[12,4,256]{2,1,0:T(4,128)S(1)} custom-call(s32[15]{0:T(128)S(1)} %get-tuple-element.70.scalars, bf16[4,3,2048,256]{3,2,1,0:T(8,128)(2,1)S(1)} %copy-done.5, s32[12,1,256]{2,1,0:T(1,128)S(1)} %compare_select_fusion.3.refs_1_, bf16[4,640,256]{2,1,0:T(8,128)(2,1)S(1)} %all-to-all-done.refs_2_, ...), custom_call_target="tpu_custom_call" | custom-call | flops 8053063680 | bytes 15204352 | tf_op jit(solution)/shard_map/pallas_call | solution.py:134
  239.4 4.3 %collective-permute-start.23 = (f32[4,768]{1,0:T(4,128)S(1)}, f32[4,768]{1,0:T(4,128)S(1)}, u32[]{:S(2)}, u32[]{:S(2)}) collective-permute-start(f32[4,768]{1,0:T(4,128)S(1)} %get-tuple-element.21), channel_id=1, source_target_pairs={{0,24},{4,28},{8,16},{12,20},{16,8},{20,12},{24,0},{28,4},{1,25},{... | collective-permute-start | bytes 36872 | tf_op jit(solution)/shard_map/ppermute | solution.py:227
  (142 shorter events, 48.0 us)
Async XLA Ops:
  2.6 22.2 %all-to-all-start.3 = ((bf16[4,320,256]{2,1,0:T(8,128)(2,1)}), bf16[4,320,256]{2,1,0:T(8,128)(2,1)S(1)}, u32[]{:S(2)}, u32[]{:S(2)}) async-start(bf16[4,320,256]{2,1,0:T(8,128)(2,1)} %slice.252), calls=%async_computation.3 | async-start | bytes 1310720 | tf_op jit(solution)/shard_map/all_to_all | solution.py:241
  24.8 40.7 %all-to-all-start.2 = ((bf16[4,480,256]{2,1,0:T(8,128)(2,1)}), bf16[4,480,256]{2,1,0:T(8,128)(2,1)}, u32[]{:S(2)}, u32[]{:S(2)}) async-start(bf16[4,480,256]{2,1,0:T(8,128)(2,1)} %slice.250), calls=%async_computation.2 | async-start | bytes 1966080 | tf_op jit(solution)/shard_map/all_to_all | solution.py:241
  29.2 34.8 %collective-permute-start = (bf16[784,512]{1,0:T(8,128)(2,1)S(1)}, bf16[784,512]{1,0:T(8,128)(2,1)}, u32[]{:S(2)}, u32[]{:S(2)}) collective-permute-start(bf16[784,512]{1,0:T(8,128)(2,1)S(1)} %constant_dynamic-update-slice_fusion), channel_id=1, source_target_pairs={{0,8},{4,12},{8,0},{12,4},{16,24},{20,28},{24,16},{28,20},{1,9},{5... | collective-permute-start | bytes 2408456 | tf_op jit(solution)/shard_map/ppermute | solution.py:227
  31.2 39.2 %collective-permute-start.6 = (bf16[784,512]{1,0:T(8,128)(2,1)S(1)}, bf16[784,512]{1,0:T(8,128)(2,1)S(1)}, u32[]{:S(2)}, u32[]{:S(2)}) collective-permute-start(bf16[784,512]{1,0:T(8,128)(2,1)S(1)} %constant_dynamic-update-slice_fusion), channel_id=1, source_target_pairs={{8,16},{12,20},{16,8},{20,12},{9,17},{13,21},{17,9},{21,13},{10,18... | collective-permute-start | bytes 2408456 | tf_op jit(solution)/shard_map/ppermute | solution.py:236
  31.9 47.4 %collective-permute-start.14 = (bf16[784,512]{1,0:T(8,128)(2,1)S(1)}, bf16[784,512]{1,0:T(8,128)(2,1)S(1)}, u32[]{:S(2)}, u32[]{:S(2)}) collective-permute-start(bf16[784,512]{1,0:T(8,128)(2,1)S(1)} %constant_dynamic-update-slice_fusion), channel_id=1, source_target_pairs={{0,2},{1,3},{2,0},{3,1},{4,6},{5,7},{6,4},{7,5},{8,10},{9,11},{10,... | collective-permute-start | bytes 2408456 | tf_op jit(solution)/shard_map/ppermute | solution.py:233
  33.5 69.5 %collective-permute-start.15 = (bf16[784,512]{1,0:T(8,128)(2,1)S(1)}, bf16[784,512]{1,0:T(8,128)(2,1)S(1)}, u32[]{:S(2)}, u32[]{:S(2)}) collective-permute-start(bf16[784,512]{1,0:T(8,128)(2,1)S(1)} %constant_dynamic-update-slice_fusion), channel_id=1, source_target_pairs={{0,1},{1,0},{2,3},{3,2},{4,5},{5,4},{6,7},{7,6},{8,9},{9,8},{10,11... | collective-permute-start | bytes 2408456 | tf_op jit(solution)/shard_map/ppermute | solution.py:233
  63.9 15.4 %collective-permute-start.1 = (bf16[784,512]{1,0:T(8,128)(2,1)}, bf16[784,512]{1,0:T(8,128)(2,1)}, u32[]{:S(2)}, u32[]{:S(2)}) collective-permute-start(bf16[784,512]{1,0:T(8,128)(2,1)} %collective-permute-done), channel_id=1, source_target_pairs={{8,16},{12,20},{16,8},{20,12},{9,17},{13,21},{17,9},{21,13},{10,18... | collective-permute-start | bytes 2408456 | tf_op jit(solution)/shard_map/ppermute | solution.py:236
  65.5 46.5 %all-to-all-start.1 = ((bf16[4,560,256]{2,1,0:T(8,128)(2,1)}), bf16[4,560,256]{2,1,0:T(8,128)(2,1)}, u32[]{:S(2)}, u32[]{:S(2)}) async-start(bf16[4,560,256]{2,1,0:T(8,128)(2,1)} %slice.248), calls=%async_computation.1 | async-start | bytes 2293760 | tf_op jit(solution)/shard_map/all_to_all | solution.py:241
  70.4 31.3 %collective-permute-start.7 = (bf16[784,512]{1,0:T(8,128)(2,1)S(1)}, bf16[784,512]{1,0:T(8,128)(2,1)}, u32[]{:S(2)}, u32[]{:S(2)}) collective-permute-start(bf16[784,512]{1,0:T(8,128)(2,1)S(1)} %collective-permute-done.6), channel_id=1, source_target_pairs={{8,0},{12,4},{16,24},{20,28},{9,1},{13,5},{17,25},{21,29},{10,2},{... | collective-permute-start | bytes 2408456 | tf_op jit(solution)/shard_map/ppermute | solution.py:236
  77.8 27.0 %collective-permute-start.11 = (bf16[784,512]{1,0:T(8,128)(2,1)}, bf16[784,512]{1,0:T(8,128)(2,1)}, u32[]{:S(2)}, u32[]{:S(2)}) collective-permute-start(bf16[784,512]{1,0:T(8,128)(2,1)} %collective-permute-done), channel_id=1, source_target_pairs={{0,2},{1,3},{2,0},{3,1},{4,6},{5,7},{6,4},{7,5},{8,10},{9,11},{10,... | collective-permute-start | bytes 2408456 | tf_op jit(solution)/shard_map/ppermute | solution.py:233
  79.3 25.2 %collective-permute-start.16 = (bf16[784,512]{1,0:T(8,128)(2,1)S(1)}, bf16[784,512]{1,0:T(8,128)(2,1)S(1)}, u32[]{:S(2)}, u32[]{:S(2)}) collective-permute-start(bf16[784,512]{1,0:T(8,128)(2,1)S(1)} %collective-permute-done.14), channel_id=1, source_target_pairs={{0,1},{1,0},{2,3},{3,2},{4,5},{5,4},{6,7},{7,6},{8,9},{9,8},{10,11... | collective-permute-start | bytes 2408456 | tf_op jit(solution)/shard_map/ppermute | solution.py:233
  79.3 56.1 %collective-permute-start.2 = (bf16[784,512]{1,0:T(8,128)(2,1)}, bf16[784,512]{1,0:T(8,128)(2,1)}, u32[]{:S(2)}, u32[]{:S(2)}) collective-permute-start(bf16[784,512]{1,0:T(8,128)(2,1)} %collective-permute-done.1), channel_id=1, source_target_pairs={{8,0},{12,4},{16,24},{20,28},{9,1},{13,5},{17,25},{21,29},{10,2},{... | collective-permute-start | bytes 2408456 | tf_op jit(solution)/shard_map/ppermute | solution.py:236
  101.7 37.0 %collective-permute-start.12 = (bf16[784,512]{1,0:T(8,128)(2,1)}, bf16[784,512]{1,0:T(8,128)(2,1)}, u32[]{:S(2)}, u32[]{:S(2)}) collective-permute-start(bf16[784,512]{1,0:T(8,128)(2,1)} %collective-permute-done), channel_id=1, source_target_pairs={{0,1},{1,0},{2,3},{3,2},{4,5},{5,4},{6,7},{7,6},{8,9},{9,8},{10,11... | collective-permute-start | bytes 2408456 | tf_op jit(solution)/shard_map/ppermute | solution.py:233
  103.0 36.3 %collective-permute-start.8 = (bf16[784,512]{1,0:T(8,128)(2,1)S(1)}, bf16[784,512]{1,0:T(8,128)(2,1)}, u32[]{:S(2)}, u32[]{:S(2)}) collective-permute-start(bf16[784,512]{1,0:T(8,128)(2,1)S(1)} %broadcast_select_fusion), channel_id=1, source_target_pairs={{0,2},{1,3},{2,0},{3,1},{4,6},{5,7},{6,4},{7,5},{8,10},{9,11},{10,... | collective-permute-start | bytes 2408456 | tf_op jit(solution)/shard_map/ppermute | solution.py:233
  104.5 45.9 %collective-permute-start.9 = (bf16[784,512]{1,0:T(8,128)(2,1)S(1)}, bf16[784,512]{1,0:T(8,128)(2,1)}, u32[]{:S(2)}, u32[]{:S(2)}) collective-permute-start(bf16[784,512]{1,0:T(8,128)(2,1)S(1)} %broadcast_select_fusion), channel_id=1, source_target_pairs={{0,1},{1,0},{2,3},{3,2},{4,5},{5,4},{6,7},{7,6},{8,9},{9,8},{10,11... | collective-permute-start | bytes 2408456 | tf_op jit(solution)/shard_map/ppermute | solution.py:233
  104.8 34.6 %collective-permute-start.13 = (bf16[784,512]{1,0:T(8,128)(2,1)}, bf16[784,512]{1,0:T(8,128)(2,1)}, u32[]{:S(2)}, u32[]{:S(2)}) collective-permute-start(bf16[784,512]{1,0:T(8,128)(2,1)} %collective-permute-done.11), channel_id=1, source_target_pairs={{0,1},{1,0},{2,3},{3,2},{4,5},{5,4},{6,7},{7,6},{8,9},{9,8},{10,11... | collective-permute-start | bytes 2408456 | tf_op jit(solution)/shard_map/ppermute | solution.py:233
  112.0 49.0 %all-to-all-start = ((bf16[4,640,256]{2,1,0:T(8,128)(2,1)}), bf16[4,640,256]{2,1,0:T(8,128)(2,1)S(1)}, u32[]{:S(2)}, u32[]{:S(2)}) async-start(bf16[4,640,256]{2,1,0:T(8,128)(2,1)} %slice.246), calls=%async_computation | async-start | bytes 2621440 | tf_op jit(solution)/shard_map/all_to_all | solution.py:241
  136.7 13.7 %collective-permute-start.3 = (bf16[784,512]{1,0:T(8,128)(2,1)S(1)}, bf16[784,512]{1,0:T(8,128)(2,1)}, u32[]{:S(2)}, u32[]{:S(2)}) collective-permute-start(bf16[784,512]{1,0:T(8,128)(2,1)S(1)} %broadcast_select_fusion.1), channel_id=1, source_target_pairs={{0,2},{1,3},{2,0},{3,1},{4,6},{5,7},{6,4},{7,5},{8,10},{9,11},{10,... | collective-permute-start | bytes 2408456 | tf_op jit(solution)/shard_map/ppermute | solution.py:233
  138.7 35.9 %collective-permute-start.20 = (bf16[4,320,256]{2,1,0:T(8,128)(2,1)}, bf16[4,320,256]{2,1,0:T(8,128)(2,1)}, u32[]{:S(2)}, u32[]{:S(2)}) collective-permute-start(bf16[4,320,256]{2,1,0:T(8,128)(2,1)} %copy-done.6), channel_id=1, source_target_pairs={{0,4},{4,0},{8,12},{12,8},{16,20},{20,16},{24,28},{28,24},{1,5},{5... | collective-permute-start | bytes 1966088 | tf_op jit(solution)/shard_map/ppermute | solution.py:230
  139.3 21.7 %collective-permute-start.4 = (bf16[784,512]{1,0:T(8,128)(2,1)S(1)}, bf16[784,512]{1,0:T(8,128)(2,1)}, u32[]{:S(2)}, u32[]{:S(2)}) collective-permute-start(bf16[784,512]{1,0:T(8,128)(2,1)S(1)} %broadcast_select_fusion.1), channel_id=1, source_target_pairs={{0,1},{1,0},{2,3},{3,2},{4,5},{5,4},{6,7},{7,6},{8,9},{9,8},{10,11... | collective-permute-start | bytes 2408456 | tf_op jit(solution)/shard_map/ppermute | solution.py:233
  139.3 11.7 %collective-permute-start.10 = (bf16[784,512]{1,0:T(8,128)(2,1)}, bf16[784,512]{1,0:T(8,128)(2,1)S(1)}, u32[]{:S(2)}, u32[]{:S(2)}) collective-permute-start(bf16[784,512]{1,0:T(8,128)(2,1)} %collective-permute-done.8), channel_id=1, source_target_pairs={{0,1},{1,0},{2,3},{3,2},{4,5},{5,4},{6,7},{7,6},{8,9},{9,8},{10,11... | collective-permute-start | bytes 2408456 | tf_op jit(solution)/shard_map/ppermute | solution.py:233
  150.4 36.7 %collective-permute-start.19 = (bf16[4,480,256]{2,1,0:T(8,128)(2,1)}, bf16[4,480,256]{2,1,0:T(8,128)(2,1)}, u32[]{:S(2)}, u32[]{:S(2)}) collective-permute-start(bf16[4,480,256]{2,1,0:T(8,128)(2,1)} %all-to-all-done.2.refs_2_), channel_id=1, source_target_pairs={{0,4},{4,0},{8,12},{12,8},{16,20},{20,16},{24,28},{28,24},{1,5},{5... | collective-permute-start | bytes 2949128 | tf_op jit(solution)/shard_map/ppermute | solution.py:230
  151.0 48.9 %collective-permute-start.18 = (bf16[4,560,256]{2,1,0:T(8,128)(2,1)}, bf16[4,560,256]{2,1,0:T(8,128)(2,1)}, u32[]{:S(2)}, u32[]{:S(2)}) collective-permute-start(bf16[4,560,256]{2,1,0:T(8,128)(2,1)} %all-to-all-done.1.refs_2_), channel_id=1, source_target_pairs={{0,4},{4,0},{8,12},{12,8},{16,20},{20,16},{24,28},{28,24},{1,5},{5... | collective-permute-start | bytes 3440648 | tf_op jit(solution)/shard_map/ppermute | solution.py:230
  161.0 66.5 %collective-permute-start.17 = (bf16[4,640,256]{2,1,0:T(8,128)(2,1)S(1)}, bf16[4,640,256]{2,1,0:T(8,128)(2,1)S(1)}, u32[]{:S(2)}, u32[]{:S(2)}) collective-permute-start(bf16[4,640,256]{2,1,0:T(8,128)(2,1)S(1)} %all-to-all-done.refs_2_), channel_id=1, source_target_pairs={{0,4},{4,0},{8,12},{12,8},{16,20},{20,16},{24,28},{28,24},{1,5},{5... | collective-permute-start | bytes 3932168 | tf_op jit(solution)/shard_map/ppermute | solution.py:230
  (21 other events, 189.8 us)

commit v2 on v0

v2 whole, which is shorter than its diff:
```python
import functools

import jax
import jax.numpy as jnp
from jax import lax
from jax.experimental import pallas as pl
from jax.experimental.pallas import tpu as pltpu
from jax.sharding import PartitionSpec as P

EPS = 1e-05
LOW = -3.0e38
LANES = 128
TILE = 16
PIECES = (8, 7, 5)
ROWS = 256
TOKEN_BYTES = 17 * 2**20


def assemble_kernel(near_first, gain_ref, *refs):
    target = refs[-1]
    sources = []
    for away, ref in enumerate(refs[:-1]):
        for index in range(ref.shape[0]):
            part = lax.axis_index("vocab") ^ (2 * index + away) if near_first else index
            sources.append((ref, index, part))
    features = refs[0].shape[3]
    for start in range(0, target.shape[3], LANES):
        lanes = slice(start, start + LANES)
        square = sum(
            jnp.sum(jnp.square(ref[at, 0, lanes].astype(jnp.float32)), axis=1, keepdims=True) for ref, at, _ in sources
        )
        scale = lax.rsqrt(square / (features * len(sources)) + EPS)
        for ref, at, part in sources:
            first = pl.multiple_of(part * features, features)
            value = ref[at, 0, lanes].astype(jnp.float32) * scale * gain_ref[:, pl.ds(first, features)]
            target[0, 0, pl.ds(first, features), lanes] = value.T.astype(target.dtype)


def assemble(gain, sources, rows):
    _, count, slots, features = sources[0].shape
    splits = slots // rows
    wide = features * sum(y.shape[0] for y in sources)
    return pl.pallas_call(
        functools.partial(assemble_kernel, len(sources) > 1),
        grid=(count, splits),
        in_specs=[pl.BlockSpec((1, wide), lambda i, j: (0, 0))]
        + [pl.BlockSpec((y.shape[0], 1, rows, features), lambda i, j: (0, i, j, 0)) for y in sources],
        out_specs=pl.BlockSpec((1, 1, wide, rows), lambda i, j: (i, j, 0, 0)),
        out_shape=jax.ShapeDtypeStruct((count, splits, wide, rows), sources[0].dtype),
        compiler_params=pltpu.CompilerParams(vmem_limit_bytes=24 * 2**20),
        cost_estimate=pl.CostEstimate(
            flops=6 * count * splits * rows * wide,
            bytes_accessed=4 * count * splits * rows * wide,
            transcendentals=count * splits * rows,
        ),
    )(gain, *sources)


def stats_kernel(plan, counts, start_ref, lens_ref, owner_ref, *refs):
    out_ref, head, held, logits, ids, order, sems, token_sems = refs[-8:]
    members = []
    for count in counts:
        members.append(refs[:count])
        refs = refs[count:]
    token_refs, id_refs, head_refs, before = members
    splits, _, rows = token_refs[0].shape[1:]
    groups = len(token_refs) * token_refs[0].shape[0]
    width, depth = head.shape[0], head_refs[0].shape[-1]
    real, base = plan.columns()

    copies = []
    for source, group in plan.head_parts(head_refs):
        lane = pl.multiple_of(group * depth, LANES)
        copies.append(pltpu.make_async_copy(source, head.at[:, pl.ds(lane, depth)], sems.at[len(copies)]))
    for copy in copies:
        copy.start()

    def one_group(group, live):
        def one_sequence(index, load):
            return load + jnp.where(owner_ref[index] == plan.group(group), lens_ref[index], 0)

        load = lax.fori_loop(0, lens_ref.shape[0], one_sequence, jnp.int32(0))
        for split in range(splits):
            order[live] = group * splits + split
            live = live + jnp.where(start_ref[0] + split * rows < load, 1, 0)
        return live

    live = lax.fori_loop(0, groups, one_group, jnp.int32(0))

    def fetch(step, slot):
        group, split = order[step] // splits, order[step] % splits
        each = token_refs[0].shape[0]
        for index, source in enumerate(token_refs):

            @pl.when(group // each == index)
            def _():
                pltpu.make_async_copy(source.at[group % each, split], held.at[slot], token_sems.at[slot]).start()

    @pl.when(live > 0)
    def _():
        fetch(0, 0)

    out_ref[...] = jnp.zeros_like(out_ref)
    for index, source in enumerate(id_refs):
        places = source[...] - base
        ids[pl.ds(index * source.shape[0], source.shape[0])] = jnp.where(places < real, places, -1)
    for copy in copies:
        copy.wait()

    def body(step, carry):
        slot = lax.rem(step, 2)
        pltpu.make_async_copy(token_refs[0].at[0, 0], held.at[slot], token_sems.at[slot]).wait()

        @pl.when(step + 1 < live)
        def _():
            fetch(step + 1, 1 - slot)

        logits[...] = jnp.dot(head[...], held[slot], preferred_element_type=jnp.float32)

        @pl.when(real < width)
        def _():
            column = lax.broadcasted_iota(jnp.int32, (width - plan.least, rows), 0) + plan.least
            logits[plan.least :] = jnp.where(column < real, logits[plan.least :], LOW)

        block = order[step]
        target = plan.slot(block // splits)
        split = block % splits
        column = lax.broadcasted_iota(jnp.int32, (width, LANES), 0)
        for start in range(0, rows, LANES):
            lanes = slice(start, start + LANES)
            values = logits[:, lanes]
            top = jnp.max(values, axis=0, keepdims=True)
            shifted = jnp.maximum(values - top, -1.0e4)
            expo = jnp.exp(shifted)
            total = jnp.sum(expo, axis=0, keepdims=True)
            weighted = jnp.sum(expo * shifted, axis=0, keepdims=True)
            picked = jnp.sum(jnp.where(column == ids[block, :, lanes], values, 0.0), axis=0, keepdims=True)
            place = pl.ds(pl.multiple_of(split * rows + start, LANES), LANES)
            if before:
                top, total, weighted, picked = joined(
                    [(top, total, weighted, picked), [before[0][target, index : index + 1, place] for index in range(4)]]
                )
            for index, member in enumerate((top, total, weighted, picked)):
                out_ref[target, index : index + 1, place] = member
        return carry

    lax.fori_loop(0, live, body, 0)


def stats(plan, start, seq_lens, seq_owner, tokens, ids, heads, before):
    groups, splits, wide, rows = tokens[0].shape
    groups *= len(tokens)
    width = plan.width
    smem = pl.BlockSpec(memory_space=pltpu.SMEM)
    vmem = pl.BlockSpec(memory_space=pltpu.VMEM)
    anywhere = pl.BlockSpec(memory_space=pl.ANY)
    return pl.pallas_call(
        functools.partial(stats_kernel, plan, (len(tokens), len(ids), len(heads), len(before))),
        in_specs=[smem] * 3
        + [anywhere] * len(tokens)
        + [vmem] * len(ids)
        + [anywhere] * len(heads)
        + [vmem] * len(before),
        out_specs=vmem,
        scratch_shapes=[
            pltpu.VMEM((width, wide), jnp.bfloat16),
            pltpu.VMEM((2, wide, rows), jnp.bfloat16),
            pltpu.VMEM((width, rows), jnp.float32),
            pltpu.VMEM((groups * splits, 1, rows), jnp.int32),
            pltpu.SMEM((groups * splits + 1,), jnp.int32),
            pltpu.SemaphoreType.DMA((wide // heads[0].shape[-1],)),
            pltpu.SemaphoreType.DMA((2,)),
        ],
        out_shape=jax.ShapeDtypeStruct((groups, 4, splits * rows), jnp.float32),
        compiler_params=pltpu.CompilerParams(vmem_limit_bytes=24 * 2**20),
        cost_estimate=pl.CostEstimate(
            flops=2 * groups * splits * rows * wide * width,
            bytes_accessed=groups * splits * rows * wide * 2 + wide * width * 2,
            transcendentals=groups * splits * rows * width,
        ),
    )(start, seq_lens, seq_owner, *tokens, *ids, *heads, *before)


class Spread:
    def __init__(self, breadth, groups):
        self.breadth = breadth
        self.cuts = [breadth * index // groups // TILE * TILE for index in range(groups)] + [breadth]
        sizes = [end - start for start, end in zip(self.cuts, self.cuts[1:])]
        self.width, self.least = max(sizes), min(sizes)

    def spread(self, turned):
        turned = jnp.pad(turned, ((0, self.cuts[-2] + self.width - self.breadth), (0, 0)))
        return jnp.stack([turned[start : start + self.width] for start in self.cuts[:-1]])

    def columns(self):
        position = lax.axis_index("dp")
        start, end = 0, self.breadth
        for index, (first, last) in enumerate(zip(self.cuts, self.cuts[1:])):
            start = jnp.where(position == index, first, start)
            end = jnp.where(position == index, last, end)
        return end - start, lax.axis_index("vocab") * self.breadth + start

    def head_parts(self, refs):
        return [(refs[0], 0)]

    def group(self, group):
        return group

    def slot(self, group):
        return group


class Line:
    def __init__(self, breadth, chunk, start, width):
        self.breadth, self.chunk, self.start = breadth, chunk, start
        self.width = self.least = width

    def columns(self):
        hi = lax.axis_index("dp") // 2
        return self.width, lax.axis_index("vocab") * self.breadth + hi * self.chunk + self.start

    def head_parts(self, refs):
        position = lax.axis_index("dp")
        hi, low = position // 2, position % 2
        here = pl.ds(self.start, self.width)
        mine = [refs[0].at[hi, here], *refs[2:5]]
        other = [refs[1].at[here], *(refs[5].at[index] for index in range(3))]
        found = [(source, 2 * (hi ^ step) + low) for step, source in enumerate(mine)]
        return found + [(source, 2 * (hi ^ step) + (low ^ 1)) for step, source in enumerate(other)]

    def slot(self, group):
        hi = lax.axis_index("dp") // 2
        middle = (hi == 1) | (hi == 2)
        return jnp.where(middle & (group >= 2), 5 - group, group)

    def group(self, group):
        position = lax.axis_index("dp")
        return 2 * (position // 2 ^ self.slot(group)) + position % 2


def after(x, *others):
    return lax.optimization_barrier((x, *others))[0]


def joined(members):
    best = functools.reduce(jnp.maximum, [top for top, _, _, _ in members])
    total = weighted = picked = 0.0
    for top, other_total, other_weighted, other_picked in members:
        shift = jnp.maximum(top - best, -1.0e4)
        factor = jnp.exp(shift)
        total += other_total * factor
        weighted += factor * (other_weighted + other_total * shift)
        picked += other_picked
    return best, total, weighted, picked


def merge(members):
    return jnp.stack(joined([[member[..., index, :] for index in range(4)] for member in members]), axis=-2)


def by_collectives(hidden, gain, head, target_ids, seq_lens, seq_owner):
    groups = lax.axis_size("dp")
    parts = lax.axis_size("vocab")
    slots, features = hidden.shape
    depth, breadth = head.shape
    plan = Spread(breadth, groups)
    ids = lax.all_gather(target_ids, "dp", axis=0)

    columns = lax.all_to_all(plan.spread(head.T), "dp", split_axis=0, concat_axis=0, tiled=True)
    columns = columns.transpose(1, 0, 2).reshape(plan.width, groups * depth)

    splits = -(-groups * slots * features * parts * 2 // TOKEN_BYTES)
    while slots % splits or (slots // splits) % LANES:
        splits += 1
    rows = slots // splits

    def score(start):
        piece = lax.dynamic_slice_in_dim(hidden, start, rows)
        x = lax.all_gather(piece, ("vocab", "dp"), axis=0).reshape(parts, groups, rows, features)
        x = assemble(gain, [x], rows)
        wanted = lax.dynamic_slice_in_dim(ids, start, rows, axis=1)[:, None]
        return stats(plan, start[None], seq_lens, seq_owner, [x], [wanted], [columns], [])

    found = lax.map(score, jnp.arange(splits, dtype=jnp.int32) * rows)
    found = found.transpose(1, 2, 0, 3).reshape(groups, 4, slots)
    found = lax.all_to_all(found, "dp", split_axis=0, concat_axis=0, tiled=True)
    mine = lax.all_gather(merge(list(found)), "vocab", axis=0)
    return merge(list(mine))


def by_axes(hidden, gain, head, target_ids, seq_lens, seq_owner):
    groups = lax.axis_size("dp")
    parts = lax.axis_size("vocab")
    tall = groups // 2
    hi = lax.axis_index("dp") // 2
    slots, features = hidden.shape
    depth, breadth = head.shape
    splits = slots // ROWS
    middle = (hi == 1) | (hi == 2)
    chunk = breadth // tall
    ends = [chunk * sum(PIECES[:n]) // sum(PIECES) // TILE * TILE for n in range(len(PIECES))] + [chunk]
    cuts = [(start, end - start) for start, end in zip(ends, ends[1:])]

    def swap_hi(x, step):
        return lax.ppermute(x, "dp", [(g, g ^ (2 * step)) for g in range(groups)])

    def swap_lo(x):
        return lax.ppermute(x, "dp", [(g, g ^ 1) for g in range(groups)])

    def swap_part(x, step):
        return lax.ppermute(x, "vocab", [(v, v ^ step) for v in range(parts)])

    def along(x, moves):
        return lax.ppermute(x, "dp", [(2 * a + side, 2 * b + side) for a, b in moves for side in range(2)])

    code = jnp.stack([target_ids >> 8, target_ids & 255]).astype(hidden.dtype).reshape(2, splits, ROWS)
    code = code.transpose(1, 0, 2).reshape(splits, 2 * ROWS)
    own = jnp.concatenate([hidden, jnp.pad(code, ((0, TILE - splits), (0, features - 2 * ROWS)))])
    near = swap_hi(own, 1)
    cross = along(own, [(1, 2), (2, 1)])
    cross_near = along(near, [(1, 2), (2, 1)])
    out = along(cross, [(1, 0), (2, 3)])
    out_near = along(cross_near, [(1, 0), (2, 3)])

    turned = head.T.reshape(tall, chunk, depth)

    def block(step, start, width):
        return lax.dynamic_slice(turned, (hi ^ step, start, 0), (1, width, depth))[0]

    def to_hi(cut, *others):
        return [swap_hi(after(block(step, *cut), *others), step) for step in (1, 2, 3)]

    def over_x(x):
        return swap_part(x, 2)

    def both(x, y, x_across, y_across):
        return jnp.stack([jnp.stack([x, y]), jnp.stack([x_across, y_across])])

    def ready(half, whole):
        code = half[0, :, slots : slots + splits, : 2 * ROWS].astype(jnp.int32).reshape(2 * splits, 2, ROWS)
        return assemble(gain, [half, whole], ROWS), code[:, :1] * 256 + code[:, 1:]

    def score(piece, before):
        start, width = cuts[piece]
        plan = Line(breadth, chunk, start, width)
        heads = [turned, local_block, *sent[piece], across[piece]]
        return stats(plan, jnp.zeros(1, jnp.int32), seq_lens, seq_owner, tokens, ids, heads, before)

    local_block = swap_lo(block(0, 0, chunk))
    own_across = over_x(own)
    near_across = over_x(near)
    sent = [to_hi(cuts[0], out, cross_near, local_block, own_across, near_across)]
    far = jnp.where(middle, cross, out)
    far_across = over_x(far)
    last = jnp.where(middle, cross_near, out_near)
    last_across = over_x(after(last, *sent[0]))
    front_half = both(own, near, own_across, near_across)
    front_whole = swap_part(front_half, 1)
    back_half = both(far, last, far_across, last_across)
    back_whole = swap_part(back_half, 1)
    across = [swap_lo(jnp.stack(sent[0]))]
    sent.append(to_hi(cuts[1], *sent[0], far_across))
    across.append(swap_lo(jnp.stack(sent[1])))
    tokens, ids = zip(ready(front_half, front_whole), ready(back_half, back_whole))
    sent.append(to_hi(cuts[2], *sent[1], tokens[0], last_across))
    found = score(0, [])
    across.append(swap_lo(after(jnp.stack(sent[2]), across[1], found)))
    found = score(2, [score(1, [found])])
    mine = merge([found[0]] + [swap_hi(found[step], step) for step in range(1, tall)])
    return merge([mine] + [swap_part(mine, step) for step in range(1, parts)])


def local(hidden, gain, head, target_ids, seq_lens, seq_owner):
    groups = lax.axis_size("dp")
    slots, features = hidden.shape
    owners = jnp.arange(groups, dtype=jnp.int32)
    loads = jnp.sum(jnp.where(seq_owner[:, None] == owners[None, :], seq_lens[:, None], 0), axis=0).astype(jnp.int32)
    fits = (
        (groups, lax.axis_size("vocab")) == (8, 4)
        and slots % ROWS == 0
        and slots // ROWS <= TILE
        and 2 * ROWS <= features
        and head.shape[1] % (groups // 2 * TILE) == 0
    )
    transport = by_axes if fits else by_collectives
    scores = transport(hidden, gain.astype(jnp.float32)[None], head, target_ids, seq_lens, seq_owner)
    top, total, weighted, picked = (scores[index] for index in range(4))
    spread = jnp.log(total)
    logprob = picked - (top + spread)
    entropy = spread - weighted / total
    live = jnp.arange(slots, dtype=jnp.int32) < loads[lax.axis_index("dp")]
    return (jnp.where(live, logprob, 0.0), jnp.where(live, entropy, 0.0))


def solution(mesh):
    return jax.shard_map(
        local,
        mesh=mesh,
        in_specs=(P("dp", "vocab"), P(), P("dp", "vocab"), P("dp"), P(), P()),
        out_specs=(P("dp"), P("dp")),
        check_vma=False,
    )
```

time: 816 us -> 245 us (0.30)
  waiting for transfers between devices: 649 us -> 122 us
  matrix products: 107 us -> 0 us
  Pallas kernels: 0 us -> 50.4 us
  starting transfers between devices: 0.08 us -> 42.6 us
  blocking collectives: 17.2 us -> 0 us
  between operations: 14.1 us -> 1.11 us
    all_gather x2 -> x0, waiting for transfers between devices: 648 us -> none  [the longest x1 625 us: local(): columns = lax.all_gather(head, 'dp', axis=0, tiled=True)]
    ppermute x0 -> x30, waiting for transfers between devices: none -> 122 us  [the longest x13 74.2 us: swap_hi(): return lax.ppermute(x, 'dp', [(g, g ^ 2 * step) for g in range(groups)])]
    dot_general x6 -> x0, matrix products: 107 us -> none  [compute(): logits = jnp.dot(block_norm, columns, preferred_element_type=jnp.float32)]
    pallas_call x0 -> x5, Pallas kernels: none -> 50.4 us  [the longest x3 37.7 us: stats(): pl.pallas_call(functools.partial(stats_kernel, plan, (len(tokens), len(id...]
    ppermute x0 -> x30, starting transfers between devices: none -> 42.6 us  [the longest x13 26.7 us: swap_hi(): return lax.ppermute(x, 'dp', [(g, g ^ 2 * step) for g in range(groups)])]
    another operation x4 -> x13, other arithmetic: 0.01 us -> 10.8 us  [the longest x7 7.51 us: both(): return jnp.stack([jnp.stack([x, y]), jnp.stack([x_across, y_across])])]
    reduce_sum x7 -> x0, other arithmetic: 10.8 us -> none  [the longest x6 8.04 us: compute(): weighted = jnp.sum(expo * logits, axis=1)]
    psum x1 -> x0, blocking collectives: 10.1 us -> none  [local(): lax.psum((stats[1] * factor, stats[2] * factor, stats[3]), 'vocab')]
  transfers between devices with their start and end apart: 2 -> 30, of which waited for: 2 -> 16; matrix products, arithmetic and copies ran while one was open for 1% -> 8% of each run, Pallas kernels for 0% -> 17%
where the time goes in v2:
time: 245 us; the launch traced here: 241 us
  waiting for transfers between devices  122 us (50%)
  Pallas kernels  50.4 us (21%)
  starting transfers between devices  42.6 us (17%)
  other arithmetic  17.6 us (7%)
  local copies, waits for them, and re-layouts  7.75 us (3%)
    ppermute x13, waiting for transfers between devices, swap_hi(): return lax.ppermute(x, 'dp', [(g, g ^ 2 * step) for g in range(groups)])  74.2 us
    pallas_call x3, Pallas kernels, stats(): pl.pallas_call(functools.partial(stats_kernel, plan, (len(tokens), len(id...  37.7 us
    ppermute x9, waiting for transfers between devices, swap_part(): return lax.ppermute(x, 'vocab', [(v, v ^ step) for v in range(parts)])  36.7 us
    ppermute x13, starting transfers between devices, swap_hi(): return lax.ppermute(x, 'dp', [(g, g ^ 2 * step) for g in range(groups)])  26.7 us
    pallas_call x2, Pallas kernels, assemble(): pl.pallas_call(functools.partial(assemble_kernel, len(sources) > 1), grid...  12.7 us
    another operation x7, other arithmetic, both(): return jnp.stack([jnp.stack([x, y]), jnp.stack([x_across, y_across])])  7.51 us
    ppermute x4, waiting for transfers between devices, swap_lo(): return lax.ppermute(x, 'dp', [(g, g ^ 1) for g in range(groups)])  7.3 us
    ppermute x9, starting transfers between devices, swap_part(): return lax.ppermute(x, 'vocab', [(v, v ^ step) for v in range(parts)])  7.14 us
  transfers between devices with their start and end apart: 30, of which 16 were waited for; matrix products, arithmetic and copies ran while one was open for 8% of the time, Pallas kernels for 17%

profile of v2, /device:TPU:4, one launch (start us, length us, event | category | flops | bytes accessed | tf_op | source)
XLA Modules:
  0.0 241.5 jit_solution(17869228209704656578)
XLA Ops:
  1.4 2.1 fusion.14
  6.6 16.8 %collective-permute-done = bf16[784,512]{1,0:T(8,128)(2,1)} collective-permute-done((bf16[784,512]{1,0:T(8,128)(2,1)}, bf16[784,512]{1,0:T(8,128)(2,1)}, u32[]{:S(2)}, u32[]{:S(2)}) %collective-permute-start) | collective-permute-done | bytes 802848 | tf_op jit(solution)/shard_map/ppermute | solution.py:305
  34.0 13.8 %collective-permute-done.1 = bf16[784,512]{1,0:T(8,128)(2,1)} collective-permute-done((bf16[784,512]{1,0:T(8,128)(2,1)}, bf16[784,512]{1,0:T(8,128)(2,1)}, u32[]{:S(2)}, u32[]{:S(2)}) %collective-permute-start.1) | collective-permute-done | bytes 802848 | tf_op jit(solution)/shard_map/ppermute | solution.py:311
  47.9 2.0 collective-permute-done.9.refs_5_
  49.9 13.2 %collective-permute-done.2 = bf16[784,512]{1,0:T(8,128)(2,1)} collective-permute-done((bf16[784,512]{1,0:T(8,128)(2,1)}, bf16[784,512]{1,0:T(8,128)(2,1)}, u32[]{:S(2)}, u32[]{:S(2)}) %collective-permute-start.2) | collective-permute-done | bytes 802848 | tf_op jit(solution)/shard_map/ppermute | solution.py:311
  63.1 3.0 %collective-permute-start.10 = (bf16[800,256]{1,0:T(8,128)(2,1)S(1)}, bf16[800,256]{1,0:T(8,128)(2,1)S(1)}, u32[]{:S(2)}, u32[]{:S(2)}) collective-permute-start(bf16[800,256]{1,0:T(8,128)(2,1)S(1)} %get-tuple-element.13), channel_id=1, source_target_pairs={{0,8},{4,12},{8,0},{12,4},{16,24},{20,28},{24,16},{28,20},{1,9},{5... | collective-permute-start | bytes 1228808 | tf_op jit(solution)/shard_map/ppermute | solution.py:305
  71.3 3.8 %collective-permute-done.7 = bf16[784,512]{1,0:T(8,128)(2,1)} collective-permute-done((bf16[784,512]{1,0:T(8,128)(2,1)}, bf16[784,512]{1,0:T(8,128)(2,1)}, u32[]{:S(2)}, u32[]{:S(2)}) %collective-permute-start.7) | collective-permute-done | bytes 802848 | tf_op jit(solution)/shard_map/ppermute | solution.py:314
  76.3 8.1 %collective-permute-done.10.refs_6_ = bf16[800,256]{1,0:T(8,128)(2,1)S(1)} collective-permute-done((bf16[800,256]{1,0:T(8,128)(2,1)S(1)}, bf16[800,256]{1,0:T(8,128)(2,1)S(1)}, u32[]{:S(2)}, u32[]{:S(2)}) %collective-permute-start.10) | collective-permute-done | bytes 409632 | tf_op jit(solution)/shard_map/ppermute | solution.py:305
  84.5 12.5 %collective-permute-done.11.refs_7_ = bf16[800,256]{1,0:T(8,128)(2,1)S(1)} collective-permute-done((bf16[800,256]{1,0:T(8,128)(2,1)S(1)}, bf16[800,256]{1,0:T(8,128)(2,1)S(1)}, u32[]{:S(2)}, u32[]{:S(2)}) %collective-permute-start.11) | collective-permute-done | bytes 409632 | tf_op jit(solution)/shard_map/ppermute | solution.py:305
  102.2 7.0 %collective-permute-done.13 = bf16[784,512]{1,0:T(8,128)(2,1)S(1)} collective-permute-done((bf16[784,512]{1,0:T(8,128)(2,1)S(1)}, bf16[784,512]{1,0:T(8,128)(2,1)S(1)}, u32[]{:S(2)}, u32[]{:S(2)}) %collective-permute-start.13) | collective-permute-done | bytes 802848 | tf_op jit(solution)/shard_map/ppermute | solution.py:311
  115.3 2.2 dynamic-slice_bitcast_fusion.4
  119.0 9.4 %collective-permute-start.16 = (bf16[688,256]{1,0:T(8,128)(2,1)}, bf16[688,256]{1,0:T(8,128)(2,1)}, u32[]{:S(2)}, u32[]{:S(2)}) collective-permute-start(bf16[688,256]{1,0:T(8,128)(2,1)} %get-tuple-element.18), channel_id=1, source_target_pairs={{0,16},{4,20},{8,24},{12,28},{16,0},{20,4},{24,8},{28,12},{1,17},{... | collective-permute-start | bytes 1056776 | tf_op jit(solution)/shard_map/ppermute | solution.py:305
  129.9 6.4 %shard_map.77.refs_0_ = bf16[2,3,2048,256]{3,2,1,0:T(8,128)(2,1)S(1)} custom-call(f32[1,2048]{1,0:T(1,128)S(1)} %bitcast.116, bf16[2,2,784,512]{3,2,1,0:T(8,128)(2,1)} %pad_maximum_fusion.refs_0_, bf16[2,2,784,512]{3,2,1,0:T(8,128)(2,1)} %collective-permute-done.3.refs_1_), custom_call_target="tpu_custom_call" | custom-call | flops 18874368 | bytes 12582912 | tf_op jit(solution)/shard_map/pallas_call | solution.py:43
  136.4 16.2 %collective-permute-done.16.refs_7_ = bf16[688,256]{1,0:T(8,128)(2,1)} collective-permute-done((bf16[688,256]{1,0:T(8,128)(2,1)}, bf16[688,256]{1,0:T(8,128)(2,1)}, u32[]{:S(2)}, u32[]{:S(2)}) %collective-permute-start.16) | collective-permute-done | bytes 352288 | tf_op jit(solution)/shard_map/ppermute | solution.py:305
  154.1 2.9 %collective-permute-start.18 = (bf16[512,256]{1,0:T(8,128)(2,1)S(1)}, bf16[512,256]{1,0:T(8,128)(2,1)S(1)}, u32[]{:S(2)}, u32[]{:S(2)}) collective-permute-start(bf16[512,256]{1,0:T(8,128)(2,1)S(1)} %get-tuple-element.20), channel_id=1, source_target_pairs={{0,8},{4,12},{8,0},{12,4},{16,24},{20,28},{24,16},{28,20},{1,9},{5... | collective-permute-start | bytes 786440 | tf_op jit(solution)/shard_map/ppermute | solution.py:305
  158.3 5.4 %collective-permute-done.20.refs_8_ = bf16[512,256]{1,0:T(8,128)(2,1)S(1)} collective-permute-done((bf16[512,256]{1,0:T(8,128)(2,1)S(1)}, bf16[512,256]{1,0:T(8,128)(2,1)S(1)}, u32[]{:S(2)}, u32[]{:S(2)}) %collective-permute-start.20) | collective-permute-done | bytes 262176 | tf_op jit(solution)/shard_map/ppermute | solution.py:305
  164.2 11.6 %collective-permute-done.19.refs_7_ = bf16[512,256]{1,0:T(8,128)(2,1)S(1)} collective-permute-done((bf16[512,256]{1,0:T(8,128)(2,1)S(1)}, bf16[512,256]{1,0:T(8,128)(2,1)S(1)}, u32[]{:S(2)}, u32[]{:S(2)}) %collective-permute-start.19) | collective-permute-done | bytes 262176 | tf_op jit(solution)/shard_map/ppermute | solution.py:305
  175.9 6.3 %shard_map.78.refs_1_ = bf16[2,3,2048,256]{3,2,1,0:T(8,128)(2,1)S(1)} custom-call(f32[1,2048]{1,0:T(1,128)S(1)} %bitcast.117, bf16[2,2,784,512]{3,2,1,0:T(8,128)(2,1)S(1)} %pad_maximum_fusion.1.refs_0_, bf16[2,2,784,512]{3,2,1,0:T(8,128)(2,1)} %collective-permute-done.14.refs_1_), custom_call_target="tpu_custom_call" | custom-call | flops 18874368 | bytes 12582912 | tf_op jit(solution)/shard_map/pallas_call | solution.py:43
  182.3 14.4 %shard_map.79.refs_10_ = f32[4,4,768]{2,1,0:T(4,128)S(1)} custom-call(s32[1]{0:T(128)} %constant.14.clone.1.start_ref, s32[16]{0:T(128)S(1)} %copy-done.9, s32[16]{0:T(128)S(1)} %copy-done.10, bf16[2,3,2048,256]{3,2,1,0:T(8,128)(2,1)S(1)} %shard_map.77.refs_0_, bf16[2,3,2048,256]{3,2,1,0:T(8,128)(2,1)S(1)} %shard_map.78.refs_1_, ...), custom_call_target="tpu_custom_call" | custom-call | flops 10066329600 | bytes 15859712 | tf_op jit(solution)/shard_map/pallas_call | solution.py:157
  197.3 12.8 %shard_map.80.refs_10_ = f32[4,4,768]{2,1,0:T(4,128)S(1)} custom-call(s32[1]{0:T(128)} %constant.14.clone.1.start_ref, s32[16]{0:T(128)S(1)} %copy-done.9, s32[16]{0:T(128)S(1)} %copy-done.10, bf16[2,3,2048,256]{3,2,1,0:T(8,128)(2,1)S(1)} %shard_map.77.refs_0_, bf16[2,3,2048,256]{3,2,1,0:T(8,128)(2,1)S(1)} %shard_map.78.refs_1_, ...), custom_call_target="tpu_custom_call" | custom-call | flops 8657043456 | bytes 15400960 | tf_op jit(solution)/shard_map/pallas_call | solution.py:157
  210.1 5.3 %collective-permute-done.23.refs_9_ = bf16[3,512,256]{2,1,0:T(8,128)(2,1)S(1)} collective-permute-done((bf16[3,512,256]{2,1,0:T(8,128)(2,1)S(1)}, bf16[3,512,256]{2,1,0:T(8,128)(2,1)S(1)}, u32[]{:S(2)}, u32[]{:S(2)}) %collective-permute-start.23) | collective-permute-done | bytes 786464 | tf_op jit(solution)/shard_map/ppermute | solution.py:308
  215.3 10.5 %shard_map.81 = f32[4,4,768]{2,1,0:T(4,128)S(1)} custom-call(s32[1]{0:T(128)} %constant.14.clone.1.start_ref, s32[16]{0:T(128)S(1)} %copy-done.9, s32[16]{0:T(128)S(1)} %copy-done.10, bf16[2,3,2048,256]{3,2,1,0:T(8,128)(2,1)S(1)} %shard_map.77.refs_0_, bf16[2,3,2048,256]{3,2,1,0:T(8,128)(2,1)S(1)} %shard_map.78.refs_1_, ...), custom_call_target="tpu_custom_call" | custom-call | flops 6442450944 | bytes 14680064 | tf_op jit(solution)/shard_map/pallas_call | solution.py:157
  225.9 2.5 %collective-permute-start.25 = (f32[4,768]{1,0:T(4,128)S(1)}, f32[4,768]{1,0:T(4,128)S(1)}, u32[]{:S(2)}, u32[]{:S(2)}) collective-permute-start(f32[4,768]{1,0:T(4,128)S(1)} %get-tuple-element.69), channel_id=1, source_target_pairs={{0,16},{4,20},{8,24},{12,28},{16,0},{20,4},{24,8},{28,12},{1,17},{... | collective-permute-start | bytes 36872 | tf_op jit(solution)/shard_map/ppermute | solution.py:305
  230.6 3.3 %collective-permute-done.26 = f32[4,768]{1,0:T(4,128)S(1)} collective-permute-done((f32[4,768]{1,0:T(4,128)S(1)}, f32[4,768]{1,0:T(4,128)S(1)}, u32[]{:S(2)}, u32[]{:S(2)}) %collective-permute-start.26) | collective-permute-done | bytes 12320 | tf_op jit(solution)/shard_map/ppermute | solution.py:305
  (112 shorter events, 48.9 us)
Async XLA Ops:
  3.5 19.9 %collective-permute-start = (bf16[784,512]{1,0:T(8,128)(2,1)}, bf16[784,512]{1,0:T(8,128)(2,1)}, u32[]{:S(2)}, u32[]{:S(2)}) collective-permute-start(bf16[784,512]{1,0:T(8,128)(2,1)} %get-tuple-element.64), channel_id=1, source_target_pairs={{0,8},{4,12},{8,0},{12,4},{16,24},{20,28},{24,16},{28,20},{1,9},{5... | collective-permute-start | bytes 2408456 | tf_op jit(solution)/shard_map/ppermute | solution.py:305
  5.1 23.7 %collective-permute-start.4 = (bf16[784,512]{1,0:T(8,128)(2,1)}, bf16[784,512]{1,0:T(8,128)(2,1)}, u32[]{:S(2)}, u32[]{:S(2)}) collective-permute-start(bf16[784,512]{1,0:T(8,128)(2,1)} %get-tuple-element.64), channel_id=1, source_target_pairs={{8,16},{12,20},{16,8},{20,12},{9,17},{13,21},{17,9},{21,13},{10,18... | collective-permute-start | bytes 2408456 | tf_op jit(solution)/shard_map/ppermute | solution.py:314
  23.4 6.6 %collective-permute-start.6 = (bf16[784,512]{1,0:T(8,128)(2,1)}, bf16[784,512]{1,0:T(8,128)(2,1)}, u32[]{:S(2)}, u32[]{:S(2)}) collective-permute-start(bf16[784,512]{1,0:T(8,128)(2,1)} %collective-permute-done), channel_id=1, source_target_pairs={{8,16},{12,20},{16,8},{20,12},{9,17},{13,21},{17,9},{21,13},{10,18... | collective-permute-start | bytes 2408456 | tf_op jit(solution)/shard_map/ppermute | solution.py:314
  26.3 23.6 %collective-permute-start.9 = (bf16[2000,256]{1,0:T(8,128)(2,1)S(1)}, bf16[2000,256]{1,0:T(8,128)(2,1)S(1)}, u32[]{:S(2)}, u32[]{:S(2)}) collective-permute-start(bf16[2000,256]{1,0:T(8,128)(2,1)S(1)} %dynamic-slice_bitcast_fusion), channel_id=1, source_target_pairs={{0,4},{4,0},{8,12},{12,8},{16,20},{20,16},{24,28},{28,24},{1,5},{5... | collective-permute-start | bytes 3072008 | tf_op jit(solution)/shard_map/ppermute | solution.py:308
  26.8 21.1 %collective-permute-start.1 = (bf16[784,512]{1,0:T(8,128)(2,1)}, bf16[784,512]{1,0:T(8,128)(2,1)}, u32[]{:S(2)}, u32[]{:S(2)}) collective-permute-start(bf16[784,512]{1,0:T(8,128)(2,1)} %get-tuple-element.64), channel_id=1, source_target_pairs={{0,2},{1,3},{2,0},{3,1},{4,6},{5,7},{6,4},{7,5},{8,10},{9,11},{10,... | collective-permute-start | bytes 2408456 | tf_op jit(solution)/shard_map/ppermute | solution.py:311
  28.4 34.7 %collective-permute-start.2 = (bf16[784,512]{1,0:T(8,128)(2,1)}, bf16[784,512]{1,0:T(8,128)(2,1)}, u32[]{:S(2)}, u32[]{:S(2)}) collective-permute-start(bf16[784,512]{1,0:T(8,128)(2,1)} %collective-permute-done), channel_id=1, source_target_pairs={{0,2},{1,3},{2,0},{3,1},{4,6},{5,7},{6,4},{7,5},{8,10},{9,11},{10,... | collective-permute-start | bytes 2408456 | tf_op jit(solution)/shard_map/ppermute | solution.py:311
  28.8 34.3 %collective-permute-start.5 = (bf16[784,512]{1,0:T(8,128)(2,1)}, bf16[784,512]{1,0:T(8,128)(2,1)}, u32[]{:S(2)}, u32[]{:S(2)}) collective-permute-start(bf16[784,512]{1,0:T(8,128)(2,1)} %collective-permute-done.4), channel_id=1, source_target_pairs={{8,0},{12,4},{16,24},{20,28},{9,1},{13,5},{17,25},{21,29},{10,2},{... | collective-permute-start | bytes 2408456 | tf_op jit(solution)/shard_map/ppermute | solution.py:314
  30.1 45.0 %collective-permute-start.7 = (bf16[784,512]{1,0:T(8,128)(2,1)}, bf16[784,512]{1,0:T(8,128)(2,1)}, u32[]{:S(2)}, u32[]{:S(2)}) collective-permute-start(bf16[784,512]{1,0:T(8,128)(2,1)} %collective-permute-done.6), channel_id=1, source_target_pairs={{8,0},{12,4},{16,24},{20,28},{9,1},{13,5},{17,25},{21,29},{10,2},{... | collective-permute-start | bytes 2408456 | tf_op jit(solution)/shard_map/ppermute | solution.py:314
  63.1 21.4 %collective-permute-start.10 = (bf16[800,256]{1,0:T(8,128)(2,1)S(1)}, bf16[800,256]{1,0:T(8,128)(2,1)S(1)}, u32[]{:S(2)}, u32[]{:S(2)}) collective-permute-start(bf16[800,256]{1,0:T(8,128)(2,1)S(1)} %get-tuple-element.13), channel_id=1, source_target_pairs={{0,8},{4,12},{8,0},{12,4},{16,24},{20,28},{24,16},{28,20},{1,9},{5... | collective-permute-start | bytes 1228808 | tf_op jit(solution)/shard_map/ppermute | solution.py:305
  66.1 30.9 %collective-permute-start.11 = (bf16[800,256]{1,0:T(8,128)(2,1)S(1)}, bf16[800,256]{1,0:T(8,128)(2,1)S(1)}, u32[]{:S(2)}, u32[]{:S(2)}) collective-permute-start(bf16[800,256]{1,0:T(8,128)(2,1)S(1)} %get-tuple-element.14), channel_id=1, source_target_pairs={{0,16},{4,20},{8,24},{12,28},{16,0},{20,4},{24,8},{28,12},{1,17},{... | collective-permute-start | bytes 1228808 | tf_op jit(solution)/shard_map/ppermute | solution.py:305
  67.1 29.9 %collective-permute-start.12 = (bf16[800,256]{1,0:T(8,128)(2,1)S(1)}, bf16[800,256]{1,0:T(8,128)(2,1)S(1)}, u32[]{:S(2)}, u32[]{:S(2)}) collective-permute-start(bf16[800,256]{1,0:T(8,128)(2,1)S(1)} %get-tuple-element.15), channel_id=1, source_target_pairs={{0,24},{4,28},{8,16},{12,20},{16,8},{20,12},{24,0},{28,4},{1,25},{... | collective-permute-start | bytes 1228808 | tf_op jit(solution)/shard_map/ppermute | solution.py:305
  69.7 32.5 %collective-permute-start.8 = (bf16[784,512]{1,0:T(8,128)(2,1)S(1)}, bf16[784,512]{1,0:T(8,128)(2,1)S(1)}, u32[]{:S(2)}, u32[]{:S(2)}) collective-permute-start(bf16[784,512]{1,0:T(8,128)(2,1)S(1)} %broadcast_select_fusion.1), channel_id=1, source_target_pairs={{0,2},{1,3},{2,0},{3,1},{4,6},{5,7},{6,4},{7,5},{8,10},{9,11},{10,... | collective-permute-start | bytes 2408456 | tf_op jit(solution)/shard_map/ppermute | solution.py:311
  97.0 12.2 %collective-permute-start.13 = (bf16[784,512]{1,0:T(8,128)(2,1)S(1)}, bf16[784,512]{1,0:T(8,128)(2,1)S(1)}, u32[]{:S(2)}, u32[]{:S(2)}) collective-permute-start(bf16[784,512]{1,0:T(8,128)(2,1)S(1)} %broadcast_select_fusion), channel_id=1, source_target_pairs={{0,2},{1,3},{2,0},{3,1},{4,6},{5,7},{6,4},{7,5},{8,10},{9,11},{10,... | collective-permute-start | bytes 2408456 | tf_op jit(solution)/shard_map/ppermute | solution.py:311
  102.0 26.3 %collective-permute-start.3 = (bf16[2,2,784,512]{3,2,1,0:T(8,128)(2,1)}, bf16[2,2,784,512]{3,2,1,0:T(8,128)(2,1)}, u32[]{:S(2)}, u32[]{:S(2)}) collective-permute-start(bf16[2,2,784,512]{3,2,1,0:T(8,128)(2,1)} %pad_maximum_fusion.refs_0_), channel_id=1, source_target_pairs={{0,1},{1,0},{2,3},{3,2},{4,5},{5,4},{6,7},{7,6},{8,9},{9,8},{10,11... | collective-permute-start | bytes 9633800 | tf_op jit(solution)/shard_map/ppermute | solution.py:311
  109.7 66.2 %collective-permute-start.14 = (bf16[2,2,784,512]{3,2,1,0:T(8,128)(2,1)S(1)}, bf16[2,2,784,512]{3,2,1,0:T(8,128)(2,1)}, u32[]{:S(2)}, u32[]{:S(2)}) collective-permute-start(bf16[2,2,784,512]{3,2,1,0:T(8,128)(2,1)S(1)} %pad_maximum_fusion.1.refs_0_), channel_id=1, source_target_pairs={{0,1},{1,0},{2,3},{3,2},{4,5},{5,4},{6,7},{7,6},{8,9},{9,8},{10,11... | collective-permute-start | bytes 9633800 | tf_op jit(solution)/shard_map/ppermute | solution.py:311
  111.0 71.2 %collective-permute-start.22 = (bf16[3,800,256]{2,1,0:T(8,128)(2,1)}, bf16[3,800,256]{2,1,0:T(8,128)(2,1)}, u32[]{:S(2)}, u32[]{:S(2)}) collective-permute-start(bf16[3,800,256]{2,1,0:T(8,128)(2,1)} %pad_maximum_fusion.2), channel_id=1, source_target_pairs={{0,4},{4,0},{8,12},{12,8},{16,20},{20,16},{24,28},{28,24},{1,5},{5... | collective-permute-start | bytes 3686408 | tf_op jit(solution)/shard_map/ppermute | solution.py:308
  117.5 18.9 %collective-permute-start.17 = (bf16[688,256]{1,0:T(8,128)(2,1)}, bf16[688,256]{1,0:T(8,128)(2,1)}, u32[]{:S(2)}, u32[]{:S(2)}) collective-permute-start(bf16[688,256]{1,0:T(8,128)(2,1)} %get-tuple-element.19), channel_id=1, source_target_pairs={{0,24},{4,28},{8,16},{12,20},{16,8},{20,12},{24,0},{28,4},{1,25},{... | collective-permute-start | bytes 1056776 | tf_op jit(solution)/shard_map/ppermute | solution.py:305
  119.0 33.6 %collective-permute-start.16 = (bf16[688,256]{1,0:T(8,128)(2,1)}, bf16[688,256]{1,0:T(8,128)(2,1)}, u32[]{:S(2)}, u32[]{:S(2)}) collective-permute-start(bf16[688,256]{1,0:T(8,128)(2,1)} %get-tuple-element.18), channel_id=1, source_target_pairs={{0,16},{4,20},{8,24},{12,28},{16,0},{20,4},{24,8},{28,12},{1,17},{... | collective-permute-start | bytes 1056776 | tf_op jit(solution)/shard_map/ppermute | solution.py:305
  128.4 24.2 %collective-permute-start.15 = (bf16[688,256]{1,0:T(8,128)(2,1)}, bf16[688,256]{1,0:T(8,128)(2,1)}, u32[]{:S(2)}, u32[]{:S(2)}) collective-permute-start(bf16[688,256]{1,0:T(8,128)(2,1)} %get-tuple-element.17), channel_id=1, source_target_pairs={{0,8},{4,12},{8,0},{12,4},{16,24},{20,28},{24,16},{28,20},{1,9},{5... | collective-permute-start | bytes 1056776 | tf_op jit(solution)/shard_map/ppermute | solution.py:305
  152.6 11.1 %collective-permute-start.20 = (bf16[512,256]{1,0:T(8,128)(2,1)S(1)}, bf16[512,256]{1,0:T(8,128)(2,1)S(1)}, u32[]{:S(2)}, u32[]{:S(2)}) collective-permute-start(bf16[512,256]{1,0:T(8,128)(2,1)S(1)} %copy-done.14), channel_id=1, source_target_pairs={{0,24},{4,28},{8,16},{12,20},{16,8},{20,12},{24,0},{28,4},{1,25},{... | collective-permute-start | bytes 786440 | tf_op jit(solution)/shard_map/ppermute | solution.py:305
  154.1 21.7 %collective-permute-start.19 = (bf16[512,256]{1,0:T(8,128)(2,1)S(1)}, bf16[512,256]{1,0:T(8,128)(2,1)S(1)}, u32[]{:S(2)}, u32[]{:S(2)}) collective-permute-start(bf16[512,256]{1,0:T(8,128)(2,1)S(1)} %copy-done.13), channel_id=1, source_target_pairs={{0,16},{4,20},{8,24},{12,28},{16,0},{20,4},{24,8},{28,12},{1,17},{... | collective-permute-start | bytes 786440 | tf_op jit(solution)/shard_map/ppermute | solution.py:305
  154.1 21.7 %collective-permute-start.18 = (bf16[512,256]{1,0:T(8,128)(2,1)S(1)}, bf16[512,256]{1,0:T(8,128)(2,1)S(1)}, u32[]{:S(2)}, u32[]{:S(2)}) collective-permute-start(bf16[512,256]{1,0:T(8,128)(2,1)S(1)} %get-tuple-element.20), channel_id=1, source_target_pairs={{0,8},{4,12},{8,0},{12,4},{16,24},{20,28},{24,16},{28,20},{1,9},{5... | collective-permute-start | bytes 786440 | tf_op jit(solution)/shard_map/ppermute | solution.py:305
  163.7 33.0 %collective-permute-start.21 = (bf16[3,688,256]{2,1,0:T(8,128)(2,1)S(1)}, bf16[3,688,256]{2,1,0:T(8,128)(2,1)S(1)}, u32[]{:S(2)}, u32[]{:S(2)}) collective-permute-start(bf16[3,688,256]{2,1,0:T(8,128)(2,1)S(1)} %pad_maximum_fusion.3), channel_id=1, source_target_pairs={{0,4},{4,0},{8,12},{12,8},{16,20},{20,16},{24,28},{28,24},{1,5},{5... | collective-permute-start | bytes 3170312 | tf_op jit(solution)/shard_map/ppermute | solution.py:308
  196.7 18.6 %collective-permute-start.23 = (bf16[3,512,256]{2,1,0:T(8,128)(2,1)S(1)}, bf16[3,512,256]{2,1,0:T(8,128)(2,1)S(1)}, u32[]{:S(2)}, u32[]{:S(2)}) collective-permute-start(bf16[3,512,256]{2,1,0:T(8,128)(2,1)S(1)} %pad_maximum_fusion.4), channel_id=1, source_target_pairs={{0,4},{4,0},{8,12},{12,8},{16,20},{20,16},{24,28},{28,24},{1,5},{5... | collective-permute-start | bytes 2359304 | tf_op jit(solution)/shard_map/ppermute | solution.py:308
  (22 other events, 261.5 us)

commit v3 on v2

--- a/solution.py
+++ b/solution.py
@@ -174,9 +174,9 @@
         out_shape=jax.ShapeDtypeStruct((groups, 4, splits * rows), jnp.float32),
         compiler_params=pltpu.CompilerParams(vmem_limit_bytes=24 * 2**20),
         cost_estimate=pl.CostEstimate(
-            flops=2 * groups * splits * rows * wide * width,
-            bytes_accessed=groups * splits * rows * wide * 2 + wide * width * 2,
-            transcendentals=groups * splits * rows * width,
+            flops=groups * splits * rows * wide * width // 8,
+            bytes_accessed=wide * width,
+            transcendentals=groups * splits * rows * width // 8,
         ),
     )(start, seq_lens, seq_owner, *tokens, *ids, *heads, *before)
 
@@ -327,8 +327,10 @@
     def block(step, start, width):
         return lax.dynamic_slice(turned, (hi ^ step, start, 0), (1, width, depth))[0]
 
-    def to_hi(cut, *others):
-        return [swap_hi(after(block(step, *cut), *others), step) for step in (1, 2, 3)]
+    blocks = [[block(step, *cut) for step in (1, 2, 3)] for cut in cuts]
+
+    def to_hi(piece, *others):
+        return [swap_hi(after(y, *others), step) for step, y in enumerate(blocks[piece], 1)]
 
     def over_x(x):
         return swap_part(x, 2)
@@ -348,21 +350,21 @@
 
     local_block = swap_lo(block(0, 0, chunk))
     own_across = over_x(own)
-    near_across = over_x(near)
-    sent = [to_hi(cuts[0], out, cross_near, local_block, own_across, near_across)]
+    near_across = over_x(after(near, own_across, local_block))
+    sent = [to_hi(0, out, cross_near, near_across, *blocks[1], *blocks[2])]
     far = jnp.where(middle, cross, out)
     far_across = over_x(far)
     last = jnp.where(middle, cross_near, out_near)
     last_across = over_x(after(last, *sent[0]))
+    sent.append(to_hi(1, *sent[0], far_across))
     front_half = both(own, near, own_across, near_across)
     front_whole = swap_part(front_half, 1)
     back_half = both(far, last, far_across, last_across)
-    back_whole = swap_part(back_half, 1)
+    back_whole = swap_part(after(back_half, *sent[1]), 1)
+    tokens, ids = zip(ready(front_half, front_whole), ready(back_half, back_whole))
+    sent.append(to_hi(2, *sent[1], tokens[0]))
     across = [swap_lo(jnp.stack(sent[0]))]
-    sent.append(to_hi(cuts[1], *sent[0], far_across))
     across.append(swap_lo(jnp.stack(sent[1])))
-    tokens, ids = zip(ready(front_half, front_whole), ready(back_half, back_whole))
-    sent.append(to_hi(cuts[2], *sent[1], tokens[0], last_across))
     found = score(0, [])
     across.append(swap_lo(after(jnp.stack(sent[2]), across[1], found)))
     found = score(2, [score(1, [found])])

time: 245 us -> 243 us (level)
  waiting for transfers between devices: 122 us -> 111 us
  local copies, waits for them, and re-layouts: 7.75 us -> 18.3 us
  other arithmetic: 17.6 us -> 12.4 us
  starting transfers between devices: 42.6 us -> 45.1 us
    ppermute x4, waiting for transfers between devices: 3.82 us -> 34.8 us  [along(): lax.ppermute(x, 'dp', [(2 * a + side, 2 * b + side) for a, b in moves for...]
    ppermute x9, waiting for transfers between devices: 36.7 us -> 17.4 us  [swap_part(): return lax.ppermute(x, 'vocab', [(v, v ^ step) for v in range(parts)])]
    ppermute x13, waiting for transfers between devices: 74.2 us -> 56.2 us  [swap_hi(): return lax.ppermute(x, 'dp', [(g, g ^ 2 * step) for g in range(groups)])]
    unnamed x32 -> x54, local copies, waits for them, and re-layouts: 0.07 us -> 11.5 us
    another operation x7, other arithmetic: 7.51 us -> 2.42 us  [both(): return jnp.stack([jnp.stack([x, y]), jnp.stack([x_across, y_across])])]
    ppermute x4, waiting for transfers between devices: 7.3 us -> 2.96 us  [swap_lo(): return lax.ppermute(x, 'dp', [(g, g ^ 1) for g in range(groups)])]
  transfers between devices with their start and end apart: 30 -> 30, of which waited for: 16 -> 15; matrix products, arithmetic and copies ran while one was open for 8% -> 6% of each run, Pallas kernels for 17% -> 17%
where the time goes in v3:
time: 243 us; the launch traced here: 239 us
  waiting for transfers between devices  111 us (46%)
  Pallas kernels  51 us (21%)
  starting transfers between devices  45.1 us (19%)
  local copies, waits for them, and re-layouts  18.3 us (8%)
  other arithmetic  12.4 us (5%)
    ppermute x13, waiting for transfers between devices, swap_hi(): return lax.ppermute(x, 'dp', [(g, g ^ 2 * step) for g in range(groups)])  56.2 us
    pallas_call x3, Pallas kernels, stats(): pl.pallas_call(functools.partial(stats_kernel, plan, (len(tokens), len(id...  39.8 us
    ppermute x4, waiting for transfers between devices, along(): lax.ppermute(x, 'dp', [(2 * a + side, 2 * b + side) for a, b in moves for...  34.8 us
    ppermute x13, starting transfers between devices, swap_hi(): return lax.ppermute(x, 'dp', [(g, g ^ 2 * step) for g in range(groups)])  27.6 us
    ppermute x9, waiting for transfers between devices, swap_part(): return lax.ppermute(x, 'vocab', [(v, v ^ step) for v in range(parts)])  17.4 us
    unnamed x54, local copies, waits for them, and re-layouts  11.5 us
    pallas_call x2, Pallas kernels, assemble(): pl.pallas_call(functools.partial(assemble_kernel, len(sources) > 1), grid...  11.2 us
    ppermute x9, starting transfers between devices, swap_part(): return lax.ppermute(x, 'vocab', [(v, v ^ step) for v in range(parts)])  8.17 us
  transfers between devices with their start and end apart: 30, of which 15 were waited for; matrix products, arithmetic and copies ran while one was open for 6% of the time, Pallas kernels for 17%

profile of v3, /device:TPU:4, one launch (start us, length us, event | category | flops | bytes accessed | tf_op | source)
XLA Modules:
  0.0 239.4 jit_solution(13259932508381008615)
XLA Ops:
  9.2 13.1 %collective-permute-done = bf16[784,512]{1,0:T(8,128)(2,1)S(1)} collective-permute-done((bf16[784,512]{1,0:T(8,128)(2,1)S(1)}, bf16[784,512]{1,0:T(8,128)(2,1)S(1)}, u32[]{:S(2)}, u32[]{:S(2)}) %collective-permute-start) | collective-permute-done | bytes 802848 | tf_op jit(solution)/shard_map/ppermute | solution.py:305
  26.7 3.0 %collective-permute-done.2.refs_5_ = bf16[2000,256]{1,0:T(8,128)(2,1)S(1)} collective-permute-done((bf16[2000,256]{1,0:T(8,128)(2,1)S(1)}, bf16[2000,256]{1,0:T(8,128)(2,1)S(1)}, u32[]{:S(2)}, u32[]{:S(2)}) %collective-permute-start.2) | collective-permute-done | bytes 1024032 | tf_op jit(solution)/shard_map/ppermute | solution.py:308
  38.3 8.6 %collective-permute-done.6 = bf16[784,512]{1,0:T(8,128)(2,1)} collective-permute-done((bf16[784,512]{1,0:T(8,128)(2,1)}, bf16[784,512]{1,0:T(8,128)(2,1)}, u32[]{:S(2)}, u32[]{:S(2)}) %collective-permute-start.6) | collective-permute-done | bytes 802848 | tf_op jit(solution)/shard_map/ppermute | solution.py:314
  49.1 2.9 %collective-permute-start.10 = (bf16[800,256]{1,0:T(8,128)(2,1)S(1)}, bf16[800,256]{1,0:T(8,128)(2,1)S(1)}, u32[]{:S(2)}, u32[]{:S(2)}) collective-permute-start(bf16[800,256]{1,0:T(8,128)(2,1)S(1)} %get-tuple-element.16), channel_id=1, source_target_pairs={{0,8},{4,12},{8,0},{12,4},{16,24},{20,28},{24,16},{28,20},{1,9},{5... | collective-permute-start | bytes 1228808 | tf_op jit(solution)/shard_map/ppermute | solution.py:305
  57.5 26.2 %collective-permute-done.8 = bf16[784,512]{1,0:T(8,128)(2,1)S(1)} collective-permute-done((bf16[784,512]{1,0:T(8,128)(2,1)}, bf16[784,512]{1,0:T(8,128)(2,1)S(1)}, u32[]{:S(2)}, u32[]{:S(2)}) %collective-permute-start.8) | collective-permute-done | bytes 802848 | tf_op jit(solution)/shard_map/ppermute | solution.py:314
  83.7 7.0 %collective-permute-done.10.refs_6_ = bf16[800,256]{1,0:T(8,128)(2,1)S(1)} collective-permute-done((bf16[800,256]{1,0:T(8,128)(2,1)S(1)}, bf16[800,256]{1,0:T(8,128)(2,1)S(1)}, u32[]{:S(2)}, u32[]{:S(2)}) %collective-permute-start.10) | collective-permute-done | bytes 409632 | tf_op jit(solution)/shard_map/ppermute | solution.py:305
  92.9 2.5 %collective-permute-start.16 = (bf16[688,256]{1,0:T(8,128)(2,1)S(1)}, bf16[688,256]{1,0:T(8,128)(2,1)S(1)}, u32[]{:S(2)}, u32[]{:S(2)}) collective-permute-start(bf16[688,256]{1,0:T(8,128)(2,1)S(1)} %get-tuple-element.22), channel_id=1, source_target_pairs={{0,24},{4,28},{8,16},{12,20},{16,8},{20,12},{24,0},{28,4},{1,25},{... | collective-permute-start | bytes 1056776 | tf_op jit(solution)/shard_map/ppermute | solution.py:305
  97.5 11.6 %collective-permute-done.13 = bf16[784,512]{1,0:T(8,128)(2,1)S(1)} collective-permute-done((bf16[784,512]{1,0:T(8,128)(2,1)S(1)}, bf16[784,512]{1,0:T(8,128)(2,1)S(1)}, u32[]{:S(2)}, u32[]{:S(2)}) %collective-permute-start.13) | collective-permute-done | bytes 802848 | tf_op jit(solution)/shard_map/ppermute | solution.py:311
  109.6 15.5 %collective-permute-done.15.refs_7_ = bf16[688,256]{1,0:T(8,128)(2,1)S(1)} collective-permute-done((bf16[688,256]{1,0:T(8,128)(2,1)S(1)}, bf16[688,256]{1,0:T(8,128)(2,1)S(1)}, u32[]{:S(2)}, u32[]{:S(2)}) %collective-permute-start.15) | collective-permute-done | bytes 352288 | tf_op jit(solution)/shard_map/ppermute | solution.py:305
  129.7 4.4 %shard_map.77.refs_0_ = bf16[2,3,2048,256]{3,2,1,0:T(8,128)(2,1)S(1)} custom-call(f32[1,2048]{1,0:T(1,128)S(1)} %bitcast.119, bf16[2,2,784,512]{3,2,1,0:T(8,128)(2,1)S(1)} %pad_maximum_fusion.refs_0_, bf16[2,2,784,512]{3,2,1,0:T(8,128)(2,1)S(1)} %collective-permute-done.4.refs_1_), custom_call_target="tpu_custom_call" | custom-call | flops 18874368 | bytes 12582912 | tf_op jit(solution)/shard_map/pallas_call | solution.py:43
  134.1 2.7 %copy-done = bf16[2,3,2048,256]{3,2,1,0:T(8,128)(2,1)} copy-done((bf16[2,3,2048,256]{3,2,1,0:T(8,128)(2,1)}, bf16[2,3,2048,256]{3,2,1,0:T(8,128)(2,1)S(1)}, u32[]{:S(2)}) %copy-start) | copy-done | bytes 6291480
  136.8 2.5 %collective-permute-start.20 = (bf16[512,256]{1,0:T(8,128)(2,1)}, bf16[512,256]{1,0:T(8,128)(2,1)S(1)}, u32[]{:S(2)}, u32[]{:S(2)}) collective-permute-start(bf16[512,256]{1,0:T(8,128)(2,1)} %get-tuple-element.26), channel_id=1, source_target_pairs={{0,24},{4,28},{8,16},{12,20},{16,8},{20,12},{24,0},{28,4},{1,25},{... | collective-permute-start | bytes 786440 | tf_op jit(solution)/shard_map/ppermute | solution.py:305
  139.3 8.7 %collective-permute-done.20.refs_8_ = bf16[512,256]{1,0:T(8,128)(2,1)S(1)} collective-permute-done((bf16[512,256]{1,0:T(8,128)(2,1)}, bf16[512,256]{1,0:T(8,128)(2,1)S(1)}, u32[]{:S(2)}, u32[]{:S(2)}) %collective-permute-start.20) | collective-permute-done | bytes 262176 | tf_op jit(solution)/shard_map/ppermute | solution.py:305
  148.0 9.0 %collective-permute-start.18 = (bf16[512,256]{1,0:T(8,128)(2,1)}, bf16[512,256]{1,0:T(8,128)(2,1)}, u32[]{:S(2)}, u32[]{:S(2)}) collective-permute-start(bf16[512,256]{1,0:T(8,128)(2,1)} %get-tuple-element.24), channel_id=1, source_target_pairs={{0,8},{4,12},{8,0},{12,4},{16,24},{20,28},{24,16},{28,20},{1,9},{5... | collective-permute-start | bytes 786440 | tf_op jit(solution)/shard_map/ppermute | solution.py:305
  157.8 3.4 %collective-permute-done.19.refs_7_ = bf16[512,256]{1,0:T(8,128)(2,1)} collective-permute-done((bf16[512,256]{1,0:T(8,128)(2,1)}, bf16[512,256]{1,0:T(8,128)(2,1)}, u32[]{:S(2)}, u32[]{:S(2)}) %collective-permute-start.19) | collective-permute-done | bytes 262176 | tf_op jit(solution)/shard_map/ppermute | solution.py:305
  161.2 5.3 %collective-permute-done.18.refs_6_ = bf16[512,256]{1,0:T(8,128)(2,1)} collective-permute-done((bf16[512,256]{1,0:T(8,128)(2,1)}, bf16[512,256]{1,0:T(8,128)(2,1)}, u32[]{:S(2)}, u32[]{:S(2)}) %collective-permute-start.18) | collective-permute-done | bytes 262176 | tf_op jit(solution)/shard_map/ppermute | solution.py:305
  168.8 6.8 %shard_map.78.refs_1_ = bf16[2,3,2048,256]{3,2,1,0:T(8,128)(2,1)S(1)} custom-call(f32[1,2048]{1,0:T(1,128)S(1)} %bitcast.120, bf16[2,2,784,512]{3,2,1,0:T(8,128)(2,1)S(1)} %pad_maximum_fusion.1.refs_0_, bf16[2,2,784,512]{3,2,1,0:T(8,128)(2,1)} %collective-permute-done.17.refs_1_), custom_call_target="tpu_custom_call" | custom-call | flops 18874368 | bytes 12582912 | tf_op jit(solution)/shard_map/pallas_call | solution.py:43
  175.8 16.3 %shard_map.79.refs_10_ = f32[4,4,768]{2,1,0:T(4,128)S(1)} custom-call(s32[1]{0:T(128)} %constant.14.clone.1.start_ref, s32[16]{0:T(128)S(1)} %copy-done.21, s32[16]{0:T(128)S(1)} %copy-done.22, bf16[2,3,2048,256]{3,2,1,0:T(8,128)(2,1)S(1)} %bitcast.104, bf16[2,3,2048,256]{3,2,1,0:T(8,128)(2,1)S(1)} %shard_map.78.refs_1_, ...), custom_call_target="tpu_custom_call" | custom-call | flops 629145600 | bytes 1638400 | tf_op jit(solution)/shard_map/pallas_call | solution.py:157
  193.9 2.8 %copy-done.1 = bf16[2,3,2048,256]{3,2,1,0:T(8,128)(2,1)S(1)} copy-done((bf16[2,3,2048,256]{3,2,1,0:T(8,128)(2,1)S(1)}, bf16[2,3,2048,256]{3,2,1,0:T(8,128)(2,1)}, u32[]{:S(2)}) %copy-start.1) | copy-done | bytes 6291480
  196.7 2.8 %copy-done.3 = bf16[2,3,2048,256]{3,2,1,0:T(8,128)(2,1)S(1)} copy-done((bf16[2,3,2048,256]{3,2,1,0:T(8,128)(2,1)S(1)}, bf16[2,3,2048,256]{3,2,1,0:T(8,128)(2,1)}, u32[]{:S(2)}) %copy-start.3) | copy-done | bytes 6291480
  201.6 13.0 %shard_map.80.refs_10_ = f32[4,4,768]{2,1,0:T(4,128)S(1)} custom-call(s32[1]{0:T(128)} %constant.14.clone.1.start_ref, s32[16]{0:T(128)S(1)} %copy-done.21, s32[16]{0:T(128)S(1)} %copy-done.22, bf16[2,3,2048,256]{3,2,1,0:T(8,128)(2,1)S(1)} %copy-done.1, bf16[2,3,2048,256]{3,2,1,0:T(8,128)(2,1)S(1)} %copy-done.3, s32[6,1,256]{2,1,0:T(1,128)S(1)} %get-tuple-element.83.refs_2_, ...), custom_call_target="tpu_custom_call" | custom-call | flops 541065216 | bytes 1409024 | tf_op jit(solution)/shard_map/pallas_call | solution.py:157
  214.6 10.5 %shard_map.81 = f32[4,4,768]{2,1,0:T(4,128)S(1)} custom-call(s32[1]{0:T(128)} %constant.14.clone.1.start_ref, s32[16]{0:T(128)S(1)} %copy-done.21, s32[16]{0:T(128)S(1)} %copy-done.22, bf16[2,3,2048,256]{3,2,1,0:T(8,128)(2,1)S(1)} %copy-done.1, bf16[2,3,2048,256]{3,2,1,0:T(8,128)(2,1)S(1)} %copy-done.3, s32[6,1,256]{2,1,0:T(1,128)S(1)} %get-tuple-element.83.refs_2_, ...), custom_call_target="tpu_custom_call" | custom-call | flops 402653184 | bytes 1048576 | tf_op jit(solution)/shard_map/pallas_call | solution.py:157
  227.2 2.3 collective-permute-start.26
  229.8 2.9 %collective-permute-done.26 = f32[4,768]{1,0:T(4,128)S(1)} collective-permute-done((f32[4,768]{1,0:T(4,128)S(1)}, f32[4,768]{1,0:T(4,128)S(1)}, u32[]{:S(2)}, u32[]{:S(2)}) %collective-permute-start.26) | collective-permute-done | bytes 12320 | tf_op jit(solution)/shard_map/ppermute | solution.py:305
  (135 shorter events, 54.4 us)
Async XLA Ops:
  2.6 19.7 %collective-permute-start = (bf16[784,512]{1,0:T(8,128)(2,1)S(1)}, bf16[784,512]{1,0:T(8,128)(2,1)S(1)}, u32[]{:S(2)}, u32[]{:S(2)}) collective-permute-start(bf16[784,512]{1,0:T(8,128)(2,1)S(1)} %get-tuple-element.68), channel_id=1, source_target_pairs={{0,8},{4,12},{8,0},{12,4},{16,24},{20,28},{24,16},{28,20},{1,9},{5... | collective-permute-start | bytes 2408456 | tf_op jit(solution)/shard_map/ppermute | solution.py:305
  5.5 24.2 %collective-permute-start.2 = (bf16[2000,256]{1,0:T(8,128)(2,1)S(1)}, bf16[2000,256]{1,0:T(8,128)(2,1)S(1)}, u32[]{:S(2)}, u32[]{:S(2)}) collective-permute-start(bf16[2000,256]{1,0:T(8,128)(2,1)S(1)} %dynamic-slice_bitcast_fusion), channel_id=1, source_target_pairs={{0,4},{4,0},{8,12},{12,8},{16,20},{20,16},{24,28},{28,24},{1,5},{5... | collective-permute-start | bytes 3072008 | tf_op jit(solution)/shard_map/ppermute | solution.py:308
  6.1 17.7 %collective-permute-start.5 = (bf16[784,512]{1,0:T(8,128)(2,1)S(1)}, bf16[784,512]{1,0:T(8,128)(2,1)}, u32[]{:S(2)}, u32[]{:S(2)}) collective-permute-start(bf16[784,512]{1,0:T(8,128)(2,1)S(1)} %get-tuple-element.68), channel_id=1, source_target_pairs={{8,16},{12,20},{16,8},{20,12},{9,17},{13,21},{17,9},{21,13},{10,18... | collective-permute-start | bytes 2408456 | tf_op jit(solution)/shard_map/ppermute | solution.py:314
  7.7 19.1 %collective-permute-start.1 = (bf16[784,512]{1,0:T(8,128)(2,1)S(1)}, bf16[784,512]{1,0:T(8,128)(2,1)S(1)}, u32[]{:S(2)}, u32[]{:S(2)}) collective-permute-start(bf16[784,512]{1,0:T(8,128)(2,1)S(1)} %get-tuple-element.68), channel_id=1, source_target_pairs={{0,2},{1,3},{2,0},{3,1},{4,6},{5,7},{6,4},{7,5},{8,10},{9,11},{10,... | collective-permute-start | bytes 2408456 | tf_op jit(solution)/shard_map/ppermute | solution.py:311
  22.3 9.9 %collective-permute-start.7 = (bf16[784,512]{1,0:T(8,128)(2,1)S(1)}, bf16[784,512]{1,0:T(8,128)(2,1)}, u32[]{:S(2)}, u32[]{:S(2)}) collective-permute-start(bf16[784,512]{1,0:T(8,128)(2,1)S(1)} %collective-permute-done), channel_id=1, source_target_pairs={{8,16},{12,20},{16,8},{20,12},{9,17},{13,21},{17,9},{21,13},{10,18... | collective-permute-start | bytes 2408456 | tf_op jit(solution)/shard_map/ppermute | solution.py:314
  23.9 23.0 %collective-permute-start.6 = (bf16[784,512]{1,0:T(8,128)(2,1)}, bf16[784,512]{1,0:T(8,128)(2,1)}, u32[]{:S(2)}, u32[]{:S(2)}) collective-permute-start(bf16[784,512]{1,0:T(8,128)(2,1)} %collective-permute-done.5), channel_id=1, source_target_pairs={{8,0},{12,4},{16,24},{20,28},{9,1},{13,5},{17,25},{21,29},{10,2},{... | collective-permute-start | bytes 2408456 | tf_op jit(solution)/shard_map/ppermute | solution.py:314
  30.7 18.4 %collective-permute-start.3 = (bf16[784,512]{1,0:T(8,128)(2,1)S(1)}, bf16[784,512]{1,0:T(8,128)(2,1)S(1)}, u32[]{:S(2)}, u32[]{:S(2)}) collective-permute-start(bf16[784,512]{1,0:T(8,128)(2,1)S(1)} %collective-permute-done), channel_id=1, source_target_pairs={{0,2},{1,3},{2,0},{3,1},{4,6},{5,7},{6,4},{7,5},{8,10},{9,11},{10,... | collective-permute-start | bytes 2408456 | tf_op jit(solution)/shard_map/ppermute | solution.py:311
  32.2 51.4 %collective-permute-start.8 = (bf16[784,512]{1,0:T(8,128)(2,1)}, bf16[784,512]{1,0:T(8,128)(2,1)S(1)}, u32[]{:S(2)}, u32[]{:S(2)}) collective-permute-start(bf16[784,512]{1,0:T(8,128)(2,1)} %collective-permute-done.7), channel_id=1, source_target_pairs={{8,0},{12,4},{16,24},{20,28},{9,1},{13,5},{17,25},{21,29},{10,2},{... | collective-permute-start | bytes 2408456 | tf_op jit(solution)/shard_map/ppermute | solution.py:314
  49.1 41.6 %collective-permute-start.10 = (bf16[800,256]{1,0:T(8,128)(2,1)S(1)}, bf16[800,256]{1,0:T(8,128)(2,1)S(1)}, u32[]{:S(2)}, u32[]{:S(2)}) collective-permute-start(bf16[800,256]{1,0:T(8,128)(2,1)S(1)} %get-tuple-element.16), channel_id=1, source_target_pairs={{0,8},{4,12},{8,0},{12,4},{16,24},{20,28},{24,16},{28,20},{1,9},{5... | collective-permute-start | bytes 1228808 | tf_op jit(solution)/shard_map/ppermute | solution.py:305
  52.0 38.8 %collective-permute-start.11 = (bf16[800,256]{1,0:T(8,128)(2,1)S(1)}, bf16[800,256]{1,0:T(8,128)(2,1)S(1)}, u32[]{:S(2)}, u32[]{:S(2)}) collective-permute-start(bf16[800,256]{1,0:T(8,128)(2,1)S(1)} %get-tuple-element.17), channel_id=1, source_target_pairs={{0,16},{4,20},{8,24},{12,28},{16,0},{20,4},{24,8},{28,12},{1,17},{... | collective-permute-start | bytes 1228808 | tf_op jit(solution)/shard_map/ppermute | solution.py:305
  53.3 37.5 %collective-permute-start.12 = (bf16[800,256]{1,0:T(8,128)(2,1)S(1)}, bf16[800,256]{1,0:T(8,128)(2,1)S(1)}, u32[]{:S(2)}, u32[]{:S(2)}) collective-permute-start(bf16[800,256]{1,0:T(8,128)(2,1)S(1)} %get-tuple-element.18), channel_id=1, source_target_pairs={{0,24},{4,28},{8,16},{12,20},{16,8},{20,12},{24,0},{28,4},{1,25},{... | collective-permute-start | bytes 1228808 | tf_op jit(solution)/shard_map/ppermute | solution.py:305
  55.9 37.0 %collective-permute-start.9 = (bf16[784,512]{1,0:T(8,128)(2,1)S(1)}, bf16[784,512]{1,0:T(8,128)(2,1)S(1)}, u32[]{:S(2)}, u32[]{:S(2)}) collective-permute-start(bf16[784,512]{1,0:T(8,128)(2,1)S(1)} %broadcast_select_fusion.1), channel_id=1, source_target_pairs={{0,2},{1,3},{2,0},{3,1},{4,6},{5,7},{6,4},{7,5},{8,10},{9,11},{10,... | collective-permute-start | bytes 2408456 | tf_op jit(solution)/shard_map/ppermute | solution.py:311
  90.8 18.3 %collective-permute-start.13 = (bf16[784,512]{1,0:T(8,128)(2,1)S(1)}, bf16[784,512]{1,0:T(8,128)(2,1)S(1)}, u32[]{:S(2)}, u32[]{:S(2)}) collective-permute-start(bf16[784,512]{1,0:T(8,128)(2,1)S(1)} %broadcast_select_fusion), channel_id=1, source_target_pairs={{0,2},{1,3},{2,0},{3,1},{4,6},{5,7},{6,4},{7,5},{8,10},{9,11},{10,... | collective-permute-start | bytes 2408456 | tf_op jit(solution)/shard_map/ppermute | solution.py:311
  92.8 36.8 %collective-permute-start.4 = (bf16[2,2,784,512]{3,2,1,0:T(8,128)(2,1)S(1)}, bf16[2,2,784,512]{3,2,1,0:T(8,128)(2,1)S(1)}, u32[]{:S(2)}, u32[]{:S(2)}) collective-permute-start(bf16[2,2,784,512]{3,2,1,0:T(8,128)(2,1)S(1)} %pad_maximum_fusion.refs_0_), channel_id=1, source_target_pairs={{0,1},{1,0},{2,3},{3,2},{4,5},{5,4},{6,7},{7,6},{8,9},{9,8},{10,11... | collective-permute-start | bytes 9633800 | tf_op jit(solution)/shard_map/ppermute | solution.py:311
  92.9 16.7 %collective-permute-start.16 = (bf16[688,256]{1,0:T(8,128)(2,1)S(1)}, bf16[688,256]{1,0:T(8,128)(2,1)S(1)}, u32[]{:S(2)}, u32[]{:S(2)}) collective-permute-start(bf16[688,256]{1,0:T(8,128)(2,1)S(1)} %get-tuple-element.22), channel_id=1, source_target_pairs={{0,24},{4,28},{8,16},{12,20},{16,8},{20,12},{24,0},{28,4},{1,25},{... | collective-permute-start | bytes 1056776 | tf_op jit(solution)/shard_map/ppermute | solution.py:305
  95.5 29.7 %collective-permute-start.15 = (bf16[688,256]{1,0:T(8,128)(2,1)S(1)}, bf16[688,256]{1,0:T(8,128)(2,1)S(1)}, u32[]{:S(2)}, u32[]{:S(2)}) collective-permute-start(bf16[688,256]{1,0:T(8,128)(2,1)S(1)} %get-tuple-element.21), channel_id=1, source_target_pairs={{0,16},{4,20},{8,24},{12,28},{16,0},{20,4},{24,8},{28,12},{1,17},{... | collective-permute-start | bytes 1056776 | tf_op jit(solution)/shard_map/ppermute | solution.py:305
  95.5 29.7 %collective-permute-start.14 = (bf16[688,256]{1,0:T(8,128)(2,1)S(1)}, bf16[688,256]{1,0:T(8,128)(2,1)S(1)}, u32[]{:S(2)}, u32[]{:S(2)}) collective-permute-start(bf16[688,256]{1,0:T(8,128)(2,1)S(1)} %get-tuple-element.20), channel_id=1, source_target_pairs={{0,8},{4,12},{8,0},{12,4},{16,24},{20,28},{24,16},{28,20},{1,9},{5... | collective-permute-start | bytes 1056776 | tf_op jit(solution)/shard_map/ppermute | solution.py:305
  125.2 43.6 %collective-permute-start.17 = (bf16[2,2,784,512]{3,2,1,0:T(8,128)(2,1)S(1)}, bf16[2,2,784,512]{3,2,1,0:T(8,128)(2,1)}, u32[]{:S(2)}, u32[]{:S(2)}) collective-permute-start(bf16[2,2,784,512]{3,2,1,0:T(8,128)(2,1)S(1)} %pad_maximum_fusion.1.refs_0_), channel_id=1, source_target_pairs={{0,1},{1,0},{2,3},{3,2},{4,5},{5,4},{6,7},{7,6},{8,9},{9,8},{10,11... | collective-permute-start | bytes 9633800 | tf_op jit(solution)/shard_map/ppermute | solution.py:311
  126.5 49.2 %collective-permute-start.22 = (bf16[3,800,256]{2,1,0:T(8,128)(2,1)}, bf16[3,800,256]{2,1,0:T(8,128)(2,1)}, u32[]{:S(2)}, u32[]{:S(2)}) collective-permute-start(bf16[3,800,256]{2,1,0:T(8,128)(2,1)} %pad_maximum_fusion.2), channel_id=1, source_target_pairs={{0,4},{4,0},{8,12},{12,8},{16,20},{20,16},{24,28},{28,24},{1,5},{5... | collective-permute-start | bytes 3686408 | tf_op jit(solution)/shard_map/ppermute | solution.py:308
  128.6 63.5 %collective-permute-start.21 = (bf16[3,688,256]{2,1,0:T(8,128)(2,1)}, bf16[3,688,256]{2,1,0:T(8,128)(2,1)}, u32[]{:S(2)}, u32[]{:S(2)}) collective-permute-start(bf16[3,688,256]{2,1,0:T(8,128)(2,1)} %pad_maximum_fusion.3), channel_id=1, source_target_pairs={{0,4},{4,0},{8,12},{12,8},{16,20},{20,16},{24,28},{28,24},{1,5},{5... | collective-permute-start | bytes 3170312 | tf_op jit(solution)/shard_map/ppermute | solution.py:308
  136.8 11.2 %collective-permute-start.20 = (bf16[512,256]{1,0:T(8,128)(2,1)}, bf16[512,256]{1,0:T(8,128)(2,1)S(1)}, u32[]{:S(2)}, u32[]{:S(2)}) collective-permute-start(bf16[512,256]{1,0:T(8,128)(2,1)} %get-tuple-element.26), channel_id=1, source_target_pairs={{0,24},{4,28},{8,16},{12,20},{16,8},{20,12},{24,0},{28,4},{1,25},{... | collective-permute-start | bytes 786440 | tf_op jit(solution)/shard_map/ppermute | solution.py:305
  139.3 21.9 %collective-permute-start.19 = (bf16[512,256]{1,0:T(8,128)(2,1)}, bf16[512,256]{1,0:T(8,128)(2,1)}, u32[]{:S(2)}, u32[]{:S(2)}) collective-permute-start(bf16[512,256]{1,0:T(8,128)(2,1)} %get-tuple-element.25), channel_id=1, source_target_pairs={{0,16},{4,20},{8,24},{12,28},{16,0},{20,4},{24,8},{28,12},{1,17},{... | collective-permute-start | bytes 786440 | tf_op jit(solution)/shard_map/ppermute | solution.py:305
  148.0 18.5 %collective-permute-start.18 = (bf16[512,256]{1,0:T(8,128)(2,1)}, bf16[512,256]{1,0:T(8,128)(2,1)}, u32[]{:S(2)}, u32[]{:S(2)}) collective-permute-start(bf16[512,256]{1,0:T(8,128)(2,1)} %get-tuple-element.24), channel_id=1, source_target_pairs={{0,8},{4,12},{8,0},{12,4},{16,24},{20,28},{24,16},{28,20},{1,9},{5... | collective-permute-start | bytes 786440 | tf_op jit(solution)/shard_map/ppermute | solution.py:305
  192.1 22.4 %collective-permute-start.23 = (bf16[3,512,256]{2,1,0:T(8,128)(2,1)}, bf16[3,512,256]{2,1,0:T(8,128)(2,1)S(1)}, u32[]{:S(2)}, u32[]{:S(2)}) collective-permute-start(bf16[3,512,256]{2,1,0:T(8,128)(2,1)} %pad_maximum_fusion.4), channel_id=1, source_target_pairs={{0,4},{4,0},{8,12},{12,8},{16,20},{20,16},{24,28},{28,24},{1,5},{5... | collective-permute-start | bytes 2359304 | tf_op jit(solution)/shard_map/ppermute | solution.py:308
  (33 other events, 333.1 us)

commit v4 on v3

--- a/solution.py
+++ b/solution.py
@@ -69,9 +69,9 @@
     real, base = plan.columns()
 
     copies = []
-    for source, group in plan.head_parts(head_refs):
-        lane = pl.multiple_of(group * depth, LANES)
-        copies.append(pltpu.make_async_copy(source, head.at[:, pl.ds(lane, depth)], sems.at[len(copies)]))
+    for source, first, group in plan.head_parts(head_refs):
+        target = head.at[pl.ds(first, source.shape[0]), pl.ds(pl.multiple_of(group * depth, LANES), depth)]
+        copies.append(pltpu.make_async_copy(source, target, sems.at[len(copies)]))
     for copy in copies:
         copy.start()
 
@@ -153,7 +153,7 @@
     width = plan.width
     smem = pl.BlockSpec(memory_space=pltpu.SMEM)
     vmem = pl.BlockSpec(memory_space=pltpu.VMEM)
-    anywhere = pl.BlockSpec(memory_space=pl.ANY)
+    anywhere = pl.BlockSpec(memory_space=pltpu.HBM)
     return pl.pallas_call(
         functools.partial(stats_kernel, plan, (len(tokens), len(ids), len(heads), len(before))),
         in_specs=[smem] * 3
@@ -168,11 +168,11 @@
             pltpu.VMEM((width, rows), jnp.float32),
             pltpu.VMEM((groups * splits, 1, rows), jnp.int32),
             pltpu.SMEM((groups * splits + 1,), jnp.int32),
-            pltpu.SemaphoreType.DMA((wide // heads[0].shape[-1],)),
+            pltpu.SemaphoreType.DMA((plan.copies,)),
             pltpu.SemaphoreType.DMA((2,)),
         ],
         out_shape=jax.ShapeDtypeStruct((groups, 4, splits * rows), jnp.float32),
-        compiler_params=pltpu.CompilerParams(vmem_limit_bytes=24 * 2**20),
+        compiler_params=pltpu.CompilerParams(vmem_limit_bytes=32 * 2**20),
         cost_estimate=pl.CostEstimate(
             flops=groups * splits * rows * wide * width // 8,
             bytes_accessed=wide * width,
@@ -187,6 +187,7 @@
         self.cuts = [breadth * index // groups // TILE * TILE for index in range(groups)] + [breadth]
         sizes = [end - start for start, end in zip(self.cuts, self.cuts[1:])]
         self.width, self.least = max(sizes), min(sizes)
+        self.copies = 1
 
     def spread(self, turned):
         turned = jnp.pad(turned, ((0, self.cuts[-2] + self.width - self.breadth), (0, 0)))
@@ -201,7 +202,7 @@
         return end - start, lax.axis_index("vocab") * self.breadth + start
 
     def head_parts(self, refs):
-        return [(refs[0], 0)]
+        return [(refs[0], 0, 0)]
 
     def group(self, group):
         return group
@@ -211,9 +212,11 @@
 
 
 class Line:
-    def __init__(self, breadth, chunk, start, width):
-        self.breadth, self.chunk, self.start = breadth, chunk, start
-        self.width = self.least = width
+    def __init__(self, breadth, chunk, cuts):
+        self.breadth, self.chunk, self.cuts = breadth, chunk, cuts
+        self.start = cuts[0][0]
+        self.width = self.least = sum(width for _, width in cuts)
+        self.copies = 2 + 6 * len(cuts)
 
     def columns(self):
         hi = lax.axis_index("dp") // 2
@@ -223,10 +226,13 @@
         position = lax.axis_index("dp")
         hi, low = position // 2, position % 2
         here = pl.ds(self.start, self.width)
-        mine = [refs[0].at[hi, here], *refs[2:5]]
-        other = [refs[1].at[here], *(refs[5].at[index] for index in range(3))]
-        found = [(source, 2 * (hi ^ step) + low) for step, source in enumerate(mine)]
-        return found + [(source, 2 * (hi ^ step) + (low ^ 1)) for step, source in enumerate(other)]
+        found = [(refs[0].at[hi, here], 0, 2 * hi + low), (refs[1].at[here], 0, 2 * hi + (low ^ 1))]
+        for index, (start, _) in enumerate(self.cuts):
+            *mine, other = refs[2 + 4 * index : 6 + 4 * index]
+            for step in (1, 2, 3):
+                found.append((mine[step - 1], start - self.start, 2 * (hi ^ step) + low))
+                found.append((other.at[step - 1], start - self.start, 2 * (hi ^ step) + (low ^ 1)))
+        return found
 
     def slot(self, group):
         hi = lax.axis_index("dp") // 2
@@ -342,15 +348,14 @@
         code = half[0, :, slots : slots + splits, : 2 * ROWS].astype(jnp.int32).reshape(2 * splits, 2, ROWS)
         return assemble(gain, [half, whole], ROWS), code[:, :1] * 256 + code[:, 1:]
 
-    def score(piece, before):
-        start, width = cuts[piece]
-        plan = Line(breadth, chunk, start, width)
-        heads = [turned, local_block, *sent[piece], across[piece]]
+    def score(pieces, before):
+        plan = Line(breadth, chunk, [cuts[piece] for piece in pieces])
+        heads = [turned, local_block, *(y for piece in pieces for y in (*sent[piece], across[piece]))]
         return stats(plan, jnp.zeros(1, jnp.int32), seq_lens, seq_owner, tokens, ids, heads, before)
 
     local_block = swap_lo(block(0, 0, chunk))
     own_across = over_x(own)
-    near_across = over_x(after(near, own_across, local_block))
+    near_across = over_x(after(near, cross, own_across, local_block))
     sent = [to_hi(0, out, cross_near, near_across, *blocks[1], *blocks[2])]
     far = jnp.where(middle, cross, out)
     far_across = over_x(far)
@@ -358,16 +363,15 @@
     last_across = over_x(after(last, *sent[0]))
     sent.append(to_hi(1, *sent[0], far_across))
     front_half = both(own, near, own_across, near_across)
-    front_whole = swap_part(front_half, 1)
+    across = [swap_lo(jnp.stack(sent[0]))]
+    front = ready(front_half, swap_part(after(front_half, *sent[1], across[0]), 1))
     back_half = both(far, last, far_across, last_across)
-    back_whole = swap_part(after(back_half, *sent[1]), 1)
-    tokens, ids = zip(ready(front_half, front_whole), ready(back_half, back_whole))
-    sent.append(to_hi(2, *sent[1], tokens[0]))
-    across = [swap_lo(jnp.stack(sent[0]))]
+    back = ready(back_half, swap_part(after(back_half, *sent[1], across[0]), 1))
+    tokens, ids = zip(front, back)
+    sent.append(to_hi(2, *sent[1]))
     across.append(swap_lo(jnp.stack(sent[1])))
-    found = score(0, [])
-    across.append(swap_lo(after(jnp.stack(sent[2]), across[1], found)))
-    found = score(2, [score(1, [found])])
+    across.append(swap_lo(after(jnp.stack(sent[2]), across[1])))
+    found = score((2,), [score((0, 1), [])])
     mine = merge([found[0]] + [swap_hi(found[step], step) for step in range(1, tall)])
     return merge([mine] + [swap_part(mine, step) for step in range(1, parts)])
 

time: 243 us -> 231 us (0.951); the launches traced: 239 us -> 230 us
  local copies, waits for them, and re-layouts: 18.3 us -> 13.2 us
  waiting for transfers between devices: 111 us -> 106 us
    ppermute x4, waiting for transfers between devices: 34.8 us -> 6.94 us  [along(): lax.ppermute(x, 'dp', [(2 * a + side, 2 * b + side) for a, b in moves for...]
    ppermute x13, waiting for transfers between devices: 56.2 us -> 82.1 us  [swap_hi(): return lax.ppermute(x, 'dp', [(g, g ^ 2 * step) for g in range(groups)])]
    unnamed x54 -> x60, local copies, waits for them, and re-layouts: 11.5 us -> 4.59 us
    ppermute x9, waiting for transfers between devices: 17.4 us -> 14.2 us  [swap_part(): return lax.ppermute(x, 'vocab', [(v, v ^ step) for v in range(parts)])]
    pallas_call x3 -> x2, Pallas kernels: 39.8 us -> 37.9 us  [stats(): pl.pallas_call(functools.partial(stats_kernel, plan, (len(tokens), len(id...]
  transfers between devices with their start and end apart: 30 -> 30, of which waited for: 15 -> 16; matrix products, arithmetic and copies ran while one was open for 6% -> 8% of each run, Pallas kernels for 17% -> 17%
where the time goes in v4:
time: 231 us; the launch traced here: 230 us
  waiting for transfers between devices  106 us (46%)
  Pallas kernels  51.1 us (22%)
  starting transfers between devices  43.9 us (19%)
  other arithmetic  14.8 us (6%)
  local copies, waits for them, and re-layouts  13.2 us (6%)
    ppermute x13, waiting for transfers between devices, swap_hi(): return lax.ppermute(x, 'dp', [(g, g ^ 2 * step) for g in range(groups)])  82.1 us
    pallas_call x2, Pallas kernels, stats(): pl.pallas_call(functools.partial(stats_kernel, plan, (len(tokens), len(id...  37.9 us
    ppermute x13, starting transfers between devices, swap_hi(): return lax.ppermute(x, 'dp', [(g, g ^ 2 * step) for g in range(groups)])  26.2 us
    ppermute x9, waiting for transfers between devices, swap_part(): return lax.ppermute(x, 'vocab', [(v, v ^ step) for v in range(parts)])  14.2 us
    pallas_call x2, Pallas kernels, assemble(): pl.pallas_call(functools.partial(assemble_kernel, len(sources) > 1), grid...  13.2 us
    ppermute x9, starting transfers between devices, swap_part(): return lax.ppermute(x, 'vocab', [(v, v ^ step) for v in range(parts)])  8.38 us
    squeeze x4, local copies, waits for them, and re-layouts, block(): lax.dynamic_slice(turned, (hi ^ step, start, 0), (1, width, depth))[0]  7.76 us
    ppermute x4, waiting for transfers between devices, along(): lax.ppermute(x, 'dp', [(2 * a + side, 2 * b + side) for a, b in moves for...  6.94 us
  transfers between devices with their start and end apart: 30, of which 16 were waited for; matrix products, arithmetic and copies ran while one was open for 8% of the time, Pallas kernels for 17%

profile of v4, /device:TPU:4, one launch (start us, length us, event | category | flops | bytes accessed | tf_op | source)
XLA Modules:
  0.0 230.2 jit_solution(16209214501375476096)
XLA Ops:
  9.2 13.2 %collective-permute-done = bf16[784,512]{1,0:T(8,128)(2,1)S(1)} collective-permute-done((bf16[784,512]{1,0:T(8,128)(2,1)S(1)}, bf16[784,512]{1,0:T(8,128)(2,1)S(1)}, u32[]{:S(2)}, u32[]{:S(2)}) %collective-permute-start) | collective-permute-done | bytes 802848 | tf_op jit(solution)/shard_map/ppermute | solution.py:311
  26.7 3.0 %collective-permute-done.3.refs_5_ = bf16[2000,256]{1,0:T(8,128)(2,1)S(1)} collective-permute-done((bf16[2000,256]{1,0:T(8,128)(2,1)S(1)}, bf16[2000,256]{1,0:T(8,128)(2,1)S(1)}, u32[]{:S(2)}, u32[]{:S(2)}) %collective-permute-start.3) | collective-permute-done | bytes 1024032 | tf_op jit(solution)/shard_map/ppermute | solution.py:314
  32.2 2.2 dynamic-slice_bitcast_fusion.4
  35.7 2.0 dynamic-slice_bitcast_fusion.7
  37.7 2.2 dynamic-slice_bitcast_fusion.1
  39.9 6.9 %collective-permute-done.5 = bf16[784,512]{1,0:T(8,128)(2,1)} collective-permute-done((bf16[784,512]{1,0:T(8,128)(2,1)}, bf16[784,512]{1,0:T(8,128)(2,1)}, u32[]{:S(2)}, u32[]{:S(2)}) %collective-permute-start.5) | collective-permute-done | bytes 802848 | tf_op jit(solution)/shard_map/ppermute | solution.py:320
  46.9 2.2 collective-permute-done.4
  50.0 3.2 %collective-permute-start.7 = (bf16[800,256]{1,0:T(8,128)(2,1)}, bf16[800,256]{1,0:T(8,128)(2,1)S(1)}, u32[]{:S(2)}, u32[]{:S(2)}) collective-permute-start(bf16[800,256]{1,0:T(8,128)(2,1)} %get-tuple-element.17), channel_id=1, source_target_pairs={{0,8},{4,12},{8,0},{12,4},{16,24},{20,28},{24,16},{28,20},{1,9},{5... | collective-permute-start | bytes 1228808 | tf_op jit(solution)/shard_map/ppermute | solution.py:311
  58.6 32.2 %collective-permute-done.7.refs_6_ = bf16[800,256]{1,0:T(8,128)(2,1)S(1)} collective-permute-done((bf16[800,256]{1,0:T(8,128)(2,1)}, bf16[800,256]{1,0:T(8,128)(2,1)S(1)}, u32[]{:S(2)}, u32[]{:S(2)}) %collective-permute-start.7) | collective-permute-done | bytes 409632 | tf_op jit(solution)/shard_map/ppermute | solution.py:311
  98.5 2.2 collective-permute-start.12
  102.4 8.5 %collective-permute-done.17 = bf16[784,512]{1,0:T(8,128)(2,1)S(1)} collective-permute-done((bf16[784,512]{1,0:T(8,128)(2,1)S(1)}, bf16[784,512]{1,0:T(8,128)(2,1)S(1)}, u32[]{:S(2)}, u32[]{:S(2)}) %collective-permute-start.17) | collective-permute-done | bytes 802848 | tf_op jit(solution)/shard_map/ppermute | solution.py:317
  112.5 12.6 %collective-permute-done.12.refs_11_ = bf16[688,256]{1,0:T(8,128)(2,1)S(1)} collective-permute-done((bf16[688,256]{1,0:T(8,128)(2,1)S(1)}, bf16[688,256]{1,0:T(8,128)(2,1)S(1)}, u32[]{:S(2)}, u32[]{:S(2)}) %collective-permute-start.12) | collective-permute-done | bytes 352288 | tf_op jit(solution)/shard_map/ppermute | solution.py:311
  125.2 2.2 pad_maximum_fusion.refs_0_
  130.4 4.5 %collective-permute-start.19 = (bf16[512,256]{1,0:T(8,128)(2,1)S(1)}, bf16[512,256]{1,0:T(8,128)(2,1)S(1)}, u32[]{:S(2)}, u32[]{:S(2)}) collective-permute-start(bf16[512,256]{1,0:T(8,128)(2,1)S(1)} %copy-done.28), channel_id=1, source_target_pairs={{0,8},{4,12},{8,0},{12,4},{16,24},{20,28},{24,16},{28,20},{1,9},{5... | collective-permute-start | bytes 786440 | tf_op jit(solution)/shard_map/ppermute | solution.py:311
  135.8 10.7 %collective-permute-done.19.refs_6_ = bf16[512,256]{1,0:T(8,128)(2,1)S(1)} collective-permute-done((bf16[512,256]{1,0:T(8,128)(2,1)S(1)}, bf16[512,256]{1,0:T(8,128)(2,1)S(1)}, u32[]{:S(2)}, u32[]{:S(2)}) %collective-permute-start.19) | collective-permute-done | bytes 262176 | tf_op jit(solution)/shard_map/ppermute | solution.py:311
  150.1 6.4 %collective-permute-done.21.refs_8_ = bf16[512,256]{1,0:T(8,128)(2,1)} collective-permute-done((bf16[512,256]{1,0:T(8,128)(2,1)}, bf16[512,256]{1,0:T(8,128)(2,1)}, u32[]{:S(2)}, u32[]{:S(2)}) %collective-permute-start.21) | collective-permute-done | bytes 262176 | tf_op jit(solution)/shard_map/ppermute | solution.py:311
  156.4 2.0 pad_maximum_fusion.4
  160.4 6.0 %shard_map.78.refs_1_ = bf16[2,3,2048,256]{3,2,1,0:T(8,128)(2,1)S(1)} custom-call(f32[1,2048]{1,0:T(1,128)S(1)} %bitcast.116, bf16[2,2,784,512]{3,2,1,0:T(8,128)(2,1)S(1)} %pad_maximum_fusion.1.refs_0_, bf16[2,2,784,512]{3,2,1,0:T(8,128)(2,1)} %collective-permute-done.18.refs_1_), custom_call_target="tpu_custom_call" | custom-call | flops 18874368 | bytes 12582912 | tf_op jit(solution)/shard_map/pallas_call | solution.py:43
  166.5 7.2 %shard_map.77.refs_0_ = bf16[2,3,2048,256]{3,2,1,0:T(8,128)(2,1)S(1)} custom-call(f32[1,2048]{1,0:T(1,128)S(1)} %bitcast.117, bf16[2,2,784,512]{3,2,1,0:T(8,128)(2,1)} %pad_maximum_fusion.refs_0_, bf16[2,2,784,512]{3,2,1,0:T(8,128)(2,1)} %collective-permute-done.15.refs_1_), custom_call_target="tpu_custom_call" | custom-call | flops 18874368 | bytes 12582912 | tf_op jit(solution)/shard_map/pallas_call | solution.py:43
  173.8 26.2 %shard_map.79.refs_10_ = f32[4,4,768]{2,1,0:T(4,128)S(1)} custom-call(s32[1]{0:T(128)} %constant.14.clone.1.start_ref, s32[16]{0:T(128)S(1)} %copy-done.17, s32[16]{0:T(128)S(1)} %copy-done.18, bf16[2,3,2048,256]{3,2,1,0:T(8,128)(2,1)S(1)} %shard_map.77.refs_0_, bf16[2,3,2048,256]{3,2,1,0:T(8,128)(2,1)S(1)} %shard_map.78.refs_1_, ...), custom_call_target="tpu_custom_call" | custom-call | flops 1170210816 | bytes 3047424 | tf_op jit(solution)/shard_map/pallas_call | solution.py:157
  200.0 11.8 %shard_map.80 = f32[4,4,768]{2,1,0:T(4,128)S(1)} custom-call(s32[1]{0:T(128)} %constant.14.clone.1.start_ref, s32[16]{0:T(128)S(1)} %copy-done.17, s32[16]{0:T(128)S(1)} %copy-done.18, bf16[2,3,2048,256]{3,2,1,0:T(8,128)(2,1)S(1)} %shard_map.77.refs_0_, bf16[2,3,2048,256]{3,2,1,0:T(8,128)(2,1)S(1)} %shard_map.78.refs_1_, ...), custom_call_target="tpu_custom_call" | custom-call | flops 402653184 | bytes 1048576 | tf_op jit(solution)/shard_map/pallas_call | solution.py:157
  211.8 5.2 %collective-permute-start.24 = (f32[4,768]{1,0:T(4,128)S(1)}, f32[4,768]{1,0:T(4,128)S(1)}, u32[]{:S(2)}, u32[]{:S(2)}) collective-permute-start(f32[4,768]{1,0:T(4,128)S(1)} %get-tuple-element.73), channel_id=1, source_target_pairs={{0,8},{4,12},{8,0},{12,4},{16,24},{20,28},{24,16},{28,20},{1,9},{5... | collective-permute-start | bytes 36872 | tf_op jit(solution)/shard_map/ppermute | solution.py:311
  217.0 2.2 collective-permute-start.26
  219.2 3.2 %collective-permute-done.26 = f32[4,768]{1,0:T(4,128)S(1)} collective-permute-done((f32[4,768]{1,0:T(4,128)S(1)}, f32[4,768]{1,0:T(4,128)S(1)}, u32[]{:S(2)}, u32[]{:S(2)}) %collective-permute-start.26) | collective-permute-done | bytes 12320 | tf_op jit(solution)/shard_map/ppermute | solution.py:311
  (139 shorter events, 51.1 us)
Async XLA Ops:
  2.6 19.7 %collective-permute-start = (bf16[784,512]{1,0:T(8,128)(2,1)S(1)}, bf16[784,512]{1,0:T(8,128)(2,1)S(1)}, u32[]{:S(2)}, u32[]{:S(2)}) collective-permute-start(bf16[784,512]{1,0:T(8,128)(2,1)S(1)} %get-tuple-element.70), channel_id=1, source_target_pairs={{0,8},{4,12},{8,0},{12,4},{16,24},{20,28},{24,16},{28,20},{1,9},{5... | collective-permute-start | bytes 2408456 | tf_op jit(solution)/shard_map/ppermute | solution.py:311
  5.5 24.2 %collective-permute-start.3 = (bf16[2000,256]{1,0:T(8,128)(2,1)S(1)}, bf16[2000,256]{1,0:T(8,128)(2,1)S(1)}, u32[]{:S(2)}, u32[]{:S(2)}) collective-permute-start(bf16[2000,256]{1,0:T(8,128)(2,1)S(1)} %dynamic-slice_bitcast_fusion), channel_id=1, source_target_pairs={{0,4},{4,0},{8,12},{12,8},{16,20},{20,16},{24,28},{28,24},{1,5},{5... | collective-permute-start | bytes 3072008 | tf_op jit(solution)/shard_map/ppermute | solution.py:314
  6.1 17.8 %collective-permute-start.2 = (bf16[784,512]{1,0:T(8,128)(2,1)S(1)}, bf16[784,512]{1,0:T(8,128)(2,1)}, u32[]{:S(2)}, u32[]{:S(2)}) collective-permute-start(bf16[784,512]{1,0:T(8,128)(2,1)S(1)} %get-tuple-element.70), channel_id=1, source_target_pairs={{8,16},{12,20},{16,8},{20,12},{9,17},{13,21},{17,9},{21,13},{10,18... | collective-permute-start | bytes 2408456 | tf_op jit(solution)/shard_map/ppermute | solution.py:320
  7.7 19.1 %collective-permute-start.1 = (bf16[784,512]{1,0:T(8,128)(2,1)S(1)}, bf16[784,512]{1,0:T(8,128)(2,1)S(1)}, u32[]{:S(2)}, u32[]{:S(2)}) collective-permute-start(bf16[784,512]{1,0:T(8,128)(2,1)S(1)} %get-tuple-element.70), channel_id=1, source_target_pairs={{0,2},{1,3},{2,0},{3,1},{4,6},{5,7},{6,4},{7,5},{8,10},{9,11},{10,... | collective-permute-start | bytes 2408456 | tf_op jit(solution)/shard_map/ppermute | solution.py:317
  22.3 12.1 %collective-permute-start.6 = (bf16[784,512]{1,0:T(8,128)(2,1)S(1)}, bf16[784,512]{1,0:T(8,128)(2,1)}, u32[]{:S(2)}, u32[]{:S(2)}) collective-permute-start(bf16[784,512]{1,0:T(8,128)(2,1)S(1)} %collective-permute-done), channel_id=1, source_target_pairs={{8,16},{12,20},{16,8},{20,12},{9,17},{13,21},{17,9},{21,13},{10,18... | collective-permute-start | bytes 2408456 | tf_op jit(solution)/shard_map/ppermute | solution.py:320
  23.9 23.0 %collective-permute-start.5 = (bf16[784,512]{1,0:T(8,128)(2,1)}, bf16[784,512]{1,0:T(8,128)(2,1)}, u32[]{:S(2)}, u32[]{:S(2)}) collective-permute-start(bf16[784,512]{1,0:T(8,128)(2,1)} %collective-permute-done.2), channel_id=1, source_target_pairs={{8,0},{12,4},{16,24},{20,28},{9,1},{13,5},{17,25},{21,29},{10,2},{... | collective-permute-start | bytes 2408456 | tf_op jit(solution)/shard_map/ppermute | solution.py:320
  30.7 18.4 %collective-permute-start.4 = (bf16[784,512]{1,0:T(8,128)(2,1)S(1)}, bf16[784,512]{1,0:T(8,128)(2,1)S(1)}, u32[]{:S(2)}, u32[]{:S(2)}) collective-permute-start(bf16[784,512]{1,0:T(8,128)(2,1)S(1)} %collective-permute-done), channel_id=1, source_target_pairs={{0,2},{1,3},{2,0},{3,1},{4,6},{5,7},{6,4},{7,5},{8,10},{9,11},{10,... | collective-permute-start | bytes 2408456 | tf_op jit(solution)/shard_map/ppermute | solution.py:317
  34.4 57.7 %collective-permute-start.16 = (bf16[784,512]{1,0:T(8,128)(2,1)}, bf16[784,512]{1,0:T(8,128)(2,1)}, u32[]{:S(2)}, u32[]{:S(2)}) collective-permute-start(bf16[784,512]{1,0:T(8,128)(2,1)} %collective-permute-done.6), channel_id=1, source_target_pairs={{8,0},{12,4},{16,24},{20,28},{9,1},{13,5},{17,25},{21,29},{10,2},{... | collective-permute-start | bytes 2408456 | tf_op jit(solution)/shard_map/ppermute | solution.py:320
  50.0 40.8 %collective-permute-start.7 = (bf16[800,256]{1,0:T(8,128)(2,1)}, bf16[800,256]{1,0:T(8,128)(2,1)S(1)}, u32[]{:S(2)}, u32[]{:S(2)}) collective-permute-start(bf16[800,256]{1,0:T(8,128)(2,1)} %get-tuple-element.17), channel_id=1, source_target_pairs={{0,8},{4,12},{8,0},{12,4},{16,24},{20,28},{24,16},{28,20},{1,9},{5... | collective-permute-start | bytes 1228808 | tf_op jit(solution)/shard_map/ppermute | solution.py:311
  53.2 37.6 %collective-permute-start.8 = (bf16[800,256]{1,0:T(8,128)(2,1)}, bf16[800,256]{1,0:T(8,128)(2,1)S(1)}, u32[]{:S(2)}, u32[]{:S(2)}) collective-permute-start(bf16[800,256]{1,0:T(8,128)(2,1)} %get-tuple-element.18), channel_id=1, source_target_pairs={{0,16},{4,20},{8,24},{12,28},{16,0},{20,4},{24,8},{28,12},{1,17},{... | collective-permute-start | bytes 1228808 | tf_op jit(solution)/shard_map/ppermute | solution.py:311
  54.4 36.4 %collective-permute-start.9 = (bf16[800,256]{1,0:T(8,128)(2,1)S(1)}, bf16[800,256]{1,0:T(8,128)(2,1)S(1)}, u32[]{:S(2)}, u32[]{:S(2)}) collective-permute-start(bf16[800,256]{1,0:T(8,128)(2,1)S(1)} %get-tuple-element.19), channel_id=1, source_target_pairs={{0,24},{4,28},{8,16},{12,20},{16,8},{20,12},{24,0},{28,4},{1,25},{... | collective-permute-start | bytes 1228808 | tf_op jit(solution)/shard_map/ppermute | solution.py:311
  57.1 39.9 %collective-permute-start.10 = (bf16[784,512]{1,0:T(8,128)(2,1)S(1)}, bf16[784,512]{1,0:T(8,128)(2,1)S(1)}, u32[]{:S(2)}, u32[]{:S(2)}) collective-permute-start(bf16[784,512]{1,0:T(8,128)(2,1)S(1)} %broadcast_select_fusion.1), channel_id=1, source_target_pairs={{0,2},{1,3},{2,0},{3,1},{4,6},{5,7},{6,4},{7,5},{8,10},{9,11},{10,... | collective-permute-start | bytes 2408456 | tf_op jit(solution)/shard_map/ppermute | solution.py:317
  91.0 34.2 %collective-permute-start.14 = (bf16[3,800,256]{2,1,0:T(8,128)(2,1)S(1)}, bf16[3,800,256]{2,1,0:T(8,128)(2,1)S(1)}, u32[]{:S(2)}, u32[]{:S(2)}) collective-permute-start(bf16[3,800,256]{2,1,0:T(8,128)(2,1)S(1)} %pad_maximum_fusion.2), channel_id=1, source_target_pairs={{0,4},{4,0},{8,12},{12,8},{16,20},{20,16},{24,28},{28,24},{1,5},{5... | collective-permute-start | bytes 3686408 | tf_op jit(solution)/shard_map/ppermute | solution.py:314
  93.3 17.6 %collective-permute-start.17 = (bf16[784,512]{1,0:T(8,128)(2,1)S(1)}, bf16[784,512]{1,0:T(8,128)(2,1)S(1)}, u32[]{:S(2)}, u32[]{:S(2)}) collective-permute-start(bf16[784,512]{1,0:T(8,128)(2,1)S(1)} %broadcast_select_fusion), channel_id=1, source_target_pairs={{0,2},{1,3},{2,0},{3,1},{4,6},{5,7},{6,4},{7,5},{8,10},{9,11},{10,... | collective-permute-start | bytes 2408456 | tf_op jit(solution)/shard_map/ppermute | solution.py:317
  97.8 14.6 %collective-permute-start.11 = (bf16[688,256]{1,0:T(8,128)(2,1)S(1)}, bf16[688,256]{1,0:T(8,128)(2,1)S(1)}, u32[]{:S(2)}, u32[]{:S(2)}) collective-permute-start(bf16[688,256]{1,0:T(8,128)(2,1)S(1)} %copy-done.27), channel_id=1, source_target_pairs={{0,8},{4,12},{8,0},{12,4},{16,24},{20,28},{24,16},{28,20},{1,9},{5... | collective-permute-start | bytes 1056776 | tf_op jit(solution)/shard_map/ppermute | solution.py:311
  98.5 26.6 %collective-permute-start.12 = (bf16[688,256]{1,0:T(8,128)(2,1)S(1)}, bf16[688,256]{1,0:T(8,128)(2,1)S(1)}, u32[]{:S(2)}, u32[]{:S(2)}) collective-permute-start(bf16[688,256]{1,0:T(8,128)(2,1)S(1)} %copy-done.26), channel_id=1, source_target_pairs={{0,16},{4,20},{8,24},{12,28},{16,0},{20,4},{24,8},{28,12},{1,17},{... | collective-permute-start | bytes 1056776 | tf_op jit(solution)/shard_map/ppermute | solution.py:311
  100.7 24.4 %collective-permute-start.13 = (bf16[688,256]{1,0:T(8,128)(2,1)S(1)}, bf16[688,256]{1,0:T(8,128)(2,1)S(1)}, u32[]{:S(2)}, u32[]{:S(2)}) collective-permute-start(bf16[688,256]{1,0:T(8,128)(2,1)S(1)} %copy-done.25), channel_id=1, source_target_pairs={{0,24},{4,28},{8,16},{12,20},{16,8},{20,12},{24,0},{28,4},{1,25},{... | collective-permute-start | bytes 1056776 | tf_op jit(solution)/shard_map/ppermute | solution.py:311
  125.1 35.3 %collective-permute-start.18 = (bf16[2,2,784,512]{3,2,1,0:T(8,128)(2,1)S(1)}, bf16[2,2,784,512]{3,2,1,0:T(8,128)(2,1)}, u32[]{:S(2)}, u32[]{:S(2)}) collective-permute-start(bf16[2,2,784,512]{3,2,1,0:T(8,128)(2,1)S(1)} %pad_maximum_fusion.1.refs_0_), channel_id=1, source_target_pairs={{0,1},{1,0},{2,3},{3,2},{4,5},{5,4},{6,7},{7,6},{8,9},{9,8},{10,11... | collective-permute-start | bytes 9633800 | tf_op jit(solution)/shard_map/ppermute | solution.py:317
  127.4 39.1 %collective-permute-start.15 = (bf16[2,2,784,512]{3,2,1,0:T(8,128)(2,1)}, bf16[2,2,784,512]{3,2,1,0:T(8,128)(2,1)}, u32[]{:S(2)}, u32[]{:S(2)}) collective-permute-start(bf16[2,2,784,512]{3,2,1,0:T(8,128)(2,1)} %pad_maximum_fusion.refs_0_), channel_id=1, source_target_pairs={{0,1},{1,0},{2,3},{3,2},{4,5},{5,4},{6,7},{7,6},{8,9},{9,8},{10,11... | collective-permute-start | bytes 9633800 | tf_op jit(solution)/shard_map/ppermute | solution.py:317
  128.9 29.5 %collective-permute-start.22 = (bf16[3,688,256]{2,1,0:T(8,128)(2,1)}, bf16[3,688,256]{2,1,0:T(8,128)(2,1)}, u32[]{:S(2)}, u32[]{:S(2)}) collective-permute-start(bf16[3,688,256]{2,1,0:T(8,128)(2,1)} %pad_maximum_fusion.3), channel_id=1, source_target_pairs={{0,4},{4,0},{8,12},{12,8},{16,20},{20,16},{24,28},{28,24},{1,5},{5... | collective-permute-start | bytes 3170312 | tf_op jit(solution)/shard_map/ppermute | solution.py:314
  130.4 16.1 %collective-permute-start.19 = (bf16[512,256]{1,0:T(8,128)(2,1)S(1)}, bf16[512,256]{1,0:T(8,128)(2,1)S(1)}, u32[]{:S(2)}, u32[]{:S(2)}) collective-permute-start(bf16[512,256]{1,0:T(8,128)(2,1)S(1)} %copy-done.28), channel_id=1, source_target_pairs={{0,8},{4,12},{8,0},{12,4},{16,24},{20,28},{24,16},{28,20},{1,9},{5... | collective-permute-start | bytes 786440 | tf_op jit(solution)/shard_map/ppermute | solution.py:311
  134.9 15.2 %collective-permute-start.20 = (bf16[512,256]{1,0:T(8,128)(2,1)}, bf16[512,256]{1,0:T(8,128)(2,1)}, u32[]{:S(2)}, u32[]{:S(2)}) collective-permute-start(bf16[512,256]{1,0:T(8,128)(2,1)} %get-tuple-element.27), channel_id=1, source_target_pairs={{0,16},{4,20},{8,24},{12,28},{16,0},{20,4},{24,8},{28,12},{1,17},{... | collective-permute-start | bytes 786440 | tf_op jit(solution)/shard_map/ppermute | solution.py:311
  146.5 10.0 %collective-permute-start.21 = (bf16[512,256]{1,0:T(8,128)(2,1)}, bf16[512,256]{1,0:T(8,128)(2,1)}, u32[]{:S(2)}, u32[]{:S(2)}) collective-permute-start(bf16[512,256]{1,0:T(8,128)(2,1)} %get-tuple-element.28), channel_id=1, source_target_pairs={{0,24},{4,28},{8,16},{12,20},{16,8},{20,12},{24,0},{28,4},{1,25},{... | collective-permute-start | bytes 786440 | tf_op jit(solution)/shard_map/ppermute | solution.py:311
  158.4 41.6 %collective-permute-start.23 = (bf16[3,512,256]{2,1,0:T(8,128)(2,1)}, bf16[3,512,256]{2,1,0:T(8,128)(2,1)}, u32[]{:S(2)}, u32[]{:S(2)}) collective-permute-start(bf16[3,512,256]{2,1,0:T(8,128)(2,1)} %pad_maximum_fusion.4), channel_id=1, source_target_pairs={{0,4},{4,0},{8,12},{12,8},{16,20},{20,16},{24,28},{28,24},{1,5},{5... | collective-permute-start | bytes 2359304 | tf_op jit(solution)/shard_map/ppermute | solution.py:314
  (36 other events, 241.8 us)

commit v5 on v4

--- a/solution.py
+++ b/solution.py
@@ -47,7 +47,7 @@
         + [pl.BlockSpec((y.shape[0], 1, rows, features), lambda i, j: (0, i, j, 0)) for y in sources],
         out_specs=pl.BlockSpec((1, 1, wide, rows), lambda i, j: (i, j, 0, 0)),
         out_shape=jax.ShapeDtypeStruct((count, splits, wide, rows), sources[0].dtype),
-        compiler_params=pltpu.CompilerParams(vmem_limit_bytes=24 * 2**20),
+        compiler_params=pltpu.CompilerParams(vmem_limit_bytes=60 * 2**20),
         cost_estimate=pl.CostEstimate(
             flops=6 * count * splits * rows * wide,
             bytes_accessed=4 * count * splits * rows * wide,
@@ -172,7 +172,7 @@
             pltpu.SemaphoreType.DMA((2,)),
         ],
         out_shape=jax.ShapeDtypeStruct((groups, 4, splits * rows), jnp.float32),
-        compiler_params=pltpu.CompilerParams(vmem_limit_bytes=32 * 2**20),
+        compiler_params=pltpu.CompilerParams(vmem_limit_bytes=60 * 2**20),
         cost_estimate=pl.CostEstimate(
             flops=groups * splits * rows * wide * width // 8,
             bytes_accessed=wide * width,
@@ -368,7 +368,8 @@
     back_half = both(far, last, far_across, last_across)
     back = ready(back_half, swap_part(after(back_half, *sent[1], across[0]), 1))
     tokens, ids = zip(front, back)
-    sent.append(to_hi(2, *sent[1]))
+    waits = (tokens[1], sent[1][1], tokens[0])
+    sent.append([swap_hi(after(y, *sent[1], wait), step) for step, (y, wait) in enumerate(zip(blocks[2], waits), 1)])
     across.append(swap_lo(jnp.stack(sent[1])))
     across.append(swap_lo(after(jnp.stack(sent[2]), across[1])))
     found = score((2,), [score((0, 1), [])])

time: 231 us -> 233 us (level)
  waiting for transfers between devices: 106 us -> 95.2 us
  Pallas kernels: 51.1 us -> 59.4 us
  local copies, waits for them, and re-layouts: 13.2 us -> 16.3 us
    ppermute x13, waiting for transfers between devices: 82.1 us -> 70.9 us  [swap_hi(): return lax.ppermute(x, 'dp', [(g, g ^ 2 * step) for g in range(groups)])]
    pallas_call x2, Pallas kernels: 37.9 us -> 43.2 us  [stats(): pl.pallas_call(functools.partial(stats_kernel, plan, (len(tokens), len(id...]
    pallas_call x2, Pallas kernels: 13.2 us -> 16.2 us  [assemble(): pl.pallas_call(functools.partial(assemble_kernel, len(sources) > 1), grid...]
    unnamed x60 -> x50, local copies, waits for them, and re-layouts: 4.59 us -> 6.18 us
  transfers between devices with their start and end apart: 30 -> 30, of which waited for: 16 -> 14; matrix products, arithmetic and copies ran while one was open for 8% -> 8% of each run, Pallas kernels for 17% -> 19%
where the time goes in v5:
time: 233 us; the launch traced here: 232 us
  waiting for transfers between devices  95.2 us (41%)
  Pallas kernels  59.4 us (25%)
  starting transfers between devices  44.4 us (19%)
  local copies, waits for them, and re-layouts  16.3 us (7%)
  other arithmetic  15.7 us (7%)
    ppermute x13, waiting for transfers between devices, swap_hi(): return lax.ppermute(x, 'dp', [(g, g ^ 2 * step) for g in range(groups)])  70.9 us
    pallas_call x2, Pallas kernels, stats(): pl.pallas_call(functools.partial(stats_kernel, plan, (len(tokens), len(id...  43.2 us
    ppermute x13, starting transfers between devices, swap_hi(): return lax.ppermute(x, 'dp', [(g, g ^ 2 * step) for g in range(groups)])  25.9 us
    pallas_call x2, Pallas kernels, assemble(): pl.pallas_call(functools.partial(assemble_kernel, len(sources) > 1), grid...  16.2 us
    ppermute x9, waiting for transfers between devices, swap_part(): return lax.ppermute(x, 'vocab', [(v, v ^ step) for v in range(parts)])  13.4 us
    ppermute x9, starting transfers between devices, swap_part(): return lax.ppermute(x, 'vocab', [(v, v ^ step) for v in range(parts)])  8.57 us
    ppermute x4, waiting for transfers between devices, along(): lax.ppermute(x, 'dp', [(2 * a + side, 2 * b + side) for a, b in moves for...  7.91 us
    squeeze x4, local copies, waits for them, and re-layouts, block(): lax.dynamic_slice(turned, (hi ^ step, start, 0), (1, width, depth))[0]  7.66 us
  transfers between devices with their start and end apart: 30, of which 14 were waited for; matrix products, arithmetic and copies ran while one was open for 8% of the time, Pallas kernels for 19%

profile of v5, /device:TPU:4, one launch (start us, length us, event | category | flops | bytes accessed | tf_op | source)
XLA Modules:
  0.0 232.0 jit_solution(627630652169412317)
XLA Ops:
  2.6 1.6 collective-permute-start
  6.1 1.6 collective-permute-start.2
  9.2 13.1 %collective-permute-done = bf16[784,512]{1,0:T(8,128)(2,1)S(1)} collective-permute-done((bf16[784,512]{1,0:T(8,128)(2,1)S(1)}, bf16[784,512]{1,0:T(8,128)(2,1)S(1)}, u32[]{:S(2)}, u32[]{:S(2)}) %collective-permute-start) | collective-permute-done | bytes 802848 | tf_op jit(solution)/shard_map/ppermute | solution.py:311
  25.2 1.6 collective-permute-done.1
  26.8 3.0 %collective-permute-done.3.refs_5_ = bf16[2000,256]{1,0:T(8,128)(2,1)} collective-permute-done((bf16[2000,256]{1,0:T(8,128)(2,1)S(1)}, bf16[2000,256]{1,0:T(8,128)(2,1)}, u32[]{:S(2)}, u32[]{:S(2)}) %collective-permute-start.3) | collective-permute-done | bytes 1024032 | tf_op jit(solution)/shard_map/ppermute | solution.py:314
  31.3 2.2 dynamic-slice_bitcast_fusion.4
  34.8 1.9 dynamic-slice_bitcast_fusion.7
  36.7 2.3 dynamic-slice_bitcast_fusion.1
  39.0 7.9 %collective-permute-done.5 = bf16[784,512]{1,0:T(8,128)(2,1)} collective-permute-done((bf16[784,512]{1,0:T(8,128)(2,1)}, bf16[784,512]{1,0:T(8,128)(2,1)}, u32[]{:S(2)}, u32[]{:S(2)}) %collective-permute-start.5) | collective-permute-done | bytes 802848 | tf_op jit(solution)/shard_map/ppermute | solution.py:320
  49.1 3.9 %collective-permute-start.7 = (bf16[800,256]{1,0:T(8,128)(2,1)}, bf16[800,256]{1,0:T(8,128)(2,1)S(1)}, u32[]{:S(2)}, u32[]{:S(2)}) collective-permute-start(bf16[800,256]{1,0:T(8,128)(2,1)} %get-tuple-element.17), channel_id=1, source_target_pairs={{0,8},{4,12},{8,0},{12,4},{16,24},{20,28},{24,16},{28,20},{1,9},{5... | collective-permute-start | bytes 1228808 | tf_op jit(solution)/shard_map/ppermute | solution.py:311
  58.4 32.4 %collective-permute-done.7.refs_6_ = bf16[800,256]{1,0:T(8,128)(2,1)S(1)} collective-permute-done((bf16[800,256]{1,0:T(8,128)(2,1)}, bf16[800,256]{1,0:T(8,128)(2,1)S(1)}, u32[]{:S(2)}, u32[]{:S(2)}) %collective-permute-start.7) | collective-permute-done | bytes 409632 | tf_op jit(solution)/shard_map/ppermute | solution.py:311
  98.3 2.4 %collective-permute-start.12 = (bf16[688,256]{1,0:T(8,128)(2,1)S(1)}, bf16[688,256]{1,0:T(8,128)(2,1)S(1)}, u32[]{:S(2)}, u32[]{:S(2)}) collective-permute-start(bf16[688,256]{1,0:T(8,128)(2,1)S(1)} %copy-done.19), channel_id=1, source_target_pairs={{0,16},{4,20},{8,24},{12,28},{16,0},{20,4},{24,8},{28,12},{1,17},{... | collective-permute-start | bytes 1056776 | tf_op jit(solution)/shard_map/ppermute | solution.py:311
  102.4 8.5 %collective-permute-done.17 = bf16[784,512]{1,0:T(8,128)(2,1)S(1)} collective-permute-done((bf16[784,512]{1,0:T(8,128)(2,1)S(1)}, bf16[784,512]{1,0:T(8,128)(2,1)S(1)}, u32[]{:S(2)}, u32[]{:S(2)}) %collective-permute-start.17) | collective-permute-done | bytes 802848 | tf_op jit(solution)/shard_map/ppermute | solution.py:317
  112.3 12.8 %collective-permute-done.12.refs_11_ = bf16[688,256]{1,0:T(8,128)(2,1)S(1)} collective-permute-done((bf16[688,256]{1,0:T(8,128)(2,1)S(1)}, bf16[688,256]{1,0:T(8,128)(2,1)S(1)}, u32[]{:S(2)}, u32[]{:S(2)}) %collective-permute-start.12) | collective-permute-done | bytes 352288 | tf_op jit(solution)/shard_map/ppermute | solution.py:311
  125.2 2.0 pad_maximum_fusion.refs_0_
  130.8 5.4 %collective-permute-start.20 = (bf16[512,256]{1,0:T(8,128)(2,1)S(1)}, bf16[512,256]{1,0:T(8,128)(2,1)S(1)}, u32[]{:S(2)}, u32[]{:S(2)}) collective-permute-start(bf16[512,256]{1,0:T(8,128)(2,1)S(1)} %copy-done.21), channel_id=1, source_target_pairs={{0,16},{4,20},{8,24},{12,28},{16,0},{20,4},{24,8},{28,12},{1,17},{... | collective-permute-start | bytes 786440 | tf_op jit(solution)/shard_map/ppermute | solution.py:311
  136.2 1.7 copy-done.3
  137.9 8.1 %shard_map.78.refs_1_ = bf16[2,3,2048,256]{3,2,1,0:T(8,128)(2,1)} custom-call(f32[1,2048]{1,0:T(1,128)} %bitcast.125, bf16[2,2,784,512]{3,2,1,0:T(8,128)(2,1)} %copy-done, bf16[2,2,784,512]{3,2,1,0:T(8,128)(2,1)} %copy-done.3), custom_call_target="tpu_custom_call" | custom-call | flops 18874368 | bytes 12582912 | tf_op jit(solution)/shard_map/pallas_call | solution.py:43
  146.0 8.1 %shard_map.77.refs_0_ = bf16[2,3,2048,256]{3,2,1,0:T(8,128)(2,1)} custom-call(f32[1,2048]{1,0:T(1,128)} %bitcast.126, bf16[2,2,784,512]{3,2,1,0:T(8,128)(2,1)} %pad_maximum_fusion.refs_0_, bf16[2,2,784,512]{3,2,1,0:T(8,128)(2,1)} %collective-permute-done.15.refs_1_), custom_call_target="tpu_custom_call" | custom-call | flops 18874368 | bytes 12582912 | tf_op jit(solution)/shard_map/pallas_call | solution.py:43
  155.6 8.1 %collective-permute-done.21.refs_8_ = bf16[512,256]{1,0:T(8,128)(2,1)S(1)} collective-permute-done((bf16[512,256]{1,0:T(8,128)(2,1)S(1)}, bf16[512,256]{1,0:T(8,128)(2,1)S(1)}, u32[]{:S(2)}, u32[]{:S(2)}) %collective-permute-start.21) | collective-permute-done | bytes 262176 | tf_op jit(solution)/shard_map/ppermute | solution.py:311
  167.8 27.7 %shard_map.79.refs_10_ = f32[4,4,768]{2,1,0:T(4,128)} custom-call(s32[1]{0:T(128)} %constant.14.clone.1.start_ref, s32[16]{0:T(128)} %lens_ref.3, s32[16]{0:T(128)} %owner_ref.3, bf16[2,3,2048,256]{3,2,1,0:T(8,128)(2,1)} %shard_map.77.refs_0_, bf16[2,3,2048,256]{3,2,1,0:T(8,128)(2,1)} %shard_map.78.refs_1_, s32[6,1,256]{2,1,0:T(1,128)} %get-tuple-element.85.refs_2_, ...), custom_call_target="tpu_custom_call" | custom-call | flops 1170210816 | bytes 3047424 | tf_op jit(solution)/shard_map/pallas_call | solution.py:157
  196.5 15.5 %shard_map.80 = f32[4,4,768]{2,1,0:T(4,128)} custom-call(s32[1]{0:T(128)} %constant.14.clone.1.start_ref, s32[16]{0:T(128)} %lens_ref.3, s32[16]{0:T(128)} %owner_ref.3, bf16[2,3,2048,256]{3,2,1,0:T(8,128)(2,1)} %shard_map.77.refs_0_, bf16[2,3,2048,256]{3,2,1,0:T(8,128)(2,1)} %shard_map.78.refs_1_, s32[6,1,256]{2,1,0:T(1,128)} %get-tuple-element.85.refs_2_, ...), custom_call_target="tpu_custom_call" | custom-call | flops 402653184 | bytes 1048576 | tf_op jit(solution)/shard_map/pallas_call | solution.py:157
  212.7 4.9 %collective-permute-start.24 = (f32[4,768]{1,0:T(4,128)S(1)}, f32[4,768]{1,0:T(4,128)S(1)}, u32[]{:S(2)}, u32[]{:S(2)}) collective-permute-start(f32[4,768]{1,0:T(4,128)S(1)} %get-tuple-element.73), channel_id=1, source_target_pairs={{0,8},{4,12},{8,0},{12,4},{16,24},{20,28},{24,16},{28,20},{1,9},{5... | collective-permute-start | bytes 36872 | tf_op jit(solution)/shard_map/ppermute | solution.py:311
  220.1 3.0 %collective-permute-done.26 = f32[4,768]{1,0:T(4,128)S(1)} collective-permute-done((f32[4,768]{1,0:T(4,128)S(1)}, f32[4,768]{1,0:T(4,128)S(1)}, u32[]{:S(2)}, u32[]{:S(2)}) %collective-permute-start.26) | collective-permute-done | bytes 12320 | tf_op jit(solution)/shard_map/ppermute | solution.py:311
  (129 shorter events, 51.4 us)
Async XLA Ops:
  2.6 19.7 %collective-permute-start = (bf16[784,512]{1,0:T(8,128)(2,1)S(1)}, bf16[784,512]{1,0:T(8,128)(2,1)S(1)}, u32[]{:S(2)}, u32[]{:S(2)}) collective-permute-start(bf16[784,512]{1,0:T(8,128)(2,1)S(1)} %get-tuple-element.70), channel_id=1, source_target_pairs={{0,8},{4,12},{8,0},{12,4},{16,24},{20,28},{24,16},{28,20},{1,9},{5... | collective-permute-start | bytes 2408456 | tf_op jit(solution)/shard_map/ppermute | solution.py:311
  5.5 24.3 %collective-permute-start.3 = (bf16[2000,256]{1,0:T(8,128)(2,1)S(1)}, bf16[2000,256]{1,0:T(8,128)(2,1)}, u32[]{:S(2)}, u32[]{:S(2)}) collective-permute-start(bf16[2000,256]{1,0:T(8,128)(2,1)S(1)} %dynamic-slice_bitcast_fusion), channel_id=1, source_target_pairs={{0,4},{4,0},{8,12},{12,8},{16,20},{20,16},{24,28},{28,24},{1,5},{5... | collective-permute-start | bytes 3072008 | tf_op jit(solution)/shard_map/ppermute | solution.py:314
  6.1 17.8 %collective-permute-start.2 = (bf16[784,512]{1,0:T(8,128)(2,1)S(1)}, bf16[784,512]{1,0:T(8,128)(2,1)}, u32[]{:S(2)}, u32[]{:S(2)}) collective-permute-start(bf16[784,512]{1,0:T(8,128)(2,1)S(1)} %get-tuple-element.70), channel_id=1, source_target_pairs={{8,16},{12,20},{16,8},{20,12},{9,17},{13,21},{17,9},{21,13},{10,18... | collective-permute-start | bytes 2408456 | tf_op jit(solution)/shard_map/ppermute | solution.py:320
  7.7 19.1 %collective-permute-start.1 = (bf16[784,512]{1,0:T(8,128)(2,1)S(1)}, bf16[784,512]{1,0:T(8,128)(2,1)S(1)}, u32[]{:S(2)}, u32[]{:S(2)}) collective-permute-start(bf16[784,512]{1,0:T(8,128)(2,1)S(1)} %get-tuple-element.70), channel_id=1, source_target_pairs={{0,2},{1,3},{2,0},{3,1},{4,6},{5,7},{6,4},{7,5},{8,10},{9,11},{10,... | collective-permute-start | bytes 2408456 | tf_op jit(solution)/shard_map/ppermute | solution.py:317
  22.3 11.2 %collective-permute-start.6 = (bf16[784,512]{1,0:T(8,128)(2,1)S(1)}, bf16[784,512]{1,0:T(8,128)(2,1)}, u32[]{:S(2)}, u32[]{:S(2)}) collective-permute-start(bf16[784,512]{1,0:T(8,128)(2,1)S(1)} %collective-permute-done), channel_id=1, source_target_pairs={{8,16},{12,20},{16,8},{20,12},{9,17},{13,21},{17,9},{21,13},{10,18... | collective-permute-start | bytes 2408456 | tf_op jit(solution)/shard_map/ppermute | solution.py:320
  23.9 23.0 %collective-permute-start.5 = (bf16[784,512]{1,0:T(8,128)(2,1)}, bf16[784,512]{1,0:T(8,128)(2,1)}, u32[]{:S(2)}, u32[]{:S(2)}) collective-permute-start(bf16[784,512]{1,0:T(8,128)(2,1)} %collective-permute-done.2), channel_id=1, source_target_pairs={{8,0},{12,4},{16,24},{20,28},{9,1},{13,5},{17,25},{21,29},{10,2},{... | collective-permute-start | bytes 2408456 | tf_op jit(solution)/shard_map/ppermute | solution.py:320
  29.8 18.4 %collective-permute-start.4 = (bf16[784,512]{1,0:T(8,128)(2,1)S(1)}, bf16[784,512]{1,0:T(8,128)(2,1)S(1)}, u32[]{:S(2)}, u32[]{:S(2)}) collective-permute-start(bf16[784,512]{1,0:T(8,128)(2,1)S(1)} %collective-permute-done), channel_id=1, source_target_pairs={{0,2},{1,3},{2,0},{3,1},{4,6},{5,7},{6,4},{7,5},{8,10},{9,11},{10,... | collective-permute-start | bytes 2408456 | tf_op jit(solution)/shard_map/ppermute | solution.py:317
  33.5 58.5 %collective-permute-start.16 = (bf16[784,512]{1,0:T(8,128)(2,1)}, bf16[784,512]{1,0:T(8,128)(2,1)}, u32[]{:S(2)}, u32[]{:S(2)}) collective-permute-start(bf16[784,512]{1,0:T(8,128)(2,1)} %collective-permute-done.6), channel_id=1, source_target_pairs={{8,0},{12,4},{16,24},{20,28},{9,1},{13,5},{17,25},{21,29},{10,2},{... | collective-permute-start | bytes 2408456 | tf_op jit(solution)/shard_map/ppermute | solution.py:320
  49.1 41.6 %collective-permute-start.7 = (bf16[800,256]{1,0:T(8,128)(2,1)}, bf16[800,256]{1,0:T(8,128)(2,1)S(1)}, u32[]{:S(2)}, u32[]{:S(2)}) collective-permute-start(bf16[800,256]{1,0:T(8,128)(2,1)} %get-tuple-element.17), channel_id=1, source_target_pairs={{0,8},{4,12},{8,0},{12,4},{16,24},{20,28},{24,16},{28,20},{1,9},{5... | collective-permute-start | bytes 1228808 | tf_op jit(solution)/shard_map/ppermute | solution.py:311
  53.0 37.8 %collective-permute-start.8 = (bf16[800,256]{1,0:T(8,128)(2,1)}, bf16[800,256]{1,0:T(8,128)(2,1)S(1)}, u32[]{:S(2)}, u32[]{:S(2)}) collective-permute-start(bf16[800,256]{1,0:T(8,128)(2,1)} %get-tuple-element.18), channel_id=1, source_target_pairs={{0,16},{4,20},{8,24},{12,28},{16,0},{20,4},{24,8},{28,12},{1,17},{... | collective-permute-start | bytes 1228808 | tf_op jit(solution)/shard_map/ppermute | solution.py:311
  54.2 36.6 %collective-permute-start.9 = (bf16[800,256]{1,0:T(8,128)(2,1)}, bf16[800,256]{1,0:T(8,128)(2,1)S(1)}, u32[]{:S(2)}, u32[]{:S(2)}) collective-permute-start(bf16[800,256]{1,0:T(8,128)(2,1)} %get-tuple-element.19), channel_id=1, source_target_pairs={{0,24},{4,28},{8,16},{12,20},{16,8},{20,12},{24,0},{28,4},{1,25},{... | collective-permute-start | bytes 1228808 | tf_op jit(solution)/shard_map/ppermute | solution.py:311
  56.9 40.1 %collective-permute-start.10 = (bf16[784,512]{1,0:T(8,128)(2,1)S(1)}, bf16[784,512]{1,0:T(8,128)(2,1)S(1)}, u32[]{:S(2)}, u32[]{:S(2)}) collective-permute-start(bf16[784,512]{1,0:T(8,128)(2,1)S(1)} %broadcast_select_fusion.1), channel_id=1, source_target_pairs={{0,2},{1,3},{2,0},{3,1},{4,6},{5,7},{6,4},{7,5},{8,10},{9,11},{10,... | collective-permute-start | bytes 2408456 | tf_op jit(solution)/shard_map/ppermute | solution.py:317
  91.0 34.2 %collective-permute-start.14 = (bf16[3,800,256]{2,1,0:T(8,128)(2,1)S(1)}, bf16[3,800,256]{2,1,0:T(8,128)(2,1)}, u32[]{:S(2)}, u32[]{:S(2)}) collective-permute-start(bf16[3,800,256]{2,1,0:T(8,128)(2,1)S(1)} %pad_maximum_fusion.2), channel_id=1, source_target_pairs={{0,4},{4,0},{8,12},{12,8},{16,20},{20,16},{24,28},{28,24},{1,5},{5... | collective-permute-start | bytes 3686408 | tf_op jit(solution)/shard_map/ppermute | solution.py:314
  93.3 17.6 %collective-permute-start.17 = (bf16[784,512]{1,0:T(8,128)(2,1)S(1)}, bf16[784,512]{1,0:T(8,128)(2,1)S(1)}, u32[]{:S(2)}, u32[]{:S(2)}) collective-permute-start(bf16[784,512]{1,0:T(8,128)(2,1)S(1)} %broadcast_select_fusion), channel_id=1, source_target_pairs={{0,2},{1,3},{2,0},{3,1},{4,6},{5,7},{6,4},{7,5},{8,10},{9,11},{10,... | collective-permute-start | bytes 2408456 | tf_op jit(solution)/shard_map/ppermute | solution.py:317
  97.8 14.4 %collective-permute-start.11 = (bf16[688,256]{1,0:T(8,128)(2,1)S(1)}, bf16[688,256]{1,0:T(8,128)(2,1)S(1)}, u32[]{:S(2)}, u32[]{:S(2)}) collective-permute-start(bf16[688,256]{1,0:T(8,128)(2,1)S(1)} %copy-done.20), channel_id=1, source_target_pairs={{0,8},{4,12},{8,0},{12,4},{16,24},{20,28},{24,16},{28,20},{1,9},{5... | collective-permute-start | bytes 1056776 | tf_op jit(solution)/shard_map/ppermute | solution.py:311
  98.3 26.8 %collective-permute-start.12 = (bf16[688,256]{1,0:T(8,128)(2,1)S(1)}, bf16[688,256]{1,0:T(8,128)(2,1)S(1)}, u32[]{:S(2)}, u32[]{:S(2)}) collective-permute-start(bf16[688,256]{1,0:T(8,128)(2,1)S(1)} %copy-done.19), channel_id=1, source_target_pairs={{0,16},{4,20},{8,24},{12,28},{16,0},{20,4},{24,8},{28,12},{1,17},{... | collective-permute-start | bytes 1056776 | tf_op jit(solution)/shard_map/ppermute | solution.py:311
  100.7 24.4 %collective-permute-start.13 = (bf16[688,256]{1,0:T(8,128)(2,1)S(1)}, bf16[688,256]{1,0:T(8,128)(2,1)S(1)}, u32[]{:S(2)}, u32[]{:S(2)}) collective-permute-start(bf16[688,256]{1,0:T(8,128)(2,1)S(1)} %copy-done.18), channel_id=1, source_target_pairs={{0,24},{4,28},{8,16},{12,20},{16,8},{20,12},{24,0},{28,4},{1,25},{... | collective-permute-start | bytes 1056776 | tf_op jit(solution)/shard_map/ppermute | solution.py:311
  125.1 11.1 %collective-permute-start.18 = (bf16[2,2,784,512]{3,2,1,0:T(8,128)(2,1)S(1)}, bf16[2,2,784,512]{3,2,1,0:T(8,128)(2,1)S(1)}, u32[]{:S(2)}, u32[]{:S(2)}) collective-permute-start(bf16[2,2,784,512]{3,2,1,0:T(8,128)(2,1)S(1)} %pad_maximum_fusion.1.refs_0_), channel_id=1, source_target_pairs={{0,1},{1,0},{2,3},{3,2},{4,5},{5,4},{6,7},{7,6},{8,9},{9,8},{10,11... | collective-permute-start | bytes 9633800 | tf_op jit(solution)/shard_map/ppermute | solution.py:317
  127.2 18.8 %collective-permute-start.15 = (bf16[2,2,784,512]{3,2,1,0:T(8,128)(2,1)}, bf16[2,2,784,512]{3,2,1,0:T(8,128)(2,1)}, u32[]{:S(2)}, u32[]{:S(2)}) collective-permute-start(bf16[2,2,784,512]{3,2,1,0:T(8,128)(2,1)} %pad_maximum_fusion.refs_0_), channel_id=1, source_target_pairs={{0,1},{1,0},{2,3},{3,2},{4,5},{5,4},{6,7},{7,6},{8,9},{9,8},{10,11... | collective-permute-start | bytes 9633800 | tf_op jit(solution)/shard_map/ppermute | solution.py:317
  128.8 35.0 %collective-permute-start.22 = (bf16[3,688,256]{2,1,0:T(8,128)(2,1)}, bf16[3,688,256]{2,1,0:T(8,128)(2,1)}, u32[]{:S(2)}, u32[]{:S(2)}) collective-permute-start(bf16[3,688,256]{2,1,0:T(8,128)(2,1)} %pad_maximum_fusion.3), channel_id=1, source_target_pairs={{0,4},{4,0},{8,12},{12,8},{16,20},{20,16},{24,28},{28,24},{1,5},{5... | collective-permute-start | bytes 3170312 | tf_op jit(solution)/shard_map/ppermute | solution.py:314
  130.8 24.9 %collective-permute-start.20 = (bf16[512,256]{1,0:T(8,128)(2,1)S(1)}, bf16[512,256]{1,0:T(8,128)(2,1)S(1)}, u32[]{:S(2)}, u32[]{:S(2)}) collective-permute-start(bf16[512,256]{1,0:T(8,128)(2,1)S(1)} %copy-done.21), channel_id=1, source_target_pairs={{0,16},{4,20},{8,24},{12,28},{16,0},{20,4},{24,8},{28,12},{1,17},{... | collective-permute-start | bytes 786440 | tf_op jit(solution)/shard_map/ppermute | solution.py:311
  146.0 9.6 %collective-permute-start.19 = (bf16[512,256]{1,0:T(8,128)(2,1)S(1)}, bf16[512,256]{1,0:T(8,128)(2,1)S(1)}, u32[]{:S(2)}, u32[]{:S(2)}) collective-permute-start(bf16[512,256]{1,0:T(8,128)(2,1)S(1)} %get-tuple-element.26), channel_id=1, source_target_pairs={{0,8},{4,12},{8,0},{12,4},{16,24},{20,28},{24,16},{28,20},{1,9},{5... | collective-permute-start | bytes 786440 | tf_op jit(solution)/shard_map/ppermute | solution.py:311
  154.1 9.6 %collective-permute-start.21 = (bf16[512,256]{1,0:T(8,128)(2,1)S(1)}, bf16[512,256]{1,0:T(8,128)(2,1)S(1)}, u32[]{:S(2)}, u32[]{:S(2)}) collective-permute-start(bf16[512,256]{1,0:T(8,128)(2,1)S(1)} %get-tuple-element.28), channel_id=1, source_target_pairs={{0,24},{4,28},{8,16},{12,20},{16,8},{20,12},{24,0},{28,4},{1,25},{... | collective-permute-start | bytes 786440 | tf_op jit(solution)/shard_map/ppermute | solution.py:311
  163.8 31.7 %collective-permute-start.23 = (bf16[3,512,256]{2,1,0:T(8,128)(2,1)S(1)}, bf16[3,512,256]{2,1,0:T(8,128)(2,1)S(1)}, u32[]{:S(2)}, u32[]{:S(2)}) collective-permute-start(bf16[3,512,256]{2,1,0:T(8,128)(2,1)S(1)} %pad_maximum_fusion.4), channel_id=1, source_target_pairs={{0,4},{4,0},{8,12},{12,8},{16,20},{20,16},{24,28},{28,24},{1,5},{5... | collective-permute-start | bytes 2359304 | tf_op jit(solution)/shard_map/ppermute | solution.py:314
  (31 other events, 282.4 us)

commit v6 on v5

--- a/solution.py
+++ b/solution.py
@@ -94,7 +94,11 @@
 
             @pl.when(group // each == index)
             def _():
-                pltpu.make_async_copy(source.at[group % each, split], held.at[slot], token_sems.at[slot]).start()
+                for first in range(0, held.shape[1], held.shape[1] // 4):
+                    part = pl.ds(first, held.shape[1] // 4)
+                    pltpu.make_async_copy(
+                        source.at[group % each, split, part], held.at[slot, part], token_sems.at[slot]
+                    ).start()
 
     @pl.when(live > 0)
     def _():
@@ -368,7 +372,7 @@
     back_half = both(far, last, far_across, last_across)
     back = ready(back_half, swap_part(after(back_half, *sent[1], across[0]), 1))
     tokens, ids = zip(front, back)
-    waits = (tokens[1], sent[1][1], tokens[0])
+    waits = (tokens[0], sent[1][1], sent[1][2])
     sent.append([swap_hi(after(y, *sent[1], wait), step) for step, (y, wait) in enumerate(zip(blocks[2], waits), 1)])
     across.append(swap_lo(jnp.stack(sent[1])))
     across.append(swap_lo(after(jnp.stack(sent[2]), across[1])))

time: 233 us -> 222 us (0.953)
  the two profiles are of different devices: /device:TPU:4 before, /device:TPU:0 now
where the time goes in v6:
time: 222 us; the launch traced here: 220 us
  waiting for transfers between devices  87 us (39%)
  Pallas kernels  55.6 us (25%)
  starting transfers between devices  46.4 us (21%)
  other arithmetic  15.6 us (7%)
  local copies, waits for them, and re-layouts  14.9 us (7%)
    ppermute x13, waiting for transfers between devices, swap_hi(): return lax.ppermute(x, 'dp', [(g, g ^ 2 * step) for g in range(groups)])  67.1 us
    pallas_call x2, Pallas kernels, stats(): pl.pallas_call(functools.partial(stats_kernel, plan, (len(tokens), len(id...  39.4 us
    ppermute x13, starting transfers between devices, swap_hi(): return lax.ppermute(x, 'dp', [(g, g ^ 2 * step) for g in range(groups)])  26.4 us
    ppermute x4, waiting for transfers between devices, along(): lax.ppermute(x, 'dp', [(2 * a + side, 2 * b + side) for a, b in moves for...  18 us
    pallas_call x2, Pallas kernels, assemble(): pl.pallas_call(functools.partial(assemble_kernel, len(sources) > 1), grid...  16.2 us
    ppermute x9, starting transfers between devices, swap_part(): return lax.ppermute(x, 'vocab', [(v, v ^ step) for v in range(parts)])  8.64 us
    squeeze x4, local copies, waits for them, and re-layouts, block(): lax.dynamic_slice(turned, (hi ^ step, start, 0), (1, width, depth))[0]  7.74 us
    ppermute x4, starting transfers between devices, along(): lax.ppermute(x, 'dp', [(2 * a + side, 2 * b + side) for a, b in moves for...  5.74 us
  transfers between devices with their start and end apart: 30, of which 13 were waited for; matrix products, arithmetic and copies ran while one was open for 9% of the time, Pallas kernels for 19%

profile of v6, /device:TPU:0, one launch (start us, length us, event | category | flops | bytes accessed | tf_op | source)
XLA Modules:
  0.0 220.4 jit_solution(4295406214264491582)
XLA Ops:
  1.9 3.0 %collective-permute-start.3 = (bf16[2000,256]{1,0:T(8,128)(2,1)S(1)}, bf16[2000,256]{1,0:T(8,128)(2,1)S(1)}, u32[]{:S(2)}, u32[]{:S(2)}) collective-permute-start(bf16[2000,256]{1,0:T(8,128)(2,1)S(1)} %dynamic-slice_bitcast_fusion), channel_id=1, source_target_pairs={{0,4},{4,0},{8,12},{12,8},{16,20},{20,16},{24,28},{28,24},{1,5},{5... | collective-permute-start | bytes 3072008 | tf_op jit(solution)/shard_map/ppermute | solution.py:318
  11.0 14.8 %collective-permute-done = bf16[784,512]{1,0:T(8,128)(2,1)} collective-permute-done((bf16[784,512]{1,0:T(8,128)(2,1)S(1)}, bf16[784,512]{1,0:T(8,128)(2,1)}, u32[]{:S(2)}, u32[]{:S(2)}) %collective-permute-start) | collective-permute-done | bytes 802848 | tf_op jit(solution)/shard_map/ppermute | solution.py:315
  31.1 2.0 dynamic-slice_bitcast_fusion.7
  33.2 2.2 %dynamic-slice_bitcast_fusion.4 = (bf16[688,256]{1,0:T(8,128)(2,1)}, bf16[688,256]{1,0:T(8,128)(2,1)}, bf16[688,256]{1,0:T(8,128)(2,1)}) fusion(bf16[4,2000,256]{2,1,0:T(8,128)(2,1)} %bitcast.105, s32[]{:T(128)S(6)} %select_n.55, s32[]{:T(128)S(6)} %select_n.54, s32[]{:T(128)S(6)} %select_n.53), kind=kLoop, calls=%fused_computation.18 | loop fusion | bytes 2113548 | tf_op jit(solution)/shard_map/squeeze | solution.py:338
  35.4 2.2 %dynamic-slice_bitcast_fusion.1 = (bf16[800,256]{1,0:T(8,128)(2,1)S(1)}, bf16[800,256]{1,0:T(8,128)(2,1)}, bf16[800,256]{1,0:T(8,128)(2,1)}) fusion(bf16[4,2000,256]{2,1,0:T(8,128)(2,1)} %bitcast.106, s32[]{:T(128)S(6)} %select_n.55, s32[]{:T(128)S(6)} %select_n.54, s32[]{:T(128)S(6)} %select_n.53), kind=kLoop, calls=%fused_computation.15 | loop fusion | bytes 2457612 | tf_op jit(solution)/shard_map/squeeze | solution.py:338
  37.6 11.3 %collective-permute-done.5 = bf16[784,512]{1,0:T(8,128)(2,1)} collective-permute-done((bf16[784,512]{1,0:T(8,128)(2,1)}, bf16[784,512]{1,0:T(8,128)(2,1)}, u32[]{:S(2)}, u32[]{:S(2)}) %collective-permute-start.5) | collective-permute-done | bytes 802848 | tf_op jit(solution)/shard_map/ppermute | solution.py:324
  48.9 3.5 %collective-permute-start.7 = (bf16[800,256]{1,0:T(8,128)(2,1)}, bf16[800,256]{1,0:T(8,128)(2,1)S(1)}, u32[]{:S(2)}, u32[]{:S(2)}) collective-permute-start(bf16[800,256]{1,0:T(8,128)(2,1)} %get-tuple-element.17), channel_id=1, source_target_pairs={{0,8},{4,12},{8,0},{12,4},{16,24},{20,28},{24,16},{28,20},{1,9},{5... | collective-permute-start | bytes 1228808 | tf_op jit(solution)/shard_map/ppermute | solution.py:315
  59.2 11.6 %collective-permute-done.7.refs_6_ = bf16[800,256]{1,0:T(8,128)(2,1)S(1)} collective-permute-done((bf16[800,256]{1,0:T(8,128)(2,1)}, bf16[800,256]{1,0:T(8,128)(2,1)S(1)}, u32[]{:S(2)}, u32[]{:S(2)}) %collective-permute-start.7) | collective-permute-done | bytes 409632 | tf_op jit(solution)/shard_map/ppermute | solution.py:315
  70.8 12.6 %collective-permute-done.8.refs_7_ = bf16[800,256]{1,0:T(8,128)(2,1)S(1)} collective-permute-done((bf16[800,256]{1,0:T(8,128)(2,1)}, bf16[800,256]{1,0:T(8,128)(2,1)S(1)}, u32[]{:S(2)}, u32[]{:S(2)}) %collective-permute-start.8) | collective-permute-done | bytes 409632 | tf_op jit(solution)/shard_map/ppermute | solution.py:315
  86.8 5.5 %collective-permute-start.11 = (bf16[688,256]{1,0:T(8,128)(2,1)S(1)}, bf16[688,256]{1,0:T(8,128)(2,1)S(1)}, u32[]{:S(2)}, u32[]{:S(2)}) collective-permute-start(bf16[688,256]{1,0:T(8,128)(2,1)S(1)} %copy-done.17), channel_id=1, source_target_pairs={{0,8},{4,12},{8,0},{12,4},{16,24},{20,28},{24,16},{28,20},{1,9},{5... | collective-permute-start | bytes 1056776 | tf_op jit(solution)/shard_map/ppermute | solution.py:315
  92.4 1.7 collective-permute-start.12
  95.2 6.7 %collective-permute-done.16 = bf16[784,512]{1,0:T(8,128)(2,1)S(1)} collective-permute-done((bf16[784,512]{1,0:T(8,128)(2,1)}, bf16[784,512]{1,0:T(8,128)(2,1)S(1)}, u32[]{:S(2)}, u32[]{:S(2)}) %collective-permute-start.16) | collective-permute-done | bytes 802848 | tf_op jit(solution)/shard_map/ppermute | solution.py:324
  103.9 11.7 %collective-permute-done.11.refs_10_ = bf16[688,256]{1,0:T(8,128)(2,1)S(1)} collective-permute-done((bf16[688,256]{1,0:T(8,128)(2,1)S(1)}, bf16[688,256]{1,0:T(8,128)(2,1)S(1)}, u32[]{:S(2)}, u32[]{:S(2)}) %collective-permute-start.11) | collective-permute-done | bytes 352288 | tf_op jit(solution)/shard_map/ppermute | solution.py:315
  115.6 2.5 %collective-permute-done.12.refs_11_ = bf16[688,256]{1,0:T(8,128)(2,1)S(1)} collective-permute-done((bf16[688,256]{1,0:T(8,128)(2,1)S(1)}, bf16[688,256]{1,0:T(8,128)(2,1)S(1)}, u32[]{:S(2)}, u32[]{:S(2)}) %collective-permute-start.12) | collective-permute-done | bytes 352288 | tf_op jit(solution)/shard_map/ppermute | solution.py:315
  123.9 5.7 %collective-permute-start.20 = (bf16[512,256]{1,0:T(8,128)(2,1)}, bf16[512,256]{1,0:T(8,128)(2,1)S(1)}, u32[]{:S(2)}, u32[]{:S(2)}) collective-permute-start(bf16[512,256]{1,0:T(8,128)(2,1)} %get-tuple-element.27), channel_id=1, source_target_pairs={{0,16},{4,20},{8,24},{12,28},{16,0},{20,4},{24,8},{28,12},{1,17},{... | collective-permute-start | bytes 786440 | tf_op jit(solution)/shard_map/ppermute | solution.py:315
  132.2 8.1 %shard_map.77.refs_0_ = bf16[2,3,2048,256]{3,2,1,0:T(8,128)(2,1)} custom-call(f32[1,2048]{1,0:T(1,128)} %bitcast.122, bf16[2,2,784,512]{3,2,1,0:T(8,128)(2,1)} %copy-done.1, bf16[2,2,784,512]{3,2,1,0:T(8,128)(2,1)} %copy-done.5), custom_call_target="tpu_custom_call" | custom-call | flops 18874368 | bytes 12582912 | tf_op jit(solution)/shard_map/pallas_call | solution.py:43
  141.1 6.9 %collective-permute-done.20.refs_7_ = bf16[512,256]{1,0:T(8,128)(2,1)S(1)} collective-permute-done((bf16[512,256]{1,0:T(8,128)(2,1)}, bf16[512,256]{1,0:T(8,128)(2,1)S(1)}, u32[]{:S(2)}, u32[]{:S(2)}) %collective-permute-start.20) | collective-permute-done | bytes 262176 | tf_op jit(solution)/shard_map/ppermute | solution.py:315
  148.0 5.0 %collective-permute-done.19.refs_6_ = bf16[512,256]{1,0:T(8,128)(2,1)} collective-permute-done((bf16[512,256]{1,0:T(8,128)(2,1)}, bf16[512,256]{1,0:T(8,128)(2,1)}, u32[]{:S(2)}, u32[]{:S(2)}) %collective-permute-start.19) | collective-permute-done | bytes 262176 | tf_op jit(solution)/shard_map/ppermute | solution.py:315
  153.0 2.0 pad_maximum_fusion.4
  157.6 8.1 %shard_map.78.refs_1_ = bf16[2,3,2048,256]{3,2,1,0:T(8,128)(2,1)} custom-call(f32[1,2048]{1,0:T(1,128)} %bitcast.123, bf16[2,2,784,512]{3,2,1,0:T(8,128)(2,1)} %copy-done, bf16[2,2,784,512]{3,2,1,0:T(8,128)(2,1)} %collective-permute-done.18.refs_1_), custom_call_target="tpu_custom_call" | custom-call | flops 18874368 | bytes 12582912 | tf_op jit(solution)/shard_map/pallas_call | solution.py:43
  165.7 25.4 %shard_map.79.refs_10_ = f32[4,4,768]{2,1,0:T(4,128)} custom-call(s32[1]{0:T(128)} %constant.14.clone.1.start_ref, s32[16]{0:T(128)} %lens_ref.3, s32[16]{0:T(128)} %owner_ref.3, bf16[2,3,2048,256]{3,2,1,0:T(8,128)(2,1)} %shard_map.77.refs_0_, bf16[2,3,2048,256]{3,2,1,0:T(8,128)(2,1)} %shard_map.78.refs_1_, s32[6,1,256]{2,1,0:T(1,128)} %get-tuple-element.85.refs_2_, ...), custom_call_target="tpu_custom_call" | custom-call | flops 1170210816 | bytes 3047424 | tf_op jit(solution)/shard_map/pallas_call | solution.py:161
  191.2 13.9 %shard_map.80 = f32[4,4,768]{2,1,0:T(4,128)} custom-call(s32[1]{0:T(128)} %constant.14.clone.1.start_ref, s32[16]{0:T(128)} %lens_ref.3, s32[16]{0:T(128)} %owner_ref.3, bf16[2,3,2048,256]{3,2,1,0:T(8,128)(2,1)} %shard_map.77.refs_0_, bf16[2,3,2048,256]{3,2,1,0:T(8,128)(2,1)} %shard_map.78.refs_1_, s32[6,1,256]{2,1,0:T(1,128)} %get-tuple-element.85.refs_2_, ...), custom_call_target="tpu_custom_call" | custom-call | flops 402653184 | bytes 1048576 | tf_op jit(solution)/shard_map/pallas_call | solution.py:161
  207.4 2.0 collective-permute-start.25
  210.2 1.7 collective-permute-done.26
  (123 shorter events, 49.1 us)
Async XLA Ops:
  1.9 26.8 %collective-permute-start.3 = (bf16[2000,256]{1,0:T(8,128)(2,1)S(1)}, bf16[2000,256]{1,0:T(8,128)(2,1)S(1)}, u32[]{:S(2)}, u32[]{:S(2)}) collective-permute-start(bf16[2000,256]{1,0:T(8,128)(2,1)S(1)} %dynamic-slice_bitcast_fusion), channel_id=1, source_target_pairs={{0,4},{4,0},{8,12},{12,8},{16,20},{20,16},{24,28},{28,24},{1,5},{5... | collective-permute-start | bytes 3072008 | tf_op jit(solution)/shard_map/ppermute | solution.py:318
  6.3 19.5 %collective-permute-start = (bf16[784,512]{1,0:T(8,128)(2,1)S(1)}, bf16[784,512]{1,0:T(8,128)(2,1)}, u32[]{:S(2)}, u32[]{:S(2)}) collective-permute-start(bf16[784,512]{1,0:T(8,128)(2,1)S(1)} %get-tuple-element.70), channel_id=1, source_target_pairs={{0,8},{4,12},{8,0},{12,4},{16,24},{20,28},{24,16},{28,20},{1,9},{5... | collective-permute-start | bytes 2408456 | tf_op jit(solution)/shard_map/ppermute | solution.py:315
  7.9 19.5 %collective-permute-start.2 = (bf16[784,512]{1,0:T(8,128)(2,1)S(1)}, bf16[784,512]{1,0:T(8,128)(2,1)}, u32[]{:S(2)}, u32[]{:S(2)}) collective-permute-start(bf16[784,512]{1,0:T(8,128)(2,1)S(1)} %get-tuple-element.70), channel_id=1, source_target_pairs={{8,16},{12,20},{16,8},{20,12},{9,17},{13,21},{17,9},{21,13},{10,18... | collective-permute-start | bytes 2408456 | tf_op jit(solution)/shard_map/ppermute | solution.py:324
  9.5 19.2 %collective-permute-start.1 = (bf16[784,512]{1,0:T(8,128)(2,1)S(1)}, bf16[784,512]{1,0:T(8,128)(2,1)S(1)}, u32[]{:S(2)}, u32[]{:S(2)}) collective-permute-start(bf16[784,512]{1,0:T(8,128)(2,1)S(1)} %get-tuple-element.70), channel_id=1, source_target_pairs={{0,2},{1,3},{2,0},{3,1},{4,6},{5,7},{6,4},{7,5},{8,10},{9,11},{10,... | collective-permute-start | bytes 2408456 | tf_op jit(solution)/shard_map/ppermute | solution.py:321
  25.8 11.8 %collective-permute-start.6 = (bf16[784,512]{1,0:T(8,128)(2,1)}, bf16[784,512]{1,0:T(8,128)(2,1)}, u32[]{:S(2)}, u32[]{:S(2)}) collective-permute-start(bf16[784,512]{1,0:T(8,128)(2,1)} %collective-permute-done), channel_id=1, source_target_pairs={{8,16},{12,20},{16,8},{20,12},{9,17},{13,21},{17,9},{21,13},{10,18... | collective-permute-start | bytes 2408456 | tf_op jit(solution)/shard_map/ppermute | solution.py:324
  27.4 21.5 %collective-permute-start.5 = (bf16[784,512]{1,0:T(8,128)(2,1)}, bf16[784,512]{1,0:T(8,128)(2,1)}, u32[]{:S(2)}, u32[]{:S(2)}) collective-permute-start(bf16[784,512]{1,0:T(8,128)(2,1)} %collective-permute-done.2), channel_id=1, source_target_pairs={{8,0},{12,4},{16,24},{20,28},{9,1},{13,5},{17,25},{21,29},{10,2},{... | collective-permute-start | bytes 2408456 | tf_op jit(solution)/shard_map/ppermute | solution.py:324
  29.6 19.3 %collective-permute-start.4 = (bf16[784,512]{1,0:T(8,128)(2,1)}, bf16[784,512]{1,0:T(8,128)(2,1)S(1)}, u32[]{:S(2)}, u32[]{:S(2)}) collective-permute-start(bf16[784,512]{1,0:T(8,128)(2,1)} %collective-permute-done), channel_id=1, source_target_pairs={{0,2},{1,3},{2,0},{3,1},{4,6},{5,7},{6,4},{7,5},{8,10},{9,11},{10,... | collective-permute-start | bytes 2408456 | tf_op jit(solution)/shard_map/ppermute | solution.py:321
  48.9 21.9 %collective-permute-start.7 = (bf16[800,256]{1,0:T(8,128)(2,1)}, bf16[800,256]{1,0:T(8,128)(2,1)S(1)}, u32[]{:S(2)}, u32[]{:S(2)}) collective-permute-start(bf16[800,256]{1,0:T(8,128)(2,1)} %get-tuple-element.17), channel_id=1, source_target_pairs={{0,8},{4,12},{8,0},{12,4},{16,24},{20,28},{24,16},{28,20},{1,9},{5... | collective-permute-start | bytes 1228808 | tf_op jit(solution)/shard_map/ppermute | solution.py:315
  52.3 31.1 %collective-permute-start.8 = (bf16[800,256]{1,0:T(8,128)(2,1)}, bf16[800,256]{1,0:T(8,128)(2,1)S(1)}, u32[]{:S(2)}, u32[]{:S(2)}) collective-permute-start(bf16[800,256]{1,0:T(8,128)(2,1)} %get-tuple-element.18), channel_id=1, source_target_pairs={{0,16},{4,20},{8,24},{12,28},{16,0},{20,4},{24,8},{28,12},{1,17},{... | collective-permute-start | bytes 1228808 | tf_op jit(solution)/shard_map/ppermute | solution.py:315
  53.7 29.8 %collective-permute-start.9 = (bf16[800,256]{1,0:T(8,128)(2,1)S(1)}, bf16[800,256]{1,0:T(8,128)(2,1)S(1)}, u32[]{:S(2)}, u32[]{:S(2)}) collective-permute-start(bf16[800,256]{1,0:T(8,128)(2,1)S(1)} %get-tuple-element.19), channel_id=1, source_target_pairs={{0,24},{4,28},{8,16},{12,20},{16,8},{20,12},{24,0},{28,4},{1,25},{... | collective-permute-start | bytes 1228808 | tf_op jit(solution)/shard_map/ppermute | solution.py:315
  56.4 29.4 %collective-permute-start.10 = (bf16[784,512]{1,0:T(8,128)(2,1)S(1)}, bf16[784,512]{1,0:T(8,128)(2,1)S(1)}, u32[]{:S(2)}, u32[]{:S(2)}) collective-permute-start(bf16[784,512]{1,0:T(8,128)(2,1)S(1)} %broadcast_select_fusion.1), channel_id=1, source_target_pairs={{0,2},{1,3},{2,0},{3,1},{4,6},{5,7},{6,4},{7,5},{8,10},{9,11},{10,... | collective-permute-start | bytes 2408456 | tf_op jit(solution)/shard_map/ppermute | solution.py:321
  57.9 44.0 %collective-permute-start.16 = (bf16[784,512]{1,0:T(8,128)(2,1)}, bf16[784,512]{1,0:T(8,128)(2,1)S(1)}, u32[]{:S(2)}, u32[]{:S(2)}) collective-permute-start(bf16[784,512]{1,0:T(8,128)(2,1)} %collective-permute-done.6), channel_id=1, source_target_pairs={{8,0},{12,4},{16,24},{20,28},{9,1},{13,5},{17,25},{21,29},{10,2},{... | collective-permute-start | bytes 2408456 | tf_op jit(solution)/shard_map/ppermute | solution.py:324
  83.6 34.5 %collective-permute-start.14 = (bf16[3,800,256]{2,1,0:T(8,128)(2,1)S(1)}, bf16[3,800,256]{2,1,0:T(8,128)(2,1)}, u32[]{:S(2)}, u32[]{:S(2)}) collective-permute-start(bf16[3,800,256]{2,1,0:T(8,128)(2,1)S(1)} %pad_maximum_fusion.2), channel_id=1, source_target_pairs={{0,4},{4,0},{8,12},{12,8},{16,20},{20,16},{24,28},{28,24},{1,5},{5... | collective-permute-start | bytes 3686408 | tf_op jit(solution)/shard_map/ppermute | solution.py:318
  86.8 28.8 %collective-permute-start.11 = (bf16[688,256]{1,0:T(8,128)(2,1)S(1)}, bf16[688,256]{1,0:T(8,128)(2,1)S(1)}, u32[]{:S(2)}, u32[]{:S(2)}) collective-permute-start(bf16[688,256]{1,0:T(8,128)(2,1)S(1)} %copy-done.17), channel_id=1, source_target_pairs={{0,8},{4,12},{8,0},{12,4},{16,24},{20,28},{24,16},{28,20},{1,9},{5... | collective-permute-start | bytes 1056776 | tf_op jit(solution)/shard_map/ppermute | solution.py:315
  92.4 25.7 %collective-permute-start.12 = (bf16[688,256]{1,0:T(8,128)(2,1)S(1)}, bf16[688,256]{1,0:T(8,128)(2,1)S(1)}, u32[]{:S(2)}, u32[]{:S(2)}) collective-permute-start(bf16[688,256]{1,0:T(8,128)(2,1)S(1)} %copy-done.16), channel_id=1, source_target_pairs={{0,16},{4,20},{8,24},{12,28},{16,0},{20,4},{24,8},{28,12},{1,17},{... | collective-permute-start | bytes 1056776 | tf_op jit(solution)/shard_map/ppermute | solution.py:315
  94.1 24.0 %collective-permute-start.13 = (bf16[688,256]{1,0:T(8,128)(2,1)S(1)}, bf16[688,256]{1,0:T(8,128)(2,1)S(1)}, u32[]{:S(2)}, u32[]{:S(2)}) collective-permute-start(bf16[688,256]{1,0:T(8,128)(2,1)S(1)} %copy-done.15), channel_id=1, source_target_pairs={{0,24},{4,28},{8,16},{12,20},{16,8},{20,12},{24,0},{28,4},{1,25},{... | collective-permute-start | bytes 1056776 | tf_op jit(solution)/shard_map/ppermute | solution.py:315
  102.0 16.3 %collective-permute-start.17 = (bf16[784,512]{1,0:T(8,128)(2,1)S(1)}, bf16[784,512]{1,0:T(8,128)(2,1)S(1)}, u32[]{:S(2)}, u32[]{:S(2)}) collective-permute-start(bf16[784,512]{1,0:T(8,128)(2,1)S(1)} %broadcast_select_fusion), channel_id=1, source_target_pairs={{0,2},{1,3},{2,0},{3,1},{4,6},{5,7},{6,4},{7,5},{8,10},{9,11},{10,... | collective-permute-start | bytes 2408456 | tf_op jit(solution)/shard_map/ppermute | solution.py:321
  118.1 12.5 %collective-permute-start.15 = (bf16[2,2,784,512]{3,2,1,0:T(8,128)(2,1)S(1)}, bf16[2,2,784,512]{3,2,1,0:T(8,128)(2,1)S(1)}, u32[]{:S(2)}, u32[]{:S(2)}) collective-permute-start(bf16[2,2,784,512]{3,2,1,0:T(8,128)(2,1)S(1)} %pad_maximum_fusion.refs_0_), channel_id=1, source_target_pairs={{0,1},{1,0},{2,3},{3,2},{4,5},{5,4},{6,7},{7,6},{8,9},{9,8},{10,11... | collective-permute-start | bytes 9633800 | tf_op jit(solution)/shard_map/ppermute | solution.py:321
  119.9 37.8 %collective-permute-start.18 = (bf16[2,2,784,512]{3,2,1,0:T(8,128)(2,1)S(1)}, bf16[2,2,784,512]{3,2,1,0:T(8,128)(2,1)}, u32[]{:S(2)}, u32[]{:S(2)}) collective-permute-start(bf16[2,2,784,512]{3,2,1,0:T(8,128)(2,1)S(1)} %pad_maximum_fusion.1.refs_0_), channel_id=1, source_target_pairs={{0,1},{1,0},{2,3},{3,2},{4,5},{5,4},{6,7},{7,6},{8,9},{9,8},{10,11... | collective-permute-start | bytes 9633800 | tf_op jit(solution)/shard_map/ppermute | solution.py:321
  121.8 33.2 %collective-permute-start.22 = (bf16[3,688,256]{2,1,0:T(8,128)(2,1)}, bf16[3,688,256]{2,1,0:T(8,128)(2,1)}, u32[]{:S(2)}, u32[]{:S(2)}) collective-permute-start(bf16[3,688,256]{2,1,0:T(8,128)(2,1)} %pad_maximum_fusion.3), channel_id=1, source_target_pairs={{0,4},{4,0},{8,12},{12,8},{16,20},{20,16},{24,28},{28,24},{1,5},{5... | collective-permute-start | bytes 3170312 | tf_op jit(solution)/shard_map/ppermute | solution.py:318
  123.9 24.1 %collective-permute-start.20 = (bf16[512,256]{1,0:T(8,128)(2,1)}, bf16[512,256]{1,0:T(8,128)(2,1)S(1)}, u32[]{:S(2)}, u32[]{:S(2)}) collective-permute-start(bf16[512,256]{1,0:T(8,128)(2,1)} %get-tuple-element.27), channel_id=1, source_target_pairs={{0,16},{4,20},{8,24},{12,28},{16,0},{20,4},{24,8},{28,12},{1,17},{... | collective-permute-start | bytes 786440 | tf_op jit(solution)/shard_map/ppermute | solution.py:315
  129.7 18.3 %collective-permute-start.21 = (bf16[512,256]{1,0:T(8,128)(2,1)}, bf16[512,256]{1,0:T(8,128)(2,1)}, u32[]{:S(2)}, u32[]{:S(2)}) collective-permute-start(bf16[512,256]{1,0:T(8,128)(2,1)} %get-tuple-element.28), channel_id=1, source_target_pairs={{0,24},{4,28},{8,16},{12,20},{16,8},{20,12},{24,0},{28,4},{1,25},{... | collective-permute-start | bytes 786440 | tf_op jit(solution)/shard_map/ppermute | solution.py:315
  140.4 12.6 %collective-permute-start.19 = (bf16[512,256]{1,0:T(8,128)(2,1)}, bf16[512,256]{1,0:T(8,128)(2,1)}, u32[]{:S(2)}, u32[]{:S(2)}) collective-permute-start(bf16[512,256]{1,0:T(8,128)(2,1)} %get-tuple-element.26), channel_id=1, source_target_pairs={{0,8},{4,12},{8,0},{12,4},{16,24},{20,28},{24,16},{28,20},{1,9},{5... | collective-permute-start | bytes 786440 | tf_op jit(solution)/shard_map/ppermute | solution.py:315
  155.0 36.2 %collective-permute-start.23 = (bf16[3,512,256]{2,1,0:T(8,128)(2,1)}, bf16[3,512,256]{2,1,0:T(8,128)(2,1)}, u32[]{:S(2)}, u32[]{:S(2)}) collective-permute-start(bf16[3,512,256]{2,1,0:T(8,128)(2,1)} %pad_maximum_fusion.4), channel_id=1, source_target_pairs={{0,4},{4,0},{8,12},{12,8},{16,20},{20,16},{24,28},{28,24},{1,5},{5... | collective-permute-start | bytes 2359304 | tf_op jit(solution)/shard_map/ppermute | solution.py:318
  (28 other events, 174.7 us)

commit v7 on v6

--- a/solution.py
+++ b/solution.py
@@ -372,8 +372,8 @@
     back_half = both(far, last, far_across, last_across)
     back = ready(back_half, swap_part(after(back_half, *sent[1], across[0]), 1))
     tokens, ids = zip(front, back)
-    waits = (tokens[0], sent[1][1], sent[1][2])
-    sent.append([swap_hi(after(y, *sent[1], wait), step) for step, (y, wait) in enumerate(zip(blocks[2], waits), 1)])
+    waits = (tokens, [], [])
+    sent.append([swap_hi(after(y, *sent[1], *wait), step) for step, (y, wait) in enumerate(zip(blocks[2], waits), 1)])
     across.append(swap_lo(jnp.stack(sent[1])))
     across.append(swap_lo(after(jnp.stack(sent[2]), across[1])))
     found = score((2,), [score((0, 1), [])])

time: 222 us -> 226 us (1.018)
  the two profiles are of different devices: /device:TPU:0 before, /device:TPU:4 now
where the time goes in v7:
time: 226 us; the launch traced here: 223 us
  waiting for transfers between devices  93.5 us (41%)
  Pallas kernels  55.6 us (25%)
  starting transfers between devices  41 us (18%)
  local copies, waits for them, and re-layouts  16.3 us (7%)
  other arithmetic  15.7 us (7%)
    ppermute x13, waiting for transfers between devices, swap_hi(): return lax.ppermute(x, 'dp', [(g, g ^ 2 * step) for g in range(groups)])  69.3 us
    pallas_call x2, Pallas kernels, stats(): pl.pallas_call(functools.partial(stats_kernel, plan, (len(tokens), len(id...  39.4 us
    ppermute x13, starting transfers between devices, swap_hi(): return lax.ppermute(x, 'dp', [(g, g ^ 2 * step) for g in range(groups)])  22.9 us
    pallas_call x2, Pallas kernels, assemble(): pl.pallas_call(functools.partial(assemble_kernel, len(sources) > 1), grid...  16.2 us
    ppermute x9, waiting for transfers between devices, swap_part(): return lax.ppermute(x, 'vocab', [(v, v ^ step) for v in range(parts)])  13.4 us
    ppermute x9, starting transfers between devices, swap_part(): return lax.ppermute(x, 'vocab', [(v, v ^ step) for v in range(parts)])  8.57 us
    ppermute x4, waiting for transfers between devices, along(): lax.ppermute(x, 'dp', [(2 * a + side, 2 * b + side) for a, b in moves for...  7.91 us
    squeeze x4, local copies, waits for them, and re-layouts, block(): lax.dynamic_slice(turned, (hi ^ step, start, 0), (1, width, depth))[0]  7.66 us
  transfers between devices with their start and end apart: 30, of which 14 were waited for; matrix products, arithmetic and copies ran while one was open for 8% of the time, Pallas kernels for 19%

profile of v7, /device:TPU:4, one launch (start us, length us, event | category | flops | bytes accessed | tf_op | source)
XLA Modules:
  0.0 223.1 jit_solution(12609039632629914359)
XLA Ops:
  2.6 1.6 collective-permute-start
  6.1 1.6 collective-permute-start.2
  9.2 13.1 %collective-permute-done = bf16[784,512]{1,0:T(8,128)(2,1)S(1)} collective-permute-done((bf16[784,512]{1,0:T(8,128)(2,1)S(1)}, bf16[784,512]{1,0:T(8,128)(2,1)S(1)}, u32[]{:S(2)}, u32[]{:S(2)}) %collective-permute-start) | collective-permute-done | bytes 802848 | tf_op jit(solution)/shard_map/ppermute | solution.py:315
  22.3 1.6 collective-permute-start.6
  25.2 1.6 collective-permute-done.1
  26.8 3.0 %collective-permute-done.3.refs_5_ = bf16[2000,256]{1,0:T(8,128)(2,1)} collective-permute-done((bf16[2000,256]{1,0:T(8,128)(2,1)S(1)}, bf16[2000,256]{1,0:T(8,128)(2,1)}, u32[]{:S(2)}, u32[]{:S(2)}) %collective-permute-start.3) | collective-permute-done | bytes 1024032 | tf_op jit(solution)/shard_map/ppermute | solution.py:318
  31.3 2.2 %dynamic-slice_bitcast_fusion.4 = (bf16[688,256]{1,0:T(8,128)(2,1)}, bf16[688,256]{1,0:T(8,128)(2,1)}, bf16[688,256]{1,0:T(8,128)(2,1)}) fusion(bf16[4,2000,256]{2,1,0:T(8,128)(2,1)} %bitcast.104, s32[]{:T(128)S(6)} %select_n.55, s32[]{:T(128)S(6)} %select_n.54, s32[]{:T(128)S(6)} %select_n.53), kind=kLoop, calls=%fused_computation.18 | loop fusion | bytes 2113548 | tf_op jit(solution)/shard_map/squeeze | solution.py:338
  34.8 1.9 dynamic-slice_bitcast_fusion.7
  36.7 2.3 %dynamic-slice_bitcast_fusion.1 = (bf16[800,256]{1,0:T(8,128)(2,1)}, bf16[800,256]{1,0:T(8,128)(2,1)}, bf16[800,256]{1,0:T(8,128)(2,1)}) fusion(bf16[4,2000,256]{2,1,0:T(8,128)(2,1)} %bitcast.106, s32[]{:T(128)S(6)} %select_n.55, s32[]{:T(128)S(6)} %select_n.54, s32[]{:T(128)S(6)} %select_n.53), kind=kLoop, calls=%fused_computation.15 | loop fusion | bytes 2457612 | tf_op jit(solution)/shard_map/squeeze | solution.py:338
  39.0 7.9 %collective-permute-done.5 = bf16[784,512]{1,0:T(8,128)(2,1)} collective-permute-done((bf16[784,512]{1,0:T(8,128)(2,1)}, bf16[784,512]{1,0:T(8,128)(2,1)}, u32[]{:S(2)}, u32[]{:S(2)}) %collective-permute-start.5) | collective-permute-done | bytes 802848 | tf_op jit(solution)/shard_map/ppermute | solution.py:324
  49.1 3.9 %collective-permute-start.7 = (bf16[800,256]{1,0:T(8,128)(2,1)}, bf16[800,256]{1,0:T(8,128)(2,1)S(1)}, u32[]{:S(2)}, u32[]{:S(2)}) collective-permute-start(bf16[800,256]{1,0:T(8,128)(2,1)} %get-tuple-element.17), channel_id=1, source_target_pairs={{0,8},{4,12},{8,0},{12,4},{16,24},{20,28},{24,16},{28,20},{1,9},{5... | collective-permute-start | bytes 1228808 | tf_op jit(solution)/shard_map/ppermute | solution.py:315
  58.4 32.4 %collective-permute-done.7.refs_6_ = bf16[800,256]{1,0:T(8,128)(2,1)S(1)} collective-permute-done((bf16[800,256]{1,0:T(8,128)(2,1)}, bf16[800,256]{1,0:T(8,128)(2,1)S(1)}, u32[]{:S(2)}, u32[]{:S(2)}) %collective-permute-start.7) | collective-permute-done | bytes 409632 | tf_op jit(solution)/shard_map/ppermute | solution.py:315
  98.3 2.4 %collective-permute-start.12 = (bf16[688,256]{1,0:T(8,128)(2,1)S(1)}, bf16[688,256]{1,0:T(8,128)(2,1)S(1)}, u32[]{:S(2)}, u32[]{:S(2)}) collective-permute-start(bf16[688,256]{1,0:T(8,128)(2,1)S(1)} %copy-done.19), channel_id=1, source_target_pairs={{0,16},{4,20},{8,24},{12,28},{16,0},{20,4},{24,8},{28,12},{1,17},{... | collective-permute-start | bytes 1056776 | tf_op jit(solution)/shard_map/ppermute | solution.py:315
  102.4 8.5 %collective-permute-done.17 = bf16[784,512]{1,0:T(8,128)(2,1)S(1)} collective-permute-done((bf16[784,512]{1,0:T(8,128)(2,1)S(1)}, bf16[784,512]{1,0:T(8,128)(2,1)S(1)}, u32[]{:S(2)}, u32[]{:S(2)}) %collective-permute-start.17) | collective-permute-done | bytes 802848 | tf_op jit(solution)/shard_map/ppermute | solution.py:321
  112.3 12.8 %collective-permute-done.12.refs_11_ = bf16[688,256]{1,0:T(8,128)(2,1)S(1)} collective-permute-done((bf16[688,256]{1,0:T(8,128)(2,1)S(1)}, bf16[688,256]{1,0:T(8,128)(2,1)S(1)}, u32[]{:S(2)}, u32[]{:S(2)}) %collective-permute-start.12) | collective-permute-done | bytes 352288 | tf_op jit(solution)/shard_map/ppermute | solution.py:315
  125.2 2.0 pad_maximum_fusion.refs_0_
  130.8 5.4 %collective-permute-start.20 = (bf16[512,256]{1,0:T(8,128)(2,1)S(1)}, bf16[512,256]{1,0:T(8,128)(2,1)S(1)}, u32[]{:S(2)}, u32[]{:S(2)}) collective-permute-start(bf16[512,256]{1,0:T(8,128)(2,1)S(1)} %copy-done.21), channel_id=1, source_target_pairs={{0,16},{4,20},{8,24},{12,28},{16,0},{20,4},{24,8},{28,12},{1,17},{... | collective-permute-start | bytes 786440 | tf_op jit(solution)/shard_map/ppermute | solution.py:315
  137.7 1.7 copy-done.3
  139.4 8.1 %shard_map.78.refs_1_ = bf16[2,3,2048,256]{3,2,1,0:T(8,128)(2,1)} custom-call(f32[1,2048]{1,0:T(1,128)} %bitcast.125, bf16[2,2,784,512]{3,2,1,0:T(8,128)(2,1)} %copy-done, bf16[2,2,784,512]{3,2,1,0:T(8,128)(2,1)} %copy-done.3), custom_call_target="tpu_custom_call" | custom-call | flops 18874368 | bytes 12582912 | tf_op jit(solution)/shard_map/pallas_call | solution.py:43
  147.5 8.1 %shard_map.77.refs_0_ = bf16[2,3,2048,256]{3,2,1,0:T(8,128)(2,1)} custom-call(f32[1,2048]{1,0:T(1,128)} %bitcast.126, bf16[2,2,784,512]{3,2,1,0:T(8,128)(2,1)} %pad_maximum_fusion.refs_0_, bf16[2,2,784,512]{3,2,1,0:T(8,128)(2,1)} %collective-permute-done.15.refs_1_), custom_call_target="tpu_custom_call" | custom-call | flops 18874368 | bytes 12582912 | tf_op jit(solution)/shard_map/pallas_call | solution.py:43
  155.6 7.4 %collective-permute-done.19.refs_6_ = bf16[512,256]{1,0:T(8,128)(2,1)S(1)} collective-permute-done((bf16[512,256]{1,0:T(8,128)(2,1)S(1)}, bf16[512,256]{1,0:T(8,128)(2,1)S(1)}, u32[]{:S(2)}, u32[]{:S(2)}) %collective-permute-start.19) | collective-permute-done | bytes 262176 | tf_op jit(solution)/shard_map/ppermute | solution.py:315
  166.6 25.4 %shard_map.79.refs_10_ = f32[4,4,768]{2,1,0:T(4,128)} custom-call(s32[1]{0:T(128)} %constant.14.clone.1.start_ref, s32[16]{0:T(128)} %lens_ref.3, s32[16]{0:T(128)} %owner_ref.3, bf16[2,3,2048,256]{3,2,1,0:T(8,128)(2,1)} %shard_map.77.refs_0_, bf16[2,3,2048,256]{3,2,1,0:T(8,128)(2,1)} %shard_map.78.refs_1_, s32[6,1,256]{2,1,0:T(1,128)} %get-tuple-element.85.refs_2_, ...), custom_call_target="tpu_custom_call" | custom-call | flops 1170210816 | bytes 3047424 | tf_op jit(solution)/shard_map/pallas_call | solution.py:161
  193.0 13.9 %shard_map.80 = f32[4,4,768]{2,1,0:T(4,128)} custom-call(s32[1]{0:T(128)} %constant.14.clone.1.start_ref, s32[16]{0:T(128)} %lens_ref.3, s32[16]{0:T(128)} %owner_ref.3, bf16[2,3,2048,256]{3,2,1,0:T(8,128)(2,1)} %shard_map.77.refs_0_, bf16[2,3,2048,256]{3,2,1,0:T(8,128)(2,1)} %shard_map.78.refs_1_, s32[6,1,256]{2,1,0:T(1,128)} %get-tuple-element.85.refs_2_, ...), custom_call_target="tpu_custom_call" | custom-call | flops 402653184 | bytes 1048576 | tf_op jit(solution)/shard_map/pallas_call | solution.py:161
  208.0 2.2 %collective-permute-start.26 = (f32[4,768]{1,0:T(4,128)S(1)}, f32[4,768]{1,0:T(4,128)S(1)}, u32[]{:S(2)}, u32[]{:S(2)}) collective-permute-start(f32[4,768]{1,0:T(4,128)S(1)} %get-tuple-element.74), channel_id=1, source_target_pairs={{0,24},{4,28},{8,16},{12,20},{16,8},{20,12},{24,0},{28,4},{1,25},{... | collective-permute-start | bytes 36872 | tf_op jit(solution)/shard_map/ppermute | solution.py:315
  (129 shorter events, 51.0 us)
Async XLA Ops:
  2.6 19.7 %collective-permute-start = (bf16[784,512]{1,0:T(8,128)(2,1)S(1)}, bf16[784,512]{1,0:T(8,128)(2,1)S(1)}, u32[]{:S(2)}, u32[]{:S(2)}) collective-permute-start(bf16[784,512]{1,0:T(8,128)(2,1)S(1)} %get-tuple-element.70), channel_id=1, source_target_pairs={{0,8},{4,12},{8,0},{12,4},{16,24},{20,28},{24,16},{28,20},{1,9},{5... | collective-permute-start | bytes 2408456 | tf_op jit(solution)/shard_map/ppermute | solution.py:315
  5.5 24.3 %collective-permute-start.3 = (bf16[2000,256]{1,0:T(8,128)(2,1)S(1)}, bf16[2000,256]{1,0:T(8,128)(2,1)}, u32[]{:S(2)}, u32[]{:S(2)}) collective-permute-start(bf16[2000,256]{1,0:T(8,128)(2,1)S(1)} %dynamic-slice_bitcast_fusion), channel_id=1, source_target_pairs={{0,4},{4,0},{8,12},{12,8},{16,20},{20,16},{24,28},{28,24},{1,5},{5... | collective-permute-start | bytes 3072008 | tf_op jit(solution)/shard_map/ppermute | solution.py:318
  6.1 17.8 %collective-permute-start.2 = (bf16[784,512]{1,0:T(8,128)(2,1)S(1)}, bf16[784,512]{1,0:T(8,128)(2,1)}, u32[]{:S(2)}, u32[]{:S(2)}) collective-permute-start(bf16[784,512]{1,0:T(8,128)(2,1)S(1)} %get-tuple-element.70), channel_id=1, source_target_pairs={{8,16},{12,20},{16,8},{20,12},{9,17},{13,21},{17,9},{21,13},{10,18... | collective-permute-start | bytes 2408456 | tf_op jit(solution)/shard_map/ppermute | solution.py:324
  7.7 19.1 %collective-permute-start.1 = (bf16[784,512]{1,0:T(8,128)(2,1)S(1)}, bf16[784,512]{1,0:T(8,128)(2,1)S(1)}, u32[]{:S(2)}, u32[]{:S(2)}) collective-permute-start(bf16[784,512]{1,0:T(8,128)(2,1)S(1)} %get-tuple-element.70), channel_id=1, source_target_pairs={{0,2},{1,3},{2,0},{3,1},{4,6},{5,7},{6,4},{7,5},{8,10},{9,11},{10,... | collective-permute-start | bytes 2408456 | tf_op jit(solution)/shard_map/ppermute | solution.py:321
  22.3 11.2 %collective-permute-start.6 = (bf16[784,512]{1,0:T(8,128)(2,1)S(1)}, bf16[784,512]{1,0:T(8,128)(2,1)}, u32[]{:S(2)}, u32[]{:S(2)}) collective-permute-start(bf16[784,512]{1,0:T(8,128)(2,1)S(1)} %collective-permute-done), channel_id=1, source_target_pairs={{8,16},{12,20},{16,8},{20,12},{9,17},{13,21},{17,9},{21,13},{10,18... | collective-permute-start | bytes 2408456 | tf_op jit(solution)/shard_map/ppermute | solution.py:324
  23.9 23.0 %collective-permute-start.5 = (bf16[784,512]{1,0:T(8,128)(2,1)}, bf16[784,512]{1,0:T(8,128)(2,1)}, u32[]{:S(2)}, u32[]{:S(2)}) collective-permute-start(bf16[784,512]{1,0:T(8,128)(2,1)} %collective-permute-done.2), channel_id=1, source_target_pairs={{8,0},{12,4},{16,24},{20,28},{9,1},{13,5},{17,25},{21,29},{10,2},{... | collective-permute-start | bytes 2408456 | tf_op jit(solution)/shard_map/ppermute | solution.py:324
  29.8 18.4 %collective-permute-start.4 = (bf16[784,512]{1,0:T(8,128)(2,1)S(1)}, bf16[784,512]{1,0:T(8,128)(2,1)S(1)}, u32[]{:S(2)}, u32[]{:S(2)}) collective-permute-start(bf16[784,512]{1,0:T(8,128)(2,1)S(1)} %collective-permute-done), channel_id=1, source_target_pairs={{0,2},{1,3},{2,0},{3,1},{4,6},{5,7},{6,4},{7,5},{8,10},{9,11},{10,... | collective-permute-start | bytes 2408456 | tf_op jit(solution)/shard_map/ppermute | solution.py:321
  33.5 58.5 %collective-permute-start.16 = (bf16[784,512]{1,0:T(8,128)(2,1)}, bf16[784,512]{1,0:T(8,128)(2,1)}, u32[]{:S(2)}, u32[]{:S(2)}) collective-permute-start(bf16[784,512]{1,0:T(8,128)(2,1)} %collective-permute-done.6), channel_id=1, source_target_pairs={{8,0},{12,4},{16,24},{20,28},{9,1},{13,5},{17,25},{21,29},{10,2},{... | collective-permute-start | bytes 2408456 | tf_op jit(solution)/shard_map/ppermute | solution.py:324
  49.1 41.6 %collective-permute-start.7 = (bf16[800,256]{1,0:T(8,128)(2,1)}, bf16[800,256]{1,0:T(8,128)(2,1)S(1)}, u32[]{:S(2)}, u32[]{:S(2)}) collective-permute-start(bf16[800,256]{1,0:T(8,128)(2,1)} %get-tuple-element.17), channel_id=1, source_target_pairs={{0,8},{4,12},{8,0},{12,4},{16,24},{20,28},{24,16},{28,20},{1,9},{5... | collective-permute-start | bytes 1228808 | tf_op jit(solution)/shard_map/ppermute | solution.py:315
  53.0 37.8 %collective-permute-start.8 = (bf16[800,256]{1,0:T(8,128)(2,1)}, bf16[800,256]{1,0:T(8,128)(2,1)S(1)}, u32[]{:S(2)}, u32[]{:S(2)}) collective-permute-start(bf16[800,256]{1,0:T(8,128)(2,1)} %get-tuple-element.18), channel_id=1, source_target_pairs={{0,16},{4,20},{8,24},{12,28},{16,0},{20,4},{24,8},{28,12},{1,17},{... | collective-permute-start | bytes 1228808 | tf_op jit(solution)/shard_map/ppermute | solution.py:315
  54.2 36.6 %collective-permute-start.9 = (bf16[800,256]{1,0:T(8,128)(2,1)}, bf16[800,256]{1,0:T(8,128)(2,1)S(1)}, u32[]{:S(2)}, u32[]{:S(2)}) collective-permute-start(bf16[800,256]{1,0:T(8,128)(2,1)} %get-tuple-element.19), channel_id=1, source_target_pairs={{0,24},{4,28},{8,16},{12,20},{16,8},{20,12},{24,0},{28,4},{1,25},{... | collective-permute-start | bytes 1228808 | tf_op jit(solution)/shard_map/ppermute | solution.py:315
  56.9 40.1 %collective-permute-start.10 = (bf16[784,512]{1,0:T(8,128)(2,1)S(1)}, bf16[784,512]{1,0:T(8,128)(2,1)S(1)}, u32[]{:S(2)}, u32[]{:S(2)}) collective-permute-start(bf16[784,512]{1,0:T(8,128)(2,1)S(1)} %broadcast_select_fusion.1), channel_id=1, source_target_pairs={{0,2},{1,3},{2,0},{3,1},{4,6},{5,7},{6,4},{7,5},{8,10},{9,11},{10,... | collective-permute-start | bytes 2408456 | tf_op jit(solution)/shard_map/ppermute | solution.py:321
  91.0 34.2 %collective-permute-start.14 = (bf16[3,800,256]{2,1,0:T(8,128)(2,1)S(1)}, bf16[3,800,256]{2,1,0:T(8,128)(2,1)}, u32[]{:S(2)}, u32[]{:S(2)}) collective-permute-start(bf16[3,800,256]{2,1,0:T(8,128)(2,1)S(1)} %pad_maximum_fusion.2), channel_id=1, source_target_pairs={{0,4},{4,0},{8,12},{12,8},{16,20},{20,16},{24,28},{28,24},{1,5},{5... | collective-permute-start | bytes 3686408 | tf_op jit(solution)/shard_map/ppermute | solution.py:318
  93.3 17.6 %collective-permute-start.17 = (bf16[784,512]{1,0:T(8,128)(2,1)S(1)}, bf16[784,512]{1,0:T(8,128)(2,1)S(1)}, u32[]{:S(2)}, u32[]{:S(2)}) collective-permute-start(bf16[784,512]{1,0:T(8,128)(2,1)S(1)} %broadcast_select_fusion), channel_id=1, source_target_pairs={{0,2},{1,3},{2,0},{3,1},{4,6},{5,7},{6,4},{7,5},{8,10},{9,11},{10,... | collective-permute-start | bytes 2408456 | tf_op jit(solution)/shard_map/ppermute | solution.py:321
  97.8 14.4 %collective-permute-start.11 = (bf16[688,256]{1,0:T(8,128)(2,1)S(1)}, bf16[688,256]{1,0:T(8,128)(2,1)S(1)}, u32[]{:S(2)}, u32[]{:S(2)}) collective-permute-start(bf16[688,256]{1,0:T(8,128)(2,1)S(1)} %copy-done.20), channel_id=1, source_target_pairs={{0,8},{4,12},{8,0},{12,4},{16,24},{20,28},{24,16},{28,20},{1,9},{5... | collective-permute-start | bytes 1056776 | tf_op jit(solution)/shard_map/ppermute | solution.py:315
  98.3 26.8 %collective-permute-start.12 = (bf16[688,256]{1,0:T(8,128)(2,1)S(1)}, bf16[688,256]{1,0:T(8,128)(2,1)S(1)}, u32[]{:S(2)}, u32[]{:S(2)}) collective-permute-start(bf16[688,256]{1,0:T(8,128)(2,1)S(1)} %copy-done.19), channel_id=1, source_target_pairs={{0,16},{4,20},{8,24},{12,28},{16,0},{20,4},{24,8},{28,12},{1,17},{... | collective-permute-start | bytes 1056776 | tf_op jit(solution)/shard_map/ppermute | solution.py:315
  100.7 24.4 %collective-permute-start.13 = (bf16[688,256]{1,0:T(8,128)(2,1)S(1)}, bf16[688,256]{1,0:T(8,128)(2,1)S(1)}, u32[]{:S(2)}, u32[]{:S(2)}) collective-permute-start(bf16[688,256]{1,0:T(8,128)(2,1)S(1)} %copy-done.18), channel_id=1, source_target_pairs={{0,24},{4,28},{8,16},{12,20},{16,8},{20,12},{24,0},{28,4},{1,25},{... | collective-permute-start | bytes 1056776 | tf_op jit(solution)/shard_map/ppermute | solution.py:315
  125.1 12.6 %collective-permute-start.18 = (bf16[2,2,784,512]{3,2,1,0:T(8,128)(2,1)S(1)}, bf16[2,2,784,512]{3,2,1,0:T(8,128)(2,1)S(1)}, u32[]{:S(2)}, u32[]{:S(2)}) collective-permute-start(bf16[2,2,784,512]{3,2,1,0:T(8,128)(2,1)S(1)} %pad_maximum_fusion.1.refs_0_), channel_id=1, source_target_pairs={{0,1},{1,0},{2,3},{3,2},{4,5},{5,4},{6,7},{7,6},{8,9},{9,8},{10,11... | collective-permute-start | bytes 9633800 | tf_op jit(solution)/shard_map/ppermute | solution.py:321
  127.2 20.3 %collective-permute-start.15 = (bf16[2,2,784,512]{3,2,1,0:T(8,128)(2,1)}, bf16[2,2,784,512]{3,2,1,0:T(8,128)(2,1)}, u32[]{:S(2)}, u32[]{:S(2)}) collective-permute-start(bf16[2,2,784,512]{3,2,1,0:T(8,128)(2,1)} %pad_maximum_fusion.refs_0_), channel_id=1, source_target_pairs={{0,1},{1,0},{2,3},{3,2},{4,5},{5,4},{6,7},{7,6},{8,9},{9,8},{10,11... | collective-permute-start | bytes 9633800 | tf_op jit(solution)/shard_map/ppermute | solution.py:321
  128.8 34.3 %collective-permute-start.22 = (bf16[3,688,256]{2,1,0:T(8,128)(2,1)}, bf16[3,688,256]{2,1,0:T(8,128)(2,1)}, u32[]{:S(2)}, u32[]{:S(2)}) collective-permute-start(bf16[3,688,256]{2,1,0:T(8,128)(2,1)} %pad_maximum_fusion.3), channel_id=1, source_target_pairs={{0,4},{4,0},{8,12},{12,8},{16,20},{20,16},{24,28},{28,24},{1,5},{5... | collective-permute-start | bytes 3170312 | tf_op jit(solution)/shard_map/ppermute | solution.py:318
  130.8 24.9 %collective-permute-start.20 = (bf16[512,256]{1,0:T(8,128)(2,1)S(1)}, bf16[512,256]{1,0:T(8,128)(2,1)S(1)}, u32[]{:S(2)}, u32[]{:S(2)}) collective-permute-start(bf16[512,256]{1,0:T(8,128)(2,1)S(1)} %copy-done.21), channel_id=1, source_target_pairs={{0,16},{4,20},{8,24},{12,28},{16,0},{20,4},{24,8},{28,12},{1,17},{... | collective-permute-start | bytes 786440 | tf_op jit(solution)/shard_map/ppermute | solution.py:315
  136.2 19.4 %collective-permute-start.21 = (bf16[512,256]{1,0:T(8,128)(2,1)S(1)}, bf16[512,256]{1,0:T(8,128)(2,1)S(1)}, u32[]{:S(2)}, u32[]{:S(2)}) collective-permute-start(bf16[512,256]{1,0:T(8,128)(2,1)S(1)} %get-tuple-element.28), channel_id=1, source_target_pairs={{0,24},{4,28},{8,16},{12,20},{16,8},{20,12},{24,0},{28,4},{1,25},{... | collective-permute-start | bytes 786440 | tf_op jit(solution)/shard_map/ppermute | solution.py:315
  155.6 7.4 %collective-permute-start.19 = (bf16[512,256]{1,0:T(8,128)(2,1)S(1)}, bf16[512,256]{1,0:T(8,128)(2,1)S(1)}, u32[]{:S(2)}, u32[]{:S(2)}) collective-permute-start(bf16[512,256]{1,0:T(8,128)(2,1)S(1)} %get-tuple-element.26), channel_id=1, source_target_pairs={{0,8},{4,12},{8,0},{12,4},{16,24},{20,28},{24,16},{28,20},{1,9},{5... | collective-permute-start | bytes 786440 | tf_op jit(solution)/shard_map/ppermute | solution.py:315
  163.1 28.9 %collective-permute-start.23 = (bf16[3,512,256]{2,1,0:T(8,128)(2,1)S(1)}, bf16[3,512,256]{2,1,0:T(8,128)(2,1)S(1)}, u32[]{:S(2)}, u32[]{:S(2)}) collective-permute-start(bf16[3,512,256]{2,1,0:T(8,128)(2,1)S(1)} %pad_maximum_fusion.4), channel_id=1, source_target_pairs={{0,4},{4,0},{8,12},{12,8},{16,20},{20,16},{24,28},{28,24},{1,5},{5... | collective-permute-start | bytes 2359304 | tf_op jit(solution)/shard_map/ppermute | solution.py:318
  (31 other events, 264.4 us)

commit v8 on v6

--- a/solution.py
+++ b/solution.py
@@ -47,7 +47,7 @@
         + [pl.BlockSpec((y.shape[0], 1, rows, features), lambda i, j: (0, i, j, 0)) for y in sources],
         out_specs=pl.BlockSpec((1, 1, wide, rows), lambda i, j: (i, j, 0, 0)),
         out_shape=jax.ShapeDtypeStruct((count, splits, wide, rows), sources[0].dtype),
-        compiler_params=pltpu.CompilerParams(vmem_limit_bytes=60 * 2**20),
+        compiler_params=pltpu.CompilerParams(vmem_limit_bytes=24 * 2**20),
         cost_estimate=pl.CostEstimate(
             flops=6 * count * splits * rows * wide,
             bytes_accessed=4 * count * splits * rows * wide,

time: 222 us -> 224 us (level)
  the two profiles are of different devices: /device:TPU:0 before, /device:TPU:4 now
where the time goes in v8:
time: 224 us; the launch traced here: 220 us
  waiting for transfers between devices  90.5 us (40%)
  Pallas kernels  49.7 us (22%)
  starting transfers between devices  44.4 us (20%)
  local copies, waits for them, and re-layouts  19.3 us (9%)
  other arithmetic  14.6 us (7%)
    ppermute x13, waiting for transfers between devices, swap_hi(): return lax.ppermute(x, 'dp', [(g, g ^ 2 * step) for g in range(groups)])  71.5 us
    pallas_call x2, Pallas kernels, stats(): pl.pallas_call(functools.partial(stats_kernel, plan, (len(tokens), len(id...  39.4 us
    ppermute x13, starting transfers between devices, swap_hi(): return lax.ppermute(x, 'dp', [(g, g ^ 2 * step) for g in range(groups)])  26.8 us
    ppermute x4, waiting for transfers between devices, along(): lax.ppermute(x, 'dp', [(2 * a + side, 2 * b + side) for a, b in moves for...  16.8 us
    pallas_call x2, Pallas kernels, assemble(): pl.pallas_call(functools.partial(assemble_kernel, len(sources) > 1), grid...  10.3 us
    unnamed x44, local copies, waits for them, and re-layouts  9.12 us
    ppermute x9, starting transfers between devices, swap_part(): return lax.ppermute(x, 'vocab', [(v, v ^ step) for v in range(parts)])  8.27 us
    squeeze x4, local copies, waits for them, and re-layouts, block(): lax.dynamic_slice(turned, (hi ^ step, start, 0), (1, width, depth))[0]  7.76 us
  transfers between devices with their start and end apart: 30, of which 15 were waited for; matrix products, arithmetic and copies ran while one was open for 8% of the time, Pallas kernels for 16%

profile of v8, /device:TPU:4, one launch (start us, length us, event | category | flops | bytes accessed | tf_op | source)
XLA Modules:
  0.0 219.5 jit_solution(15411985120652247266)
XLA Ops:
  3.3 2.1 collective-permute-start
  8.5 14.7 %collective-permute-done = bf16[784,512]{1,0:T(8,128)(2,1)} collective-permute-done((bf16[784,512]{1,0:T(8,128)(2,1)S(1)}, bf16[784,512]{1,0:T(8,128)(2,1)}, u32[]{:S(2)}, u32[]{:S(2)}) %collective-permute-start) | collective-permute-done | bytes 802848 | tf_op jit(solution)/shard_map/ppermute | solution.py:315
  28.6 2.0 dynamic-slice_bitcast_fusion.7
  30.7 2.2 %dynamic-slice_bitcast_fusion.4 = (bf16[688,256]{1,0:T(8,128)(2,1)}, bf16[688,256]{1,0:T(8,128)(2,1)}, bf16[688,256]{1,0:T(8,128)(2,1)}) fusion(bf16[4,2000,256]{2,1,0:T(8,128)(2,1)} %bitcast.107, s32[]{:T(128)S(6)} %select_n.55, s32[]{:T(128)S(6)} %select_n.54, s32[]{:T(128)S(6)} %select_n.53), kind=kLoop, calls=%fused_computation.18 | loop fusion | bytes 2113548 | tf_op jit(solution)/shard_map/squeeze | solution.py:338
  32.9 2.2 %dynamic-slice_bitcast_fusion.1 = (bf16[800,256]{1,0:T(8,128)(2,1)S(1)}, bf16[800,256]{1,0:T(8,128)(2,1)}, bf16[800,256]{1,0:T(8,128)(2,1)}) fusion(bf16[4,2000,256]{2,1,0:T(8,128)(2,1)} %bitcast.108, s32[]{:T(128)S(6)} %select_n.55, s32[]{:T(128)S(6)} %select_n.54, s32[]{:T(128)S(6)} %select_n.53), kind=kLoop, calls=%fused_computation.15 | loop fusion | bytes 2457612 | tf_op jit(solution)/shard_map/squeeze | solution.py:338
  35.1 11.3 %collective-permute-done.5 = bf16[784,512]{1,0:T(8,128)(2,1)} collective-permute-done((bf16[784,512]{1,0:T(8,128)(2,1)}, bf16[784,512]{1,0:T(8,128)(2,1)}, u32[]{:S(2)}, u32[]{:S(2)}) %collective-permute-start.5) | collective-permute-done | bytes 802848 | tf_op jit(solution)/shard_map/ppermute | solution.py:324
  46.4 3.5 %collective-permute-start.7 = (bf16[800,256]{1,0:T(8,128)(2,1)}, bf16[800,256]{1,0:T(8,128)(2,1)S(1)}, u32[]{:S(2)}, u32[]{:S(2)}) collective-permute-start(bf16[800,256]{1,0:T(8,128)(2,1)} %get-tuple-element.17), channel_id=1, source_target_pairs={{0,8},{4,12},{8,0},{12,4},{16,24},{20,28},{24,16},{28,20},{1,9},{5... | collective-permute-start | bytes 1228808 | tf_op jit(solution)/shard_map/ppermute | solution.py:315
  56.7 11.7 %collective-permute-done.7.refs_6_ = bf16[800,256]{1,0:T(8,128)(2,1)S(1)} collective-permute-done((bf16[800,256]{1,0:T(8,128)(2,1)}, bf16[800,256]{1,0:T(8,128)(2,1)S(1)}, u32[]{:S(2)}, u32[]{:S(2)}) %collective-permute-start.7) | collective-permute-done | bytes 409632 | tf_op jit(solution)/shard_map/ppermute | solution.py:315
  68.4 12.7 %collective-permute-done.8.refs_7_ = bf16[800,256]{1,0:T(8,128)(2,1)S(1)} collective-permute-done((bf16[800,256]{1,0:T(8,128)(2,1)}, bf16[800,256]{1,0:T(8,128)(2,1)S(1)}, u32[]{:S(2)}, u32[]{:S(2)}) %collective-permute-start.8) | collective-permute-done | bytes 409632 | tf_op jit(solution)/shard_map/ppermute | solution.py:315
  85.4 5.5 %collective-permute-start.11 = (bf16[688,256]{1,0:T(8,128)(2,1)S(1)}, bf16[688,256]{1,0:T(8,128)(2,1)S(1)}, u32[]{:S(2)}, u32[]{:S(2)}) collective-permute-start(bf16[688,256]{1,0:T(8,128)(2,1)S(1)} %copy-done.17), channel_id=1, source_target_pairs={{0,8},{4,12},{8,0},{12,4},{16,24},{20,28},{24,16},{28,20},{1,9},{5... | collective-permute-start | bytes 1056776 | tf_op jit(solution)/shard_map/ppermute | solution.py:315
  93.7 5.4 %collective-permute-done.16 = bf16[784,512]{1,0:T(8,128)(2,1)S(1)} collective-permute-done((bf16[784,512]{1,0:T(8,128)(2,1)}, bf16[784,512]{1,0:T(8,128)(2,1)S(1)}, u32[]{:S(2)}, u32[]{:S(2)}) %collective-permute-start.16) | collective-permute-done | bytes 802848 | tf_op jit(solution)/shard_map/ppermute | solution.py:324
  101.2 7.7 %collective-permute-done.11.refs_10_ = bf16[688,256]{1,0:T(8,128)(2,1)S(1)} collective-permute-done((bf16[688,256]{1,0:T(8,128)(2,1)S(1)}, bf16[688,256]{1,0:T(8,128)(2,1)S(1)}, u32[]{:S(2)}, u32[]{:S(2)}) %collective-permute-start.11) | collective-permute-done | bytes 352288 | tf_op jit(solution)/shard_map/ppermute | solution.py:315
  108.9 7.7 %collective-permute-done.12.refs_11_ = bf16[688,256]{1,0:T(8,128)(2,1)S(1)} collective-permute-done((bf16[688,256]{1,0:T(8,128)(2,1)S(1)}, bf16[688,256]{1,0:T(8,128)(2,1)S(1)}, u32[]{:S(2)}, u32[]{:S(2)}) %collective-permute-start.12) | collective-permute-done | bytes 352288 | tf_op jit(solution)/shard_map/ppermute | solution.py:315
  121.2 5.6 %collective-permute-start.20 = (bf16[512,256]{1,0:T(8,128)(2,1)}, bf16[512,256]{1,0:T(8,128)(2,1)S(1)}, u32[]{:S(2)}, u32[]{:S(2)}) collective-permute-start(bf16[512,256]{1,0:T(8,128)(2,1)} %get-tuple-element.27), channel_id=1, source_target_pairs={{0,16},{4,20},{8,24},{12,28},{16,0},{20,4},{24,8},{28,12},{1,17},{... | collective-permute-start | bytes 786440 | tf_op jit(solution)/shard_map/ppermute | solution.py:315
  127.9 4.4 %shard_map.77.refs_0_ = bf16[2,3,2048,256]{3,2,1,0:T(8,128)(2,1)S(1)} custom-call(f32[1,2048]{1,0:T(1,128)S(1)} %bitcast.103, bf16[2,2,784,512]{3,2,1,0:T(8,128)(2,1)S(1)} %pad_maximum_fusion.refs_0_, bf16[2,2,784,512]{3,2,1,0:T(8,128)(2,1)S(1)} %collective-permute-done.15.refs_1_), custom_call_target="tpu_custom_call" | custom-call | flops 18874368 | bytes 12582912 | tf_op jit(solution)/shard_map/pallas_call | solution.py:43
  132.3 2.7 %copy-done = bf16[2,3,2048,256]{3,2,1,0:T(8,128)(2,1)} copy-done((bf16[2,3,2048,256]{3,2,1,0:T(8,128)(2,1)}, bf16[2,3,2048,256]{3,2,1,0:T(8,128)(2,1)S(1)}, u32[]{:S(2)}) %copy-start) | copy-done | bytes 6291480
  135.6 9.8 %collective-permute-done.20.refs_7_ = bf16[512,256]{1,0:T(8,128)(2,1)S(1)} collective-permute-done((bf16[512,256]{1,0:T(8,128)(2,1)}, bf16[512,256]{1,0:T(8,128)(2,1)S(1)}, u32[]{:S(2)}, u32[]{:S(2)}) %collective-permute-start.20) | collective-permute-done | bytes 262176 | tf_op jit(solution)/shard_map/ppermute | solution.py:315
  145.4 5.3 %collective-permute-done.19.refs_6_ = bf16[512,256]{1,0:T(8,128)(2,1)} collective-permute-done((bf16[512,256]{1,0:T(8,128)(2,1)}, bf16[512,256]{1,0:T(8,128)(2,1)}, u32[]{:S(2)}, u32[]{:S(2)}) %collective-permute-start.19) | collective-permute-done | bytes 262176 | tf_op jit(solution)/shard_map/ppermute | solution.py:315
  150.7 2.0 pad_maximum_fusion.4
  156.3 6.0 %shard_map.78.refs_1_ = bf16[2,3,2048,256]{3,2,1,0:T(8,128)(2,1)S(1)} custom-call(f32[1,2048]{1,0:T(1,128)S(1)} %bitcast.104, bf16[2,2,784,512]{3,2,1,0:T(8,128)(2,1)S(1)} %pad_maximum_fusion.1.refs_0_, bf16[2,2,784,512]{3,2,1,0:T(8,128)(2,1)} %collective-permute-done.18.refs_1_), custom_call_target="tpu_custom_call" | custom-call | flops 18874368 | bytes 12582912 | tf_op jit(solution)/shard_map/pallas_call | solution.py:43
  162.3 2.6 %copy-done.1 = bf16[2,3,2048,256]{3,2,1,0:T(8,128)(2,1)} copy-done((bf16[2,3,2048,256]{3,2,1,0:T(8,128)(2,1)}, bf16[2,3,2048,256]{3,2,1,0:T(8,128)(2,1)S(1)}, u32[]{:S(2)}) %copy-start.1) | copy-done | bytes 6291480
  164.9 25.4 %shard_map.79.refs_10_ = f32[4,4,768]{2,1,0:T(4,128)} custom-call(s32[1]{0:T(128)} %constant.14.clone.1.start_ref, s32[16]{0:T(128)} %lens_ref.3, s32[16]{0:T(128)} %owner_ref.3, bf16[2,3,2048,256]{3,2,1,0:T(8,128)(2,1)} %copy-done, bf16[2,3,2048,256]{3,2,1,0:T(8,128)(2,1)} %copy-done.1, s32[6,1,256]{2,1,0:T(1,128)} %get-tuple-element.85.refs_2_, ...), custom_call_target="tpu_custom_call" | custom-call | flops 1170210816 | bytes 3047424 | tf_op jit(solution)/shard_map/pallas_call | solution.py:161
  190.4 13.9 %shard_map.80 = f32[4,4,768]{2,1,0:T(4,128)} custom-call(s32[1]{0:T(128)} %constant.14.clone.1.start_ref, s32[16]{0:T(128)} %lens_ref.3, s32[16]{0:T(128)} %owner_ref.3, bf16[2,3,2048,256]{3,2,1,0:T(8,128)(2,1)} %copy-done, bf16[2,3,2048,256]{3,2,1,0:T(8,128)(2,1)} %copy-done.1, s32[6,1,256]{2,1,0:T(1,128)} %get-tuple-element.85.refs_2_, ...), custom_call_target="tpu_custom_call" | custom-call | flops 402653184 | bytes 1048576 | tf_op jit(solution)/shard_map/pallas_call | solution.py:161
  206.7 1.9 collective-permute-start.25
  (123 shorter events, 50.1 us)
Async XLA Ops:
  1.9 24.4 %collective-permute-start.3 = (bf16[2000,256]{1,0:T(8,128)(2,1)S(1)}, bf16[2000,256]{1,0:T(8,128)(2,1)S(1)}, u32[]{:S(2)}, u32[]{:S(2)}) collective-permute-start(bf16[2000,256]{1,0:T(8,128)(2,1)S(1)} %dynamic-slice_bitcast_fusion), channel_id=1, source_target_pairs={{0,4},{4,0},{8,12},{12,8},{16,20},{20,16},{24,28},{28,24},{1,5},{5... | collective-permute-start | bytes 3072008 | tf_op jit(solution)/shard_map/ppermute | solution.py:318
  3.3 19.8 %collective-permute-start = (bf16[784,512]{1,0:T(8,128)(2,1)S(1)}, bf16[784,512]{1,0:T(8,128)(2,1)}, u32[]{:S(2)}, u32[]{:S(2)}) collective-permute-start(bf16[784,512]{1,0:T(8,128)(2,1)S(1)} %get-tuple-element.70), channel_id=1, source_target_pairs={{0,8},{4,12},{8,0},{12,4},{16,24},{20,28},{24,16},{28,20},{1,9},{5... | collective-permute-start | bytes 2408456 | tf_op jit(solution)/shard_map/ppermute | solution.py:315
  5.5 19.3 %collective-permute-start.2 = (bf16[784,512]{1,0:T(8,128)(2,1)S(1)}, bf16[784,512]{1,0:T(8,128)(2,1)}, u32[]{:S(2)}, u32[]{:S(2)}) collective-permute-start(bf16[784,512]{1,0:T(8,128)(2,1)S(1)} %get-tuple-element.70), channel_id=1, source_target_pairs={{8,16},{12,20},{16,8},{20,12},{9,17},{13,21},{17,9},{21,13},{10,18... | collective-permute-start | bytes 2408456 | tf_op jit(solution)/shard_map/ppermute | solution.py:324
  7.0 19.1 %collective-permute-start.1 = (bf16[784,512]{1,0:T(8,128)(2,1)S(1)}, bf16[784,512]{1,0:T(8,128)(2,1)S(1)}, u32[]{:S(2)}, u32[]{:S(2)}) collective-permute-start(bf16[784,512]{1,0:T(8,128)(2,1)S(1)} %get-tuple-element.70), channel_id=1, source_target_pairs={{0,2},{1,3},{2,0},{3,1},{4,6},{5,7},{6,4},{7,5},{8,10},{9,11},{10,... | collective-permute-start | bytes 2408456 | tf_op jit(solution)/shard_map/ppermute | solution.py:321
  23.2 11.9 %collective-permute-start.6 = (bf16[784,512]{1,0:T(8,128)(2,1)}, bf16[784,512]{1,0:T(8,128)(2,1)}, u32[]{:S(2)}, u32[]{:S(2)}) collective-permute-start(bf16[784,512]{1,0:T(8,128)(2,1)} %collective-permute-done), channel_id=1, source_target_pairs={{8,16},{12,20},{16,8},{20,12},{9,17},{13,21},{17,9},{21,13},{10,18... | collective-permute-start | bytes 2408456 | tf_op jit(solution)/shard_map/ppermute | solution.py:324
  24.7 21.7 %collective-permute-start.5 = (bf16[784,512]{1,0:T(8,128)(2,1)}, bf16[784,512]{1,0:T(8,128)(2,1)}, u32[]{:S(2)}, u32[]{:S(2)}) collective-permute-start(bf16[784,512]{1,0:T(8,128)(2,1)} %collective-permute-done.2), channel_id=1, source_target_pairs={{8,0},{12,4},{16,24},{20,28},{9,1},{13,5},{17,25},{21,29},{10,2},{... | collective-permute-start | bytes 2408456 | tf_op jit(solution)/shard_map/ppermute | solution.py:324
  27.0 19.4 %collective-permute-start.4 = (bf16[784,512]{1,0:T(8,128)(2,1)}, bf16[784,512]{1,0:T(8,128)(2,1)S(1)}, u32[]{:S(2)}, u32[]{:S(2)}) collective-permute-start(bf16[784,512]{1,0:T(8,128)(2,1)} %collective-permute-done), channel_id=1, source_target_pairs={{0,2},{1,3},{2,0},{3,1},{4,6},{5,7},{6,4},{7,5},{8,10},{9,11},{10,... | collective-permute-start | bytes 2408456 | tf_op jit(solution)/shard_map/ppermute | solution.py:321
  46.4 22.0 %collective-permute-start.7 = (bf16[800,256]{1,0:T(8,128)(2,1)}, bf16[800,256]{1,0:T(8,128)(2,1)S(1)}, u32[]{:S(2)}, u32[]{:S(2)}) collective-permute-start(bf16[800,256]{1,0:T(8,128)(2,1)} %get-tuple-element.17), channel_id=1, source_target_pairs={{0,8},{4,12},{8,0},{12,4},{16,24},{20,28},{24,16},{28,20},{1,9},{5... | collective-permute-start | bytes 1228808 | tf_op jit(solution)/shard_map/ppermute | solution.py:315
  49.9 31.1 %collective-permute-start.8 = (bf16[800,256]{1,0:T(8,128)(2,1)}, bf16[800,256]{1,0:T(8,128)(2,1)S(1)}, u32[]{:S(2)}, u32[]{:S(2)}) collective-permute-start(bf16[800,256]{1,0:T(8,128)(2,1)} %get-tuple-element.18), channel_id=1, source_target_pairs={{0,16},{4,20},{8,24},{12,28},{16,0},{20,4},{24,8},{28,12},{1,17},{... | collective-permute-start | bytes 1228808 | tf_op jit(solution)/shard_map/ppermute | solution.py:315
  51.2 29.9 %collective-permute-start.9 = (bf16[800,256]{1,0:T(8,128)(2,1)S(1)}, bf16[800,256]{1,0:T(8,128)(2,1)S(1)}, u32[]{:S(2)}, u32[]{:S(2)}) collective-permute-start(bf16[800,256]{1,0:T(8,128)(2,1)S(1)} %get-tuple-element.19), channel_id=1, source_target_pairs={{0,24},{4,28},{8,16},{12,20},{16,8},{20,12},{24,0},{28,4},{1,25},{... | collective-permute-start | bytes 1228808 | tf_op jit(solution)/shard_map/ppermute | solution.py:315
  53.9 30.5 %collective-permute-start.10 = (bf16[784,512]{1,0:T(8,128)(2,1)S(1)}, bf16[784,512]{1,0:T(8,128)(2,1)S(1)}, u32[]{:S(2)}, u32[]{:S(2)}) collective-permute-start(bf16[784,512]{1,0:T(8,128)(2,1)S(1)} %broadcast_select_fusion.1), channel_id=1, source_target_pairs={{0,2},{1,3},{2,0},{3,1},{4,6},{5,7},{6,4},{7,5},{8,10},{9,11},{10,... | collective-permute-start | bytes 2408456 | tf_op jit(solution)/shard_map/ppermute | solution.py:321
  55.4 43.7 %collective-permute-start.16 = (bf16[784,512]{1,0:T(8,128)(2,1)}, bf16[784,512]{1,0:T(8,128)(2,1)S(1)}, u32[]{:S(2)}, u32[]{:S(2)}) collective-permute-start(bf16[784,512]{1,0:T(8,128)(2,1)} %collective-permute-done.6), channel_id=1, source_target_pairs={{8,0},{12,4},{16,24},{20,28},{9,1},{13,5},{17,25},{21,29},{10,2},{... | collective-permute-start | bytes 2408456 | tf_op jit(solution)/shard_map/ppermute | solution.py:324
  81.2 35.5 %collective-permute-start.14 = (bf16[3,800,256]{2,1,0:T(8,128)(2,1)S(1)}, bf16[3,800,256]{2,1,0:T(8,128)(2,1)S(1)}, u32[]{:S(2)}, u32[]{:S(2)}) collective-permute-start(bf16[3,800,256]{2,1,0:T(8,128)(2,1)S(1)} %pad_maximum_fusion.2), channel_id=1, source_target_pairs={{0,4},{4,0},{8,12},{12,8},{16,20},{20,16},{24,28},{28,24},{1,5},{5... | collective-permute-start | bytes 3686408 | tf_op jit(solution)/shard_map/ppermute | solution.py:318
  85.4 23.4 %collective-permute-start.11 = (bf16[688,256]{1,0:T(8,128)(2,1)S(1)}, bf16[688,256]{1,0:T(8,128)(2,1)S(1)}, u32[]{:S(2)}, u32[]{:S(2)}) collective-permute-start(bf16[688,256]{1,0:T(8,128)(2,1)S(1)} %copy-done.17), channel_id=1, source_target_pairs={{0,8},{4,12},{8,0},{12,4},{16,24},{20,28},{24,16},{28,20},{1,9},{5... | collective-permute-start | bytes 1056776 | tf_op jit(solution)/shard_map/ppermute | solution.py:315
  91.0 25.7 %collective-permute-start.12 = (bf16[688,256]{1,0:T(8,128)(2,1)S(1)}, bf16[688,256]{1,0:T(8,128)(2,1)S(1)}, u32[]{:S(2)}, u32[]{:S(2)}) collective-permute-start(bf16[688,256]{1,0:T(8,128)(2,1)S(1)} %copy-done.16), channel_id=1, source_target_pairs={{0,16},{4,20},{8,24},{12,28},{16,0},{20,4},{24,8},{28,12},{1,17},{... | collective-permute-start | bytes 1056776 | tf_op jit(solution)/shard_map/ppermute | solution.py:315
  92.6 24.1 %collective-permute-start.13 = (bf16[688,256]{1,0:T(8,128)(2,1)S(1)}, bf16[688,256]{1,0:T(8,128)(2,1)S(1)}, u32[]{:S(2)}, u32[]{:S(2)}) collective-permute-start(bf16[688,256]{1,0:T(8,128)(2,1)S(1)} %copy-done.15), channel_id=1, source_target_pairs={{0,24},{4,28},{8,16},{12,20},{16,8},{20,12},{24,0},{28,4},{1,25},{... | collective-permute-start | bytes 1056776 | tf_op jit(solution)/shard_map/ppermute | solution.py:315
  99.3 18.7 %collective-permute-start.17 = (bf16[784,512]{1,0:T(8,128)(2,1)S(1)}, bf16[784,512]{1,0:T(8,128)(2,1)S(1)}, u32[]{:S(2)}, u32[]{:S(2)}) collective-permute-start(bf16[784,512]{1,0:T(8,128)(2,1)S(1)} %broadcast_select_fusion), channel_id=1, source_target_pairs={{0,2},{1,3},{2,0},{3,1},{4,6},{5,7},{6,4},{7,5},{8,10},{9,11},{10,... | collective-permute-start | bytes 2408456 | tf_op jit(solution)/shard_map/ppermute | solution.py:321
  116.7 11.2 %collective-permute-start.15 = (bf16[2,2,784,512]{3,2,1,0:T(8,128)(2,1)S(1)}, bf16[2,2,784,512]{3,2,1,0:T(8,128)(2,1)S(1)}, u32[]{:S(2)}, u32[]{:S(2)}) collective-permute-start(bf16[2,2,784,512]{3,2,1,0:T(8,128)(2,1)S(1)} %pad_maximum_fusion.refs_0_), channel_id=1, source_target_pairs={{0,1},{1,0},{2,3},{3,2},{4,5},{5,4},{6,7},{7,6},{8,9},{9,8},{10,11... | collective-permute-start | bytes 9633800 | tf_op jit(solution)/shard_map/ppermute | solution.py:321
  119.4 36.9 %collective-permute-start.18 = (bf16[2,2,784,512]{3,2,1,0:T(8,128)(2,1)S(1)}, bf16[2,2,784,512]{3,2,1,0:T(8,128)(2,1)}, u32[]{:S(2)}, u32[]{:S(2)}) collective-permute-start(bf16[2,2,784,512]{3,2,1,0:T(8,128)(2,1)S(1)} %pad_maximum_fusion.1.refs_0_), channel_id=1, source_target_pairs={{0,1},{1,0},{2,3},{3,2},{4,5},{5,4},{6,7},{7,6},{8,9},{9,8},{10,11... | collective-permute-start | bytes 9633800 | tf_op jit(solution)/shard_map/ppermute | solution.py:321
  120.7 32.0 %collective-permute-start.22 = (bf16[3,688,256]{2,1,0:T(8,128)(2,1)}, bf16[3,688,256]{2,1,0:T(8,128)(2,1)}, u32[]{:S(2)}, u32[]{:S(2)}) collective-permute-start(bf16[3,688,256]{2,1,0:T(8,128)(2,1)} %pad_maximum_fusion.3), channel_id=1, source_target_pairs={{0,4},{4,0},{8,12},{12,8},{16,20},{20,16},{24,28},{28,24},{1,5},{5... | collective-permute-start | bytes 3170312 | tf_op jit(solution)/shard_map/ppermute | solution.py:318
  121.2 24.2 %collective-permute-start.20 = (bf16[512,256]{1,0:T(8,128)(2,1)}, bf16[512,256]{1,0:T(8,128)(2,1)S(1)}, u32[]{:S(2)}, u32[]{:S(2)}) collective-permute-start(bf16[512,256]{1,0:T(8,128)(2,1)} %get-tuple-element.27), channel_id=1, source_target_pairs={{0,16},{4,20},{8,24},{12,28},{16,0},{20,4},{24,8},{28,12},{1,17},{... | collective-permute-start | bytes 786440 | tf_op jit(solution)/shard_map/ppermute | solution.py:315
  126.8 18.6 %collective-permute-start.21 = (bf16[512,256]{1,0:T(8,128)(2,1)}, bf16[512,256]{1,0:T(8,128)(2,1)}, u32[]{:S(2)}, u32[]{:S(2)}) collective-permute-start(bf16[512,256]{1,0:T(8,128)(2,1)} %get-tuple-element.28), channel_id=1, source_target_pairs={{0,24},{4,28},{8,16},{12,20},{16,8},{20,12},{24,0},{28,4},{1,25},{... | collective-permute-start | bytes 786440 | tf_op jit(solution)/shard_map/ppermute | solution.py:315
  135.0 15.7 %collective-permute-start.19 = (bf16[512,256]{1,0:T(8,128)(2,1)}, bf16[512,256]{1,0:T(8,128)(2,1)}, u32[]{:S(2)}, u32[]{:S(2)}) collective-permute-start(bf16[512,256]{1,0:T(8,128)(2,1)} %get-tuple-element.26), channel_id=1, source_target_pairs={{0,8},{4,12},{8,0},{12,4},{16,24},{20,28},{24,16},{28,20},{1,9},{5... | collective-permute-start | bytes 786440 | tf_op jit(solution)/shard_map/ppermute | solution.py:315
  152.7 37.7 %collective-permute-start.23 = (bf16[3,512,256]{2,1,0:T(8,128)(2,1)}, bf16[3,512,256]{2,1,0:T(8,128)(2,1)}, u32[]{:S(2)}, u32[]{:S(2)}) collective-permute-start(bf16[3,512,256]{2,1,0:T(8,128)(2,1)} %pad_maximum_fusion.4), channel_id=1, source_target_pairs={{0,4},{4,0},{8,12},{12,8},{16,20},{20,16},{24,28},{28,24},{1,5},{5... | collective-permute-start | bytes 2359304 | tf_op jit(solution)/shard_map/ppermute | solution.py:318
  (28 other events, 145.4 us)
